TPU v7x, 32 devices: a whole 2x2x4 slice. The times are simulated.
32 devices in a mesh: gx: 4 (over x, core), gy: 4 (over z), gz: 2 (over y).
Axes of the slice: x: 2, y: 2, z: 4, core: 2. Of those that a mesh axis runs over, the one named last changes fastest.
Arguments:
- e_forward: float32 [3, 64, 128, 256], P(None, 'gx', 'gy', 'gz'), may hold values from -6 to 6
- h_forward: float32 [3, 64, 128, 256], P(None, 'gx', 'gy', 'gz'), may hold values from -6 to 6
- e_adjoint: float32 [3, 64, 128, 256], P(None, 'gx', 'gy', 'gz'), may hold values from -6 to 6
- h_adjoint: float32 [3, 64, 128, 256], P(None, 'gx', 'gy', 'gz'), may hold values from -6 to 6
- material: int32 [64, 128, 256], P('gx', 'gy', 'gz'), may hold values from 0 to 3
- dft_forward: float32 [3, 2, 3, 96, 64, 128], P(None, None, None, 'gz', 'gx', 'gy'), may hold values from -6 to 6
- dft_adjoint: float32 [3, 2, 3, 96, 64, 128], P(None, None, None, 'gz', 'gx', 'gy'), may hold values from -6 to 6
- angular_freq: float32 [3], replicated, may hold values from 0.05 to 0.6
- layer_map: int32 [96], replicated, may hold values from 0 to 15, as said below
Outputs:
- e_forward_new: float32 [3, 64, 128, 256], P(None, 'gx', 'gy', 'gz')
- h_forward_new: float32 [3, 64, 128, 256], P(None, 'gx', 'gy', 'gz')
- e_adjoint_new: float32 [3, 64, 128, 256], P(None, 'gx', 'gy', 'gz')
- h_adjoint_new: float32 [3, 64, 128, 256], P(None, 'gx', 'gy', 'gz')
- gradient: float32 [16, 64, 128], P('gz', 'gx', 'gy')
Inputs may be any that keep to these rules, and one draw needn't show every extreme that they name: `layer_map`: every design layer owns one contiguous nonempty run of the 96 slab cells; the runs' order along the slab is arbitrary.
All inputs are finite; a program needn't handle non-finite values.
Results may differ from a plain program's by a relative error of at most 0.000073.
Values sent between devices are 32-bit elements; how exact they have to be, the bound alone decides.
No kernel may reach another device: no remote copies, remote signals or barrier semaphores. Data moves between devices by JAX's collectives and lax.ppermute only.
A program may use at most 128 MiB of HBM per device.

v0:
```python
import jax
import jax.numpy as jnp
from jax import lax
from jax.sharding import PartitionSpec as P

LAYERS = 16
STEP = 40


PERMITTIVITIES = (1.0, 2.1, 4.0, 12.0)
COURANT = 0.5


def shifted(x, axis, by):
    peers = lax.axis_size(axis)
    return lax.ppermute(x, axis, [(i, (i + by) % peers) for i in range(peers)])


def shifted_2(x, axis, by):
    peers = lax.axis_size(axis)
    pairs = [(i, i + by) for i in range(peers) if 0 <= i + by < peers]
    return lax.ppermute(x, axis, pairs)


def update_coefficient(material):
    result = jnp.zeros(material.shape, jnp.float32)
    for material_id, value_eps in enumerate(PERMITTIVITIES):
        result = result + jnp.where(material == material_id, COURANT / value_eps, 0.0).astype(
            jnp.float32
        )
    return result


def curl_forward(field_e, uppers):
    above_x, above_y, above_z = uppers
    comp_x = (
        above_y[..., 2, :, :, :]
        - field_e[..., 2, :, :, :]
        - (above_z[..., 1, :, :, :] - field_e[..., 1, :, :, :])
    )
    comp_y = (
        above_z[..., 0, :, :, :]
        - field_e[..., 0, :, :, :]
        - (above_x[..., 2, :, :, :] - field_e[..., 2, :, :, :])
    )
    comp_z = (
        above_x[..., 1, :, :, :]
        - field_e[..., 1, :, :, :]
        - (above_y[..., 0, :, :, :] - field_e[..., 0, :, :, :])
    )
    return jnp.stack([comp_x, comp_y, comp_z], axis=-4)


def curl_backward(field_h, lowers):
    below_x, below_y, below_z = lowers
    comp_x = (
        field_h[..., 2, :, :, :]
        - below_y[..., 2, :, :, :]
        - (field_h[..., 1, :, :, :] - below_z[..., 1, :, :, :])
    )
    comp_y = (
        field_h[..., 0, :, :, :]
        - below_z[..., 0, :, :, :]
        - (field_h[..., 2, :, :, :] - below_x[..., 2, :, :, :])
    )
    comp_z = (
        field_h[..., 1, :, :, :]
        - below_x[..., 1, :, :, :]
        - (field_h[..., 0, :, :, :] - below_y[..., 0, :, :, :])
    )
    return jnp.stack([comp_x, comp_y, comp_z], axis=-4)


def shards(
    e_forward,
    h_forward,
    e_adjoint,
    h_adjoint,
    material,
    dft_forward,
    dft_adjoint,
    angular_freq,
    layer_map,
):
    coefficient = update_coefficient(material)
    depth = e_forward.shape[3]
    gz_index = lax.axis_index("gz")
    gz_count = lax.axis_size("gz")
    both_e = jnp.stack([e_forward, e_adjoint])
    both_h = jnp.stack([h_forward, h_adjoint])
    from_x = shifted(both_e[:, :, :1], "gx", -1)
    from_y = shifted(both_e[:, :, :, :1], "gy", -1)
    from_z = shifted_2(both_e[:, :, :, :, :1], "gz", -1)
    uppers = (
        jnp.concatenate([both_e[:, :, 1:], from_x], axis=2),
        jnp.concatenate([both_e[:, :, :, 1:], from_y], axis=3),
        jnp.concatenate([both_e[:, :, :, :, 1:], from_z], axis=4),
    )
    new_h = both_h - COURANT * curl_forward(both_e, uppers)
    into_x = shifted(new_h[:, :, -1:], "gx", 1)
    into_y = shifted(new_h[:, :, :, -1:], "gy", 1)
    into_z = shifted_2(new_h[:, :, :, :, -1:], "gz", 1)
    lowers = (
        jnp.concatenate([into_x, new_h[:, :, :-1]], axis=2),
        jnp.concatenate([into_y, new_h[:, :, :, :-1]], axis=3),
        jnp.concatenate([into_z, new_h[:, :, :, :, :-1]], axis=4),
    )
    new_e = both_e + coefficient * curl_backward(new_h, lowers)
    slab_half = dft_forward.shape[3]
    slab_offset = (1 - gz_index) * (depth - slab_half)
    slab_cells = lax.dynamic_slice_in_dim(new_e, slab_offset, slab_half, axis=4)
    slab_cells = jnp.transpose(slab_cells, (0, 1, 4, 2, 3))
    phases = angular_freq * STEP
    cosine = jnp.cos(phases)[:, None, None, None, None]
    sine_term = jnp.sin(phases)[:, None, None, None, None]
    real_fwd = dft_forward[:, 0] + cosine * slab_cells[0][None]
    imag_fwd = dft_forward[:, 1] - sine_term * slab_cells[0][None]
    real_adj = dft_adjoint[:, 0] + cosine * slab_cells[1][None]
    imag_adj = dft_adjoint[:, 1] - sine_term * slab_cells[1][None]
    products = jnp.sum(real_fwd * real_adj - imag_fwd * imag_adj, axis=(0, 1))
    layer_ids = jnp.arange(LAYERS, dtype=jnp.int32)[:, None]
    local_map = lax.dynamic_slice_in_dim(layer_map, gz_index * slab_half, slab_half)
    local_onehot = (local_map[None, :] == layer_ids).astype(jnp.float32)
    partial_sums = jnp.einsum(
        "ls,sxy->lxy", local_onehot, products, precision=lax.Precision.HIGHEST
    )
    owned_sums = lax.psum_scatter(partial_sums, "gz", scatter_dimension=0, tiled=True)
    thickness = jnp.sum((layer_map[None, :] == layer_ids).astype(jnp.float32), axis=1)
    owned_count = LAYERS // gz_count
    owned_thickness = lax.dynamic_slice_in_dim(thickness, gz_index * owned_count, owned_count)
    gradient = owned_sums / (3.0 * owned_thickness)[:, None, None]
    return (new_e[0], new_h[0], new_e[1], new_h[1], gradient)


def solution(mesh):
    in_specs = (
        P(None, "gx", "gy", "gz"),
        P(None, "gx", "gy", "gz"),
        P(None, "gx", "gy", "gz"),
        P(None, "gx", "gy", "gz"),
        P("gx", "gy", "gz"),
        P(None, None, None, "gz", "gx", "gy"),
        P(None, None, None, "gz", "gx", "gy"),
        P(),
        P(),
    )
    out_specs = (
        P(None, "gx", "gy", "gz"),
        P(None, "gx", "gy", "gz"),
        P(None, "gx", "gy", "gz"),
        P(None, "gx", "gy", "gz"),
        P("gz", "gx", "gy"),
    )
    return jax.shard_map(shards, mesh=mesh, in_specs=in_specs, out_specs=out_specs, check_vma=False)
```

profile of v0, /device:TPU:0, one launch (start us, length us, event | category | flops | bytes accessed | tf_op | source)
XLA Modules:
  0.0 80.4 jit_solution(10091303249384446184)
XLA Ops:
  7.2 1.5 %fusion.6 = f32[2,3,16,32,1]{4,3,2,1,0:T(8,128)S(1)} fusion(f32[1,3,16,32,128]{4,3,2,1,0:T(8,128)} %bitcast.64, f32[1,3,16,32,128]{4,3,2,1,0:T(8,128)} %bitcast.56), kind=kLoop, calls=%fused_computation.29 | loop fusion | flops 3072 | bytes 1585152 | tf_op jit(solution)/shard_map/stack | solution.py:89
  8.7 1.2 %copy.79 = f32[2,3,16,32,1]{3,2,4,1,0:T(8,128)} copy(f32[2,3,16,32,1]{4,3,2,1,0:T(8,128)S(1)} %fusion.6) | data formatting | bytes 24576
  10.0 1.3 %collective-permute-start.1 = (f32[2,3,16,32,1]{3,2,4,1,0:T(8,128)}, f32[2,3,16,32,1]{3,2,4,1,0:T(8,128)}, u32[]{:S(2)}, u32[]{:S(2)}) collective-permute-start(f32[2,3,16,32,1]{3,2,4,1,0:T(8,128)} %copy.79), channel_id=1, source_target_pairs={{1,0},{3,2},{5,4},{7,6},{9,8},{11,10},{13,12},{15,14},{17,16},{19,... | collective-permute-start | bytes 36872 | tf_op jit(solution)/shard_map/ppermute | solution.py:22
  11.9 2.4 %collective-permute-start.2 = (f32[2,3,1,32,128]{4,3,2,1,0:T(8,128)}, f32[2,3,1,32,128]{4,3,2,1,0:T(8,128)S(1)}, u32[]{:S(2)}, u32[]{:S(2)}) collective-permute-start(f32[2,3,1,32,128]{4,3,2,1,0:T(8,128)} %fusion.24), channel_id=1, source_target_pairs={{0,24},{8,0},{16,8},{24,16},{1,25},{9,1},{17,9},{25,17},{2,26},{10... | collective-permute-start | bytes 294920 | tf_op jit(solution)/shard_map/ppermute | solution.py:16
  15.0 3.6 %collective-permute-start = (f32[2,3,16,1,128]{4,2,3,1,0:T(8,128)}, f32[2,3,16,1,128]{4,2,3,1,0:T(8,128)S(1)}, u32[]{:S(2)}, u32[]{:S(2)}) collective-permute-start(f32[2,3,16,1,128]{4,2,3,1,0:T(8,128)} %bitcast.17), channel_id=1, source_target_pairs={{0,6},{2,0},{4,2},{6,4},{1,7},{3,1},{5,3},{7,5},{8,14},{10,8},{12,... | collective-permute-start | bytes 147464 | tf_op jit(solution)/shard_map/ppermute | solution.py:16
  18.8 1.6 %fusion.5 = f32[2,3,16,32,127]{4,3,2,1,0:T(8,128)} fusion(f32[1,3,16,32,128]{4,3,2,1,0:T(8,128)S(1)} %bitcast.68, f32[1,3,16,32,128]{4,3,2,1,0:T(8,128)S(1)} %bitcast.60), kind=kLoop, calls=%fused_computation.28 | loop fusion | flops 390144 | bytes 3133440 | tf_op jit(solution)/shard_map/stack | solution.py:89
  20.5 1.3 %fusion.8 = f32[2,3,15,32,128]{4,3,2,1,0:T(8,128)} fusion(f32[1,3,16,32,128]{4,3,2,1,0:T(8,128)S(1)} %bitcast.69, f32[1,3,16,32,128]{4,3,2,1,0:T(8,128)S(1)} %bitcast.61), kind=kLoop, calls=%fused_computation.37 | loop fusion | flops 368640 | bytes 3047424 | tf_op jit(solution)/shard_map/stack | solution.py:89
  23.1 1.3 %convert_reduce_fusion = f32[16]{0:T(128)} fusion(s32[96]{0:T(128)} %param.17), kind=kLoop, calls=%fused_computation.75 | loop fusion | flops 4592 | bytes 448 | tf_op jit(solution)/shard_map/reduce_sum | solution.py:128
  24.4 1.3 %dynamic-slice_multiply_fusion = f32[8]{0:T(128)} fusion(f32[16]{0:T(128)} %convert_reduce_fusion, s32[]{:T(128)S(6)} %select_n.28), kind=kLoop, calls=%fused_computation.81 | loop fusion | flops 8 | bytes 68 | tf_op jit(solution)/shard_map/mul | solution.py:131
  25.7 1.3 %dynamic_slice.9 = s32[48]{0:T(128)} dynamic-slice(s32[96]{0:T(128)} %param.17, s32[]{:T(128)S(6)} %select_n.26), dynamic_slice_sizes={48} | dynamic-slice | bytes 388 | tf_op jit(solution)/shard_map/dynamic_slice | solution.py:122
  27.0 2.6 %copy.64 = f32[2,3,16,32,1]{4,3,2,1,0:T(8,128)} copy(f32[2,3,16,32,1]{3,2,4,1,0:T(8,128)} %collective-permute-done.1) | data formatting | bytes 24576 | tf_op jit(solution)/shard_map/ppermute | solution.py:22
  29.6 2.7 %fusion.23 = (f32[2,1,16,32,128]{4,3,2,1,0:T(8,128)S(1)}, f32[2,1,16,32,128]{4,3,2,1,0:T(8,128)S(1)}, f32[2,1,16,32,128]{4,3,2,1,0:T(8,128)S(1)}) fusion(f32[2,3,16,32,1]{4,3,2,1,0:T(8,128)} %copy.64, f32[2,3,16,32,127]{4,3,2,1,0:T(8,128)} %fusion.5, f32[2,3,16,1,128]{4,3,2,1,0:T(1,128)S(1)} %bitcast.78, f32[2,3,16,31,128]{4,3,2,1,0:T(8,128)S(1)} %fusion.4, ...), kind=kLoop, calls=%fused_computation.69 | loop fusion | flops 2752512 | bytes 7864320 | tf_op jit(solution)/shard_map/sub | solution.py:37
  32.6 2.2 %copy_subtract_fusion = f32[2,3,16,32,128]{4,2,3,1,0:T(8,128)S(1)} fusion(f32[2,3,16,32,128]{4,3,2,1,0:T(8,128)S(1)} %get-tuple-element.39, f32[2,3,16,32,128]{4,3,2,1,0:T(8,128)S(1)} %get-tuple-element.40), kind=kLoop, calls=%fused_computation.34 | loop fusion | flops 786432 | bytes 4718592 | tf_op jit(solution)/shard_map/sub | solution.py:99
  34.9 1.6 %slice.190 = f32[2,3,16,32,1]{4,2,3,1,0:T(8,128)} slice(f32[2,3,16,32,128]{4,2,3,1,0:T(8,128)S(1)} %copy_subtract_fusion), slice={[0:2], [0:3], [0:16], [0:32], [127:128]} | slice | bytes 24576 | tf_op jit(solution)/shard_map/slice | solution.py:102
  37.8 2.7 %copy.67 = f32[2,3,16,32,1]{3,2,4,1,0:T(8,128)} copy(f32[2,3,16,32,1]{4,2,3,1,0:T(8,128)} %slice.190) | data formatting | bytes 24576 | tf_op jit(solution)/shard_map/slice | solution.py:102
  40.5 5.5 %collective-permute-start.4 = (f32[2,3,16,32,1]{3,2,4,1,0:T(8,128)}, f32[2,3,16,32,1]{3,2,4,1,0:T(8,128)}, u32[]{:S(2)}, u32[]{:S(2)}) collective-permute-start(f32[2,3,16,32,1]{3,2,4,1,0:T(8,128)} %copy.67), channel_id=1, source_target_pairs={{0,1},{2,3},{4,5},{6,7},{8,9},{10,11},{12,13},{14,15},{16,17},{18,... | collective-permute-start | bytes 36872 | tf_op jit(solution)/shard_map/ppermute | solution.py:22
  46.1 1.3 %slice.188 = f32[2,3,16,31,128]{4,2,3,1,0:T(8,128)} slice(f32[2,3,16,32,128]{4,2,3,1,0:T(8,128)S(1)} %copy_subtract_fusion), slice={[0:2], [0:3], [0:16], [0:31], [0:128]} | slice | bytes 3047424 | tf_op jit(solution)/shard_map/slice | solution.py:105
  49.7 2.6 %copy.68 = f32[2,3,16,32,1]{4,2,3,1,0:T(8,128)} copy(f32[2,3,16,32,1]{3,2,4,1,0:T(8,128)} %collective-permute-done.4) | data formatting | bytes 24576 | tf_op jit(solution)/shard_map/ppermute | solution.py:22
  52.6 2.0 %fusion.17 = (f32[2,1,16,32,128]{4,2,3,1,0:T(8,128)S(1)}, f32[2,1,16,32,128]{4,2,3,1,0:T(8,128)S(1)}, f32[2,1,16,32,128]{4,2,3,1,0:T(8,128)S(1)}) fusion(f32[2,3,16,32,127]{4,2,3,1,0:T(8,128)S(1)} %bitcast.54, f32[2,3,16,32,1]{4,2,3,1,0:T(8,128)} %copy.68, f32[2,3,16,31,128]{4,2,3,1,0:T(8,128)} %slice.188, ...), kind=kLoop, calls=%fused_computation.57 | loop fusion | flops 1966080 | bytes 7864320 | tf_op jit(solution)/shard_map/sub | solution.py:57
  57.0 1.3 %slice-done.2 = s8[4194304]{0:T(1024)(128)(4,1)S(1)} async-done(((s8[4718592]{0:T(1024)(128)(4,1)}), s8[4194304]{0:T(1024)(128)(4,1)S(1)}, s32[]{:S(2)}) %slice-start.2) | async-done | bytes 4194328
  58.5 1.5 %fusion.2 = f32[48,16,32]{0,2,1:T(8,128)S(1)} fusion(f32[3,2,3,48,16,32]{3,5,4,2,1,0:T(8,128)S(1)} %bitcast.73, f32[3,2,3,48,16,32]{3,5,4,2,1,0:T(8,128)S(1)} %bitcast.75, f32[3]{0:T(128)S(1)} %copy-done.7, f32[3,48,16,32]{1,3,2,0:T(8,128)S(1)} %get-tuple-element.32, f32[3,48,16,32]{1,3,2,0:T(8,128)S(1)} %get-tuple-element.31, f32[3]{0:T(128)S(1)} %copy-done.6), kind=kLoop, calls=%fused_computation.22 | loop fusion | flops 2629632 | bytes 4227096 | tf_op jit(solution)/shard_map/reduce_sum | solution.py:120
  60.0 1.3 %fusion.27 = f32[16,16,32]{2,0,1:T(8,128)} fusion(f32[48,16,32]{0,2,1:T(8,128)S(1)} %fusion.2, s32[48]{0:T(128)S(1)} %copy-done.8), kind=kOutput, calls=%fused_computation.79 | convolution fusion | flops 4719360 | bytes 131264 | tf_op jit(solution)/shard_map/ls,sxy->lxy/dot_general | solution.py:124
  61.3 1.3 %slice_bitcast_fusion.3 = (f32[3,16,32,128]{3,2,1,0:T(8,128)}, f32[3,16,32,128]{3,2,1,0:T(8,128)}) fusion(f32[2,3,16,32,128]{4,3,2,1,0:T(8,128)S(1)} %fusion.7), kind=kLoop, calls=%fused_computation.41 | loop fusion | bytes 3145728 | tf_op jit(solution)/shard_map/squeeze | solution.py:132
  62.6 9.4 %reduce-scatter.2.cloned.1.call-done = f32[8,16,32]{2,0,1:T(8,128)} async-done(((f32[16,16,32]{2,0,1:T(8,128)}), f32[8,16,32]{2,0,1:T(8,128)}) %reduce-scatter.2.cloned.1.call-update) | async-done | bytes 16400 | tf_op jit(solution)/shard_map/reduce_scatter | solution.py:127
  (56 shorter events, 11.5 us)
Async XLA Ops:
  7.2 64.8 %reduce-scatter.2.cloned.1.call-start = ((), (), s32[]{:S(2)}) async-start(), calls=%async_computation.1 | async-start | bytes 196608 | tf_op jit(solution)/shard_map/reduce_scatter | solution.py:127
  8.7 2.6 %copy-start = (f32[3,16,32,128]{3,2,1,0:T(8,128)S(1)}, f32[3,16,32,128]{3,2,1,0:T(8,128)}, u32[]{:S(2)}) copy-start(f32[3,16,32,128]{3,2,1,0:T(8,128)} %param.11) | copy-start | bytes 2359300
  8.7 2.6 %copy-start.1 = (f32[3,16,32,128]{3,2,1,0:T(8,128)S(1)}, f32[3,16,32,128]{3,2,1,0:T(8,128)}, u32[]{:S(2)}) copy-start(f32[3,16,32,128]{3,2,1,0:T(8,128)} %param.9) | copy-start | bytes 2359300
  10.0 17.0 %collective-permute-start.1 = (f32[2,3,16,32,1]{3,2,4,1,0:T(8,128)}, f32[2,3,16,32,1]{3,2,4,1,0:T(8,128)}, u32[]{:S(2)}, u32[]{:S(2)}) collective-permute-start(f32[2,3,16,32,1]{3,2,4,1,0:T(8,128)} %copy.79), channel_id=1, source_target_pairs={{1,0},{3,2},{5,4},{7,6},{9,8},{11,10},{13,12},{15,14},{17,16},{19,... | collective-permute-start | bytes 36872 | tf_op jit(solution)/shard_map/ppermute | solution.py:22
  11.9 17.6 %collective-permute-start.2 = (f32[2,3,1,32,128]{4,3,2,1,0:T(8,128)}, f32[2,3,1,32,128]{4,3,2,1,0:T(8,128)S(1)}, u32[]{:S(2)}, u32[]{:S(2)}) collective-permute-start(f32[2,3,1,32,128]{4,3,2,1,0:T(8,128)} %fusion.24), channel_id=1, source_target_pairs={{0,24},{8,0},{16,8},{24,16},{1,25},{9,1},{17,9},{25,17},{2,26},{10... | collective-permute-start | bytes 294920 | tf_op jit(solution)/shard_map/ppermute | solution.py:16
  15.0 14.6 %collective-permute-start = (f32[2,3,16,1,128]{4,2,3,1,0:T(8,128)}, f32[2,3,16,1,128]{4,2,3,1,0:T(8,128)S(1)}, u32[]{:S(2)}, u32[]{:S(2)}) collective-permute-start(f32[2,3,16,1,128]{4,2,3,1,0:T(8,128)} %bitcast.17), channel_id=1, source_target_pairs={{0,6},{2,0},{4,2},{6,4},{1,7},{3,1},{5,3},{7,5},{8,14},{10,8},{12,... | collective-permute-start | bytes 147464 | tf_op jit(solution)/shard_map/ppermute | solution.py:16
  20.5 1.3 %copy-start.4 = (s32[16,32,128]{2,1,0:T(8,128)S(1)}, s32[16,32,128]{2,1,0:T(8,128)}, u32[]{:S(2)}) copy-start(s32[16,32,128]{2,1,0:T(8,128)} %param.13) | copy-start | bytes 786436
  29.6 2.7 %copy-start.2 = (f32[3,16,32,128]{3,2,1,0:T(8,128)S(1)}, f32[3,16,32,128]{3,2,1,0:T(8,128)}, u32[]{:S(2)}) copy-start(f32[3,16,32,128]{3,2,1,0:T(8,128)} %param.12) | copy-start | bytes 2359300
  29.6 2.7 %copy-start.3 = (f32[3,16,32,128]{3,2,1,0:T(8,128)S(1)}, f32[3,16,32,128]{3,2,1,0:T(8,128)}, u32[]{:S(2)}) copy-start(f32[3,16,32,128]{3,2,1,0:T(8,128)} %param.10) | copy-start | bytes 2359300
  40.5 9.2 %collective-permute-start.4 = (f32[2,3,16,32,1]{3,2,4,1,0:T(8,128)}, f32[2,3,16,32,1]{3,2,4,1,0:T(8,128)}, u32[]{:S(2)}, u32[]{:S(2)}) collective-permute-start(f32[2,3,16,32,1]{3,2,4,1,0:T(8,128)} %copy.67), channel_id=1, source_target_pairs={{0,1},{2,3},{4,5},{6,7},{8,9},{10,11},{12,13},{14,15},{16,17},{18,... | collective-permute-start | bytes 36872 | tf_op jit(solution)/shard_map/ppermute | solution.py:22
  46.0 6.6 %collective-permute-start.5 = (f32[2,3,1,32,128]{4,2,3,1,0:T(1,128)}, f32[2,3,1,32,128]{4,2,3,1,0:T(1,128)S(1)}, u32[]{:S(2)}, u32[]{:S(2)}) collective-permute-start(f32[2,3,1,32,128]{4,2,3,1,0:T(1,128)} %slice.193), channel_id=1, source_target_pairs={{0,8},{8,16},{16,24},{24,0},{1,9},{9,17},{17,25},{25,1},{2,10},{10... | collective-permute-start | bytes 294920 | tf_op jit(solution)/shard_map/ppermute | solution.py:16
  46.0 6.6 %collective-permute-start.3 = (f32[2,3,16,1,128]{4,2,3,1,0:T(8,128)}, f32[2,3,16,1,128]{4,2,3,1,0:T(8,128)S(1)}, u32[]{:S(2)}, u32[]{:S(2)}) collective-permute-start(f32[2,3,16,1,128]{4,2,3,1,0:T(8,128)} %slice.187), channel_id=1, source_target_pairs={{0,2},{2,4},{4,6},{6,0},{1,3},{3,5},{5,7},{7,1},{8,10},{10,12},{12... | collective-permute-start | bytes 147464 | tf_op jit(solution)/shard_map/ppermute | solution.py:16
  54.8 2.2 %slice-start = ((s8[4718592]{0:T(1024)(128)(4,1)}), s8[4194304]{0:T(1024)(128)(4,1)S(1)}, s32[]{:S(2)}) async-start(s8[4718592]{0:T(1024)(128)(4,1)} %bitcast.72), calls=%async_computation.2 | async-start | bytes 8388608
  54.8 3.5 %slice-start.2 = ((s8[4718592]{0:T(1024)(128)(4,1)}), s8[4194304]{0:T(1024)(128)(4,1)S(1)}, s32[]{:S(2)}) async-start(s8[4718592]{0:T(1024)(128)(4,1)} %bitcast.74), calls=%async_computation.4 | async-start | bytes 8388608
  55.1 3.2 %slice-start.1 = ((s8[4718592]{0:T(1024)(128)(4,1)}), s8[524288]{0:T(1024)(128)(4,1)S(1)}, s32[]{:S(2)}) async-start(s8[4718592]{0:T(1024)(128)(4,1)} %bitcast.72), calls=%async_computation.3 | async-start | bytes 1048576
  55.1 3.4 %slice-start.3 = ((s8[4718592]{0:T(1024)(128)(4,1)}), s8[524288]{0:T(1024)(128)(4,1)S(1)}, s32[]{:S(2)}) async-start(s8[4718592]{0:T(1024)(128)(4,1)} %bitcast.74), calls=%async_computation.5 | async-start | bytes 1048576
  56.0 2.5 %copy-start.6 = (f32[3]{0:T(128)S(1)}, f32[3]{0:T(128)}, u32[]{:S(2)}) copy-start(f32[3]{0:T(128)} %get-tuple-element.37) | copy-start | bytes 40
  56.0 2.5 %copy-start.7 = (f32[3]{0:T(128)S(1)}, f32[3]{0:T(128)}, u32[]{:S(2)}) copy-start(f32[3]{0:T(128)} %get-tuple-element.38) | copy-start | bytes 40
  58.5 1.5 %copy-start.8 = (s32[48]{0:T(128)S(1)}, s32[48]{0:T(128)}, u32[]{:S(2)}) copy-start(s32[48]{0:T(128)} %dynamic_slice.9) | copy-start | bytes 580
  61.3 10.6 %copy-start.5 = (f32[8]{0:T(128)S(1)}, f32[8]{0:T(128)}, u32[]{:S(2)}) copy-start(f32[8]{0:T(128)} %dynamic-slice_multiply_fusion) | copy-start | bytes 100
Sparse Core Ops, SparseCore 0:
  61.4 10.4 reduce-scatter.1
where the time goes:
time: 80.8 us; the launch traced here: 80.4 us
  local copies, waits for them, and re-layouts  22.4 us (28%)
  other arithmetic  19.9 us (25%)
  between operations  14.3 us (18%)
  starting transfers between devices  12.8 us (16%)
  waiting for transfers between devices  9.71 us (12%)
  matrix products  1.27 us (2%)
    reduce_scatter x1, waiting for transfers between devices, shards(): lax.psum_scatter(partial_sums, 'gz', scatter_dimension=0, tiled=True)  9.36 us
    ppermute x2, starting transfers between devices, shifted_2(): return lax.ppermute(x, axis, pairs)  6.75 us
    unnamed x30, local copies, waits for them, and re-layouts  6.51 us
    ppermute x4, starting transfers between devices, shifted(): return lax.ppermute(x, axis, [(i, (i + by) % peers) for i in range(peers)])  5.99 us
    another operation x6, other arithmetic, shards(): both_e = jnp.stack([e_forward, e_adjoint])  5.97 us
    ppermute x2, local copies, waits for them, and re-layouts, shifted_2(): return lax.ppermute(x, axis, pairs)  5.18 us
    slice x2, local copies, waits for them, and re-layouts, shards(): into_z = shifted_2(new_h[:, :, :, :, -1:], 'gz', 1)  4.29 us
    sub x1, other arithmetic, curl_forward(): above_y[..., 2, :, :, :] - field_e[..., 2, :, :, :]  2.67 us
  transfers between devices with their start and end apart: 7, of which 2 were waited for; matrix products, arithmetic and copies ran while one was open for 25% of the time, Pallas kernels for 0%

commit v1 on v0

v1 whole, which is shorter than its diff:
```python
import functools

import jax
import jax.numpy as jnp
from jax import lax
from jax.experimental import pallas as pl
from jax.experimental.pallas import tpu as pltpu
from jax.sharding import PartitionSpec as P

LAYERS = 16
STEP = 40
PERMITTIVITIES = (1.0, 2.1, 4.0, 12.0)
COURANT = 0.5
LANES = 128
VMEM_LIMIT = 48 * 1024 * 1024
ANY = pl.BlockSpec(memory_space=pl.ANY)
VMEM = pl.BlockSpec(memory_space=pltpu.VMEM)


def f32(*shape):
    return jax.ShapeDtypeStruct(shape, jnp.float32)


def ring(x, axis, by):
    peers = lax.axis_size(axis)
    return lax.ppermute(x, axis, [(i, (i + by) % peers) for i in range(peers)])


def line(x, axis, by):
    peers = lax.axis_size(axis)
    return lax.ppermute(x, axis, [(i, i + by) for i in range(peers) if 0 <= i + by < peers])


def call(body, outs, out_specs, in_specs, scratch, flops, nbytes, name):
    return pl.pallas_call(
        body,
        out_shape=outs,
        in_specs=in_specs,
        out_specs=out_specs,
        scratch_shapes=scratch,
        compiler_params=pltpu.CompilerParams(vmem_limit_bytes=VMEM_LIMIT),
        cost_estimate=pl.CostEstimate(flops=flops, bytes_accessed=nbytes, transcendentals=0),
        name=name,
    )


def lane_ids(rows):
    return lax.broadcasted_iota(jnp.int32, (rows, LANES), 1)


def row_ids(rows):
    return lax.broadcasted_iota(jnp.int32, (rows, LANES), 0)


def column(a, lane):
    return jnp.broadcast_to(a[:, lane : lane + 1], a.shape)


def up_y(a, row):
    n = a.shape[0]
    return jnp.where(row_ids(n) == n - 1, jnp.broadcast_to(row, a.shape), pltpu.roll(a, n - 1, 0))


def down_y(a, row):
    return jnp.where(row_ids(a.shape[0]) == 0, jnp.broadcast_to(row, a.shape), pltpu.roll(a, 1, 0))


def up_z(a, col):
    n = a.shape[1]
    return jnp.where(lane_ids(a.shape[0]) == n - 1, col, pltpu.roll(a, n - 1, 1))


def down_z(a, col):
    return jnp.where(lane_ids(a.shape[0]) == 0, col, pltpu.roll(a, 1, 1))


def first_faces_body(nx, chunk, ef, ea, xs, ys, zs, xy, zrow, sems):
    fields = (ef, ea)
    copies = {}
    for r, e in enumerate(fields):
        copies[r, "x"] = pltpu.make_async_copy(e.at[1:3, 0], xs.at[r], sems.at[r, 0])
        copies[r, "z"] = pltpu.make_async_copy(e.at[2, :, 0:8], zrow.at[r], sems.at[r, 1])
        for i in range(nx // chunk):
            part = pl.ds(i * chunk, chunk)
            copies[r, i] = pltpu.make_async_copy(e.at[0:2, part], xy.at[r, :, part], sems.at[r, 2 + i])
    for i in range(nx // chunk):
        for r in range(2):
            copies[r, i].start()
    for r in range(2):
        copies[r, "x"].start()
        copies[r, "z"].start()
    ny = xy.shape[3]
    lane = lane_ids(ny)
    total = jnp.zeros((ny, LANES), jnp.float32)
    for i in range(nx // chunk):
        for r in range(2):
            copies[r, i].wait()
            for x in range(i * chunk, (i + 1) * chunk):
                for c in range(2):
                    a = xy[r, c, x]
                    total = jnp.where(lane == (r * 2 + c) * nx + x, column(a, 0), total)
                ys[r, 0, x : x + 1, :] = xy[r, 0, x, 0:1, :]
    zs[...] = total
    for r in range(2):
        copies[r, "x"].wait()
        copies[r, "z"].wait()
        for x in range(nx):
            ys[r, 1, x : x + 1, :] = zrow[r, x, 0:1, :]


def first_faces(ef, ea):
    _, nx, ny, nz = ef.shape
    chunk = 4
    return call(
        functools.partial(first_faces_body, nx, chunk),
        (f32(2, 2, ny, nz), f32(2, 2, nx, nz), f32(ny, LANES)),
        (VMEM, VMEM, VMEM),
        [ANY, ANY],
        [
            pltpu.VMEM((2, 2, nx, ny, nz), jnp.float32),
            pltpu.VMEM((2, nx, 8, nz), jnp.float32),
            pltpu.SemaphoreType.DMA((2, 2 + nx // chunk)),
        ],
        1000,
        1500000,
        "first_faces",
    )(ef, ea)


def magnetic_body(nx, chunk, ef, hf, ea, ha, xr, yr, zr, hfn, han, xs, ys, zs, ev, hv, insem, outsem):
    runs = ((ef, hf, hfn), (ea, ha, han))
    ny, nz = ev.shape[3], ev.shape[4]
    n = nx // chunk
    copies, outs = {}, {}
    for i in range(n):
        part = pl.ds(i * chunk, chunk)
        for r, (e, h, hn) in enumerate(runs):
            copies[r, i, 0] = pltpu.make_async_copy(e.at[:, part], ev.at[r, :, part], insem.at[r, i, 0])
            copies[r, i, 1] = pltpu.make_async_copy(h.at[:, part], hv.at[r, :, part], insem.at[r, i, 1])
            outs[r, i] = pltpu.make_async_copy(hv.at[r, :, part], hn.at[:, part], outsem.at[r, i])
    for i in range(n):
        for r in range(2):
            copies[r, i, 0].start()
            copies[r, i, 1].start()
    lane = lane_ids(ny)
    total = jnp.zeros((ny, LANES), jnp.float32)
    zcol = zr[...]
    for i in range(n):
        for r in range(2):
            if i == 0:
                copies[r, 0, 0].wait()
            copies[r, i, 1].wait()
            if i + 1 < n:
                copies[r, i + 1, 0].wait()
            for x in range(i * chunk, (i + 1) * chunk):
                ex, ey, ez = ev[r, 0, x], ev[r, 1, x], ev[r, 2, x]
                ey_x, ez_x = (ev[r, 1, x + 1], ev[r, 2, x + 1]) if x + 1 < nx else (xr[r, 0], xr[r, 1])
                ex_y = up_y(ex, yr[r, 0, x : x + 1, :])
                ez_y = up_y(ez, yr[r, 1, x : x + 1, :])
                ex_z = up_z(ex, column(zcol, (r * 2 + 0) * nx + x))
                ey_z = up_z(ey, column(zcol, (r * 2 + 1) * nx + x))
                hx = hv[r, 0, x] - COURANT * ((ez_y - ez) - (ey_z - ey))
                hy = hv[r, 1, x] - COURANT * ((ex_z - ex) - (ez_x - ez))
                hz = hv[r, 2, x] - COURANT * ((ey_x - ey) - (ex_y - ex))
                hv[r, 0, x] = hx
                hv[r, 1, x] = hy
                hv[r, 2, x] = hz
                ys[r, 0, x : x + 1, :] = hx[ny - 1 : ny, :]
                ys[r, 1, x : x + 1, :] = hz[ny - 1 : ny, :]
                total = jnp.where(lane == (r * 2 + 0) * nx + x, column(hx, nz - 1), total)
                total = jnp.where(lane == (r * 2 + 1) * nx + x, column(hy, nz - 1), total)
                if x == nx - 1:
                    xs[r, 0] = hy
                    xs[r, 1] = hz
            outs[r, i].start()
    zs[...] = total
    for i in range(n):
        for r in range(2):
            outs[r, i].wait()


def magnetic(ef, hf, ea, ha, xr, yr, zr):
    _, nx, ny, nz = ef.shape
    chunk = 4
    field = f32(3, nx, ny, nz)
    return call(
        functools.partial(magnetic_body, nx, chunk),
        (field, field, f32(2, 2, ny, nz), f32(2, 2, nx, nz), f32(ny, LANES)),
        (ANY, ANY, VMEM, VMEM, VMEM),
        [ANY, ANY, ANY, ANY, VMEM, VMEM, VMEM],
        [
            pltpu.VMEM((2, 3, nx, ny, nz), jnp.float32),
            pltpu.VMEM((2, 3, nx, ny, nz), jnp.float32),
            pltpu.SemaphoreType.DMA((2, nx // chunk, 2)),
            pltpu.SemaphoreType.DMA((2, nx // chunk)),
        ],
        6000000,
        4800000,
        "magnetic",
    )(ef, hf, ea, ha, xr, yr, zr)


def slab_start(nz, half):
    return (1 - lax.axis_index("gz")) * (nz - half)


def spectra_body(half, nz, df, da, freq, out):
    phase = freq[...] * float(STEP)
    cos, sin = jnp.cos(phase), jnp.sin(phase)
    freqs, xc, ny = df.shape[0], df.shape[3], df.shape[4]
    shift = slab_start(nz, half)
    blank = jnp.zeros((ny, LANES - half), jnp.float32)

    def place(a):
        return pltpu.roll(jnp.concatenate([a, blank], axis=1), shift, 1)

    cs = [jnp.broadcast_to(cos[:, f : f + 1], (ny, half)) for f in range(freqs)]
    sn = [jnp.broadcast_to(sin[:, f : f + 1], (ny, half)) for f in range(freqs)]
    for x in range(xc):
        base = jnp.zeros((ny, half), jnp.float32)
        for c in range(3):
            with_forward = jnp.zeros((ny, half), jnp.float32)
            with_adjoint = jnp.zeros((ny, half), jnp.float32)
            for f in range(freqs):
                rf, jf, ra, ja = df[f, 0, c, x], df[f, 1, c, x], da[f, 0, c, x], da[f, 1, c, x]
                base = base + (rf * ra - jf * ja)
                with_forward = with_forward + (cs[f] * ra + sn[f] * ja)
                with_adjoint = with_adjoint + (cs[f] * rf + sn[f] * jf)
            out[1 + c, x] = place(with_forward)
            out[4 + c, x] = place(with_adjoint)
        out[0, x] = place(base)


def spectra(df, da, freq, nz):
    freqs, _, _, nx, ny, half = df.shape
    chunk = 2
    spec = pl.BlockSpec((freqs, 2, 3, chunk, ny, half), lambda i: (0, 0, 0, i, 0, 0))
    return pl.pallas_call(
        functools.partial(spectra_body, half, nz),
        out_shape=f32(7, nx, ny, LANES),
        grid=(nx // chunk,),
        in_specs=[spec, spec, pl.BlockSpec((1, freqs), lambda i: (0, 0))],
        out_specs=pl.BlockSpec((7, chunk, ny, LANES), lambda i: (0, i, 0, 0)),
        compiler_params=pltpu.CompilerParams(vmem_limit_bytes=VMEM_LIMIT),
        cost_estimate=pl.CostEstimate(flops=10000000, bytes_accessed=11000000, transcendentals=0),
        name="spectra",
    )(df, da, freq)


def electric_body(
    nx, chunk, half, ef, ea, hf, ha, material, xr, yr, zr, spec, freq, layer_map,
    efn, ean, own, other, ev, hv, mv, sv, insem, outsem,
):
    runs = ((ef, hf, efn), (ea, ha, ean))
    ny, nz = ev.shape[3], ev.shape[4]
    n = nx // chunk
    copies, outs = {}, {}
    for i in range(n):
        part = pl.ds(i * chunk, chunk)
        for r, (e, h, en) in enumerate(runs):
            copies[i, r] = pltpu.make_async_copy(h.at[:, part], hv.at[r, :, part], insem.at[i, r])
            copies[i, 2 + r] = pltpu.make_async_copy(e.at[:, part], ev.at[r, :, part], insem.at[i, 2 + r])
            outs[i, r] = pltpu.make_async_copy(ev.at[r, :, part], en.at[:, part], outsem.at[i, r])
        copies[i, 4] = pltpu.make_async_copy(material.at[part], mv.at[part], insem.at[i, 4])
        copies[i, 5] = pltpu.make_async_copy(spec.at[:, part], sv.at[:, part], insem.at[i, 5])
    for i in range(n):
        for k in range(6):
            copies[i, k].start()
    phase = freq[...] * float(STEP)
    cos, sin = jnp.cos(phase), jnp.sin(phase)
    both = jnp.sum(cos * cos - sin * sin, axis=1, keepdims=True)
    gz = lax.axis_index("gz")
    start = slab_start(nz, half)
    slab = layer_map.shape[1]
    cells = jnp.concatenate([layer_map[...], jnp.full((1, LANES - slab), -1, jnp.int32)], axis=1)
    cells = pltpu.roll(jnp.broadcast_to(cells, (8, LANES)), lax.rem(start + LANES - gz * half, LANES), 1)
    owned = own.shape[0]
    lane = lane_ids(owned)
    inside = (lane >= start) & (lane < start + half)
    cells = jnp.broadcast_to(cells[0:1, :], (owned, LANES))
    layer = row_ids(owned)
    own_hot = jnp.where(inside & (cells == layer + gz * owned), 1.0, 0.0)
    other_hot = jnp.where(inside & (cells == layer + (1 - gz) * owned), 1.0, 0.0)
    zcol = zr[...]
    for i in range(n):
        for k in range(6):
            copies[i, k].wait()
        products = []
        for x in range(i * chunk, (i + 1) * chunk):
            m = mv[x]
            coefficient = jnp.where(
                m == 0,
                COURANT / PERMITTIVITIES[0],
                jnp.where(
                    m == 1,
                    COURANT / PERMITTIVITIES[1],
                    jnp.where(m == 2, COURANT / PERMITTIVITIES[2], COURANT / PERMITTIVITIES[3]),
                ),
            )
            news = []
            for r in range(2):
                hx, hy, hz = hv[r, 0, x], hv[r, 1, x], hv[r, 2, x]
                hy_x, hz_x = (hv[r, 1, x - 1], hv[r, 2, x - 1]) if x else (xr[r, 0], xr[r, 1])
                hx_y = down_y(hx, yr[r, 0, x : x + 1, :])
                hz_y = down_y(hz, yr[r, 1, x : x + 1, :])
                hx_z = down_z(hx, column(zcol, (r * 2 + 0) * nx + x))
                hy_z = down_z(hy, column(zcol, (r * 2 + 1) * nx + x))
                ex = ev[r, 0, x] + coefficient * ((hz - hz_y) - (hy - hy_z))
                ey = ev[r, 1, x] + coefficient * ((hx - hx_z) - (hz - hz_x))
                ez = ev[r, 2, x] + coefficient * ((hy - hy_x) - (hx - hx_y))
                ev[r, 0, x] = ex
                ev[r, 1, x] = ey
                ev[r, 2, x] = ez
                news.append((ex, ey, ez))
            total = sv[0, x]
            for c in range(3):
                f, a = news[0][c], news[1][c]
                total = total + (f * (sv[1 + c, x] + both * a) + a * sv[4 + c, x])
            products.append(total)
        for r in range(2):
            outs[i, r].start()
        block = jnp.concatenate(products, axis=0)
        dims = (((1,), (1,)), ((), ()))
        where = pl.ds(i * chunk * ny, chunk * ny)
        for hot, result in ((own_hot, own), (other_hot, other)):
            result[:, where] = lax.dot_general(
                hot, block, dims, precision=lax.Precision.HIGHEST, preferred_element_type=jnp.float32
            )
    for i in range(n):
        for r in range(2):
            outs[i, r].wait()


def electric(ef, ea, hf, ha, material, xr, yr, zr, spec, freq, layer_map, half, owned):
    _, nx, ny, nz = ef.shape
    chunk = 4
    field = f32(3, nx, ny, nz)
    return call(
        functools.partial(electric_body, nx, chunk, half),
        (field, field, f32(owned, nx * ny), f32(owned, nx * ny)),
        (ANY, ANY, VMEM, VMEM),
        [ANY, ANY, ANY, ANY, ANY, VMEM, VMEM, VMEM, ANY, VMEM, VMEM],
        [
            pltpu.VMEM((2, 3, nx, ny, nz), jnp.float32),
            pltpu.VMEM((2, 3, nx, ny, nz), jnp.float32),
            pltpu.VMEM((nx, ny, nz), jnp.int32),
            pltpu.VMEM((7, nx, ny, LANES), jnp.float32),
            pltpu.SemaphoreType.DMA((nx // chunk, 6)),
            pltpu.SemaphoreType.DMA((nx // chunk, 2)),
        ],
        9000000,
        6700000,
        "electric",
    )(ef, ea, hf, ha, material, xr, yr, zr, spec, freq, layer_map)


def gradient_body(own, came, layer_map, out):
    owned, nx, ny = out.shape
    slab = layer_map.shape[1]
    layer = lax.broadcasted_iota(jnp.int32, (owned, slab), 0) + lax.axis_index("gz") * owned
    same = jnp.where(jnp.broadcast_to(layer_map[...], (owned, slab)) == layer, 1.0, 0.0)
    thickness = jnp.sum(same, axis=1, keepdims=True)
    result = (own[...] + came[...]) / (3.0 * thickness)
    for x in range(nx):
        out[:, x, :] = result[:, x * ny : (x + 1) * ny]


def gradient(own, came, layer_map, nx, ny):
    owned = own.shape[0]
    return call(
        gradient_body,
        f32(owned, nx, ny),
        VMEM,
        [VMEM, VMEM, VMEM],
        [],
        10000,
        100000,
        "gradient",
    )(own, came, layer_map)


def shards(ef, hf, ea, ha, material, df, da, angular_freq, layer_map):
    _, nx, ny, nz = ef.shape
    half = df.shape[3]
    owned = LAYERS // lax.axis_size("gz")
    freq = angular_freq.reshape(1, -1)
    layer_map = layer_map.reshape(1, -1)
    df = jnp.transpose(df, (0, 1, 2, 4, 5, 3))
    da = jnp.transpose(da, (0, 1, 2, 4, 5, 3))
    xs, ys, zs = first_faces(ef, ea)
    yr = ring(ys, "gy", -1)
    xr = ring(xs, "gx", -1)
    zr = line(zs, "gz", -1)
    spec = spectra(df, da, freq, nz)
    hfn, han, xs, ys, zs = magnetic(ef, hf, ea, ha, xr, yr, zr)
    yr = ring(ys, "gy", 1)
    xr = ring(xs, "gx", 1)
    zr = line(zs, "gz", 1)
    efn, ean, own, other = electric(ef, ea, hfn, han, material, xr, yr, zr, spec, freq, layer_map, half, owned)
    came = ring(other, "gz", 1)
    return efn, hfn, ean, han, gradient(own, came, layer_map, nx, ny)


def solution(mesh):
    field = P(None, "gx", "gy", "gz")
    dft = P(None, None, None, "gz", "gx", "gy")
    return jax.shard_map(
        shards,
        mesh=mesh,
        in_specs=(field, field, field, field, P("gx", "gy", "gz"), dft, dft, P(), P()),
        out_specs=(field, field, field, field, P("gz", "gx", "gy")),
        check_vma=False,
    )
```

time: 80.8 us -> 42.3 us (0.52)
  other arithmetic: 19.9 us -> 0 us
  Pallas kernels: 0 us -> 19.3 us
  local copies, waits for them, and re-layouts: 22.4 us -> 4.56 us
  between operations: 14.3 us -> 0.83 us
  starting transfers between devices: 12.8 us -> 9.13 us
  waiting for transfers between devices: 9.71 us -> 8.09 us
  matrix products: 1.27 us -> 0 us
    pallas_call x0 -> x5, Pallas kernels: none -> 19.3 us  [the longest x1 7.18 us: spectra(): pl.pallas_call(functools.partial(spectra_body, half, nz), out_shape=f32(7...]
    reduce_scatter x1 -> x0, waiting for transfers between devices: 9.36 us -> none  [shards(): lax.psum_scatter(partial_sums, 'gz', scatter_dimension=0, tiled=True)]
    ppermute x6 -> x7, waiting for transfers between devices: 0.33 us -> 8.09 us  [the longest x2 4.34 us: line(): lax.ppermute(x, axis, [(i, i + by) for i in range(peers) if 0 <= i + by <...]
    sub x3 -> x0, other arithmetic: 6.94 us -> none  [the longest x1 2.67 us: curl_forward(): above_y[..., 2, :, :, :] - field_e[..., 2, :, :, :]]
    slice x5 -> x0, local copies, waits for them, and re-layouts: 6.9 us -> none  [the longest x2 4.29 us: shards(): into_z = shifted_2(new_h[:, :, :, :, -1:], 'gz', 1)]
    another operation x7 -> x0, other arithmetic: 6.28 us -> none  [the longest x6 5.97 us: shards(): both_e = jnp.stack([e_forward, e_adjoint])]
    ppermute x2 -> x0, local copies, waits for them, and re-layouts: 5.18 us -> none  [shifted_2(): return lax.ppermute(x, axis, pairs)]
    ppermute x6 -> x7, starting transfers between devices: 12.7 us -> 9.13 us  [the longest x5 6.22 us: ring(): return lax.ppermute(x, axis, [(i, (i + by) % peers) for i in range(peers)])]
  transfers between devices with their start and end apart: 7 -> 7, of which waited for: 2 -> 2; matrix products, arithmetic and copies ran while one was open for 25% -> 0% of each run, Pallas kernels for 0% -> 17%
where the time goes in v1:
time: 42.3 us; the launch traced here: 41.9 us
  Pallas kernels  19.3 us (46%)
  starting transfers between devices  9.13 us (22%)
  waiting for transfers between devices  8.09 us (19%)
  local copies, waits for them, and re-layouts  4.56 us (11%)
  between operations  0.83 us (2%)
    pallas_call x1, Pallas kernels, spectra(): pl.pallas_call(functools.partial(spectra_body, half, nz), out_shape=f32(7...  7.18 us
    ppermute x5, starting transfers between devices, ring(): return lax.ppermute(x, axis, [(i, (i + by) % peers) for i in range(peers)])  6.22 us
    pallas_call x1, Pallas kernels, electric(): call(functools.partial(electric_body, nx, chunk, half), (field, field, f3...  5.1 us
    unnamed x20, local copies, waits for them, and re-layouts  4.56 us
    pallas_call x1, Pallas kernels, magnetic(): call(functools.partial(magnetic_body, nx, chunk), (field, field, f32(2, 2...  4.41 us
    ppermute x2, waiting for transfers between devices, line(): lax.ppermute(x, axis, [(i, i + by) for i in range(peers) if 0 <= i + by <...  4.34 us
    ppermute x5, waiting for transfers between devices, ring(): return lax.ppermute(x, axis, [(i, (i + by) % peers) for i in range(peers)])  3.75 us
    ppermute x2, starting transfers between devices, line(): lax.ppermute(x, axis, [(i, i + by) for i in range(peers) if 0 <= i + by <...  2.92 us
  transfers between devices with their start and end apart: 7, of which 2 were waited for; matrix products, arithmetic and copies ran while one was open for 0% of the time, Pallas kernels for 17%

profile of v1, /device:TPU:0, one launch (start us, length us, event | category | flops | bytes accessed | tf_op | source)
XLA Modules:
  0.0 41.9 jit_solution(16017407073451372897)
XLA Ops:
  0.6 0.0 copy-start
  0.6 1.1 %copy-done = f32[3,16,32,128]{3,2,1,0:T(8,128)S(1)} copy-done((f32[3,16,32,128]{3,2,1,0:T(8,128)S(1)}, f32[3,16,32,128]{3,2,1,0:T(8,128)}, u32[]{:S(2)}) %copy-start) | copy-done | bytes 786456
  1.8 1.1 %copy-done.2 = f32[3,16,32,128]{3,2,1,0:T(8,128)S(1)} copy-done((f32[3,16,32,128]{3,2,1,0:T(8,128)S(1)}, f32[3,16,32,128]{3,2,1,0:T(8,128)}, u32[]{:S(2)}) %copy-start.2) | copy-done | bytes 786456
  2.9 1.7 %first_faces.1 = (f32[2,2,32,128]{3,2,1,0:T(8,128)S(1)}, f32[2,2,16,128]{3,2,1,0:T(8,128)S(1)}, f32[32,128]{1,0:T(8,128)S(1)}) custom-call(f32[3,16,32,128]{3,2,1,0:T(8,128)S(1)} %copy-done, f32[3,16,32,128]{3,2,1,0:T(8,128)S(1)} %copy-done.2), custom_call_target="tpu_custom_call" | custom-call | flops 1000 | bytes 1500000 | tf_op jit(solution)/shard_map/first_faces/pallas_call | solution.py:114
  4.6 2.4 %collective-permute-start = (f32[2,2,32,128]{3,2,1,0:T(8,128)S(1)}, f32[2,2,32,128]{3,2,1,0:T(8,128)S(1)}, u32[]{:S(2)}, u32[]{:S(2)}) collective-permute-start(f32[2,2,32,128]{3,2,1,0:T(8,128)S(1)} %get-tuple-element.17), channel_id=1, source_target_pairs={{0,24},{8,0},{16,8},{24,16},{1,25},{9,1},{17,9},{25,17},{2,26},{10... | collective-permute-start | bytes 196616 | tf_op jit(solution)/shard_map/ppermute | solution.py:26
  7.0 3.6 %collective-permute-start.1 = (f32[2,2,16,128]{3,2,1,0:T(8,128)S(1)}, f32[2,2,16,128]{3,2,1,0:T(8,128)S(1)}, u32[]{:S(2)}, u32[]{:S(2)}) collective-permute-start(f32[2,2,16,128]{3,2,1,0:T(8,128)S(1)} %get-tuple-element.18), channel_id=1, source_target_pairs={{0,6},{2,0},{4,2},{6,4},{1,7},{3,1},{5,3},{7,5},{8,14},{10,8},{12,... | collective-permute-start | bytes 98312 | tf_op jit(solution)/shard_map/ppermute | solution.py:26
  10.6 1.3 %collective-permute-start.2 = (f32[32,128]{1,0:T(8,128)S(1)}, f32[32,128]{1,0:T(8,128)S(1)}, u32[]{:S(2)}, u32[]{:S(2)}) collective-permute-start(f32[32,128]{1,0:T(8,128)S(1)} %get-tuple-element.19), channel_id=1, source_target_pairs={{1,0},{3,2},{5,4},{7,6},{9,8},{11,10},{13,12},{15,14},{17,16},{19,... | collective-permute-start | bytes 49160 | tf_op jit(solution)/shard_map/ppermute | solution.py:31
  11.9 4.3 %collective-permute-done.2.zr = f32[32,128]{1,0:T(8,128)S(1)} collective-permute-done((f32[32,128]{1,0:T(8,128)S(1)}, f32[32,128]{1,0:T(8,128)S(1)}, u32[]{:S(2)}, u32[]{:S(2)}) %collective-permute-start.2) | collective-permute-done | bytes 16416 | tf_op jit(solution)/shard_map/ppermute | solution.py:31
  16.3 1.1 %copy-done.3 = f32[3,16,32,128]{3,2,1,0:T(8,128)S(1)} copy-done((f32[3,16,32,128]{3,2,1,0:T(8,128)S(1)}, f32[3,16,32,128]{3,2,1,0:T(8,128)}, u32[]{:S(2)}) %copy-start.3) | copy-done | bytes 786456
  17.4 1.1 %copy-done.4 = f32[3,16,32,128]{3,2,1,0:T(8,128)S(1)} copy-done((f32[3,16,32,128]{3,2,1,0:T(8,128)S(1)}, f32[3,16,32,128]{3,2,1,0:T(8,128)}, u32[]{:S(2)}) %copy-start.4) | copy-done | bytes 786456
  18.5 4.4 %magnetic.1 = (f32[3,16,32,128]{3,2,1,0:T(8,128)}, f32[3,16,32,128]{3,2,1,0:T(8,128)}, f32[2,2,32,128]{3,2,1,0:T(8,128)S(1)}, f32[2,2,16,128]{3,2,1,0:T(8,128)S(1)}, f32[32,128]{1,0:T(8,128)S(1)}) custom-call(f32[3,16,32,128]{3,2,1,0:T(8,128)S(1)} %copy-done, f32[3,16,32,128]{3,2,1,0:T(8,128)S(1)} %copy-done.3, f32[3,16,32,128]{3,2,1,0:T(8,128)S(1)} %copy-done.2, ...), custom_call_target="tpu_custom_call" | custom-call | flops 6000000 | bytes 4800000 | tf_op jit(solution)/shard_map/magnetic/pallas_call | solution.py:186
  22.9 0.1 collective-permute-start.3
  23.0 0.1 collective-permute-start.4
  23.1 1.6 %collective-permute-start.5 = (f32[32,128]{1,0:T(8,128)S(1)}, f32[32,128]{1,0:T(8,128)S(1)}, u32[]{:S(2)}, u32[]{:S(2)}) collective-permute-start(f32[32,128]{1,0:T(8,128)S(1)} %get-tuple-element.24), channel_id=1, source_target_pairs={{0,1},{2,3},{4,5},{6,7},{8,9},{10,11},{12,13},{14,15},{16,17},{18,... | collective-permute-start | bytes 49160 | tf_op jit(solution)/shard_map/ppermute | solution.py:31
  24.7 0.0 copy-start.1
  24.7 0.0 copy-start.5
  24.7 0.0 copy-start.6
  24.8 0.0 copy-start.7
  24.8 0.0 copy-start.9
  24.8 7.2 %spectra.1.spec = f32[7,16,32,128]{3,2,1,0:T(8,128)S(1)} custom-call(f32[3,2,3,16,32,48]{5,4,3,2,1,0:T(8,128)} %bitcast.8, f32[3,2,3,16,32,48]{5,4,3,2,1,0:T(8,128)} %bitcast.9, f32[1,3]{1,0:T(1,128)S(1)} %bitcast.4), custom_call_target="tpu_custom_call" | custom-call | flops 10000000 | bytes 11000000 | tf_op jit(solution)/shard_map/spectra/pallas_call | solution.py:238
  32.1 5.1 %electric.1 = (f32[3,16,32,128]{3,2,1,0:T(8,128)}, f32[3,16,32,128]{3,2,1,0:T(8,128)}, f32[8,512]{1,0:T(8,128)S(1)}, f32[8,512]{1,0:T(8,128)S(1)}) custom-call(f32[3,16,32,128]{3,2,1,0:T(8,128)S(1)} %copy-done.1, f32[3,16,32,128]{3,2,1,0:T(8,128)S(1)} %copy-done.2, f32[3,16,32,128]{3,2,1,0:T(8,128)S(1)} %copy-done.5, f32[3,16,32,128]{3,2,1,0:T(8,128)S(1)} %copy-done.6, ...), custom_call_target="tpu_custom_call" | custom-call | flops 9000000 | bytes 6700000 | tf_op jit(solution)/shard_map/electric/pallas_call | solution.py:338
  37.2 0.1 collective-permute-start.6
  37.2 3.7 %collective-permute-done.6.came = f32[8,512]{1,0:T(8,128)S(1)} collective-permute-done((f32[8,512]{1,0:T(8,128)S(1)}, f32[8,512]{1,0:T(8,128)S(1)}, u32[]{:S(2)}, u32[]{:S(2)}) %collective-permute-start.6) | collective-permute-done | bytes 16416 | tf_op jit(solution)/shard_map/ppermute | solution.py:26
  41.0 0.9 %gradient.1 = f32[8,16,32]{2,1,0:T(8,128)} custom-call(f32[8,512]{1,0:T(8,128)S(1)} %get-tuple-element.27.own, f32[8,512]{1,0:T(8,128)S(1)} %collective-permute-done.6.came, s32[1,96]{1,0:T(1,128)S(1)} %bitcast.7), custom_call_target="tpu_custom_call" | custom-call | flops 10000 | bytes 100000 | tf_op jit(solution)/shard_map/gradient/pallas_call | solution.py:370
  (15 shorter events, 0.0 us)
Async XLA Ops:
  0.6 1.1 %copy-start = (f32[3,16,32,128]{3,2,1,0:T(8,128)S(1)}, f32[3,16,32,128]{3,2,1,0:T(8,128)}, u32[]{:S(2)}) copy-start(f32[3,16,32,128]{3,2,1,0:T(8,128)} %ef.5) | copy-start | bytes 2359300
  1.8 1.1 %copy-start.2 = (f32[3,16,32,128]{3,2,1,0:T(8,128)S(1)}, f32[3,16,32,128]{3,2,1,0:T(8,128)}, u32[]{:S(2)}) copy-start(f32[3,16,32,128]{3,2,1,0:T(8,128)} %ea.5) | copy-start | bytes 2359300
  2.9 21.8 %copy-start.8 = (f32[3]{0:T(128)S(1)}, f32[3]{0:T(128)}, u32[]{:S(2)}) copy-start(f32[3]{0:T(128)} %param.16) | copy-start | bytes 40
  4.6 11.7 %collective-permute-start = (f32[2,2,32,128]{3,2,1,0:T(8,128)S(1)}, f32[2,2,32,128]{3,2,1,0:T(8,128)S(1)}, u32[]{:S(2)}, u32[]{:S(2)}) collective-permute-start(f32[2,2,32,128]{3,2,1,0:T(8,128)S(1)} %get-tuple-element.17), channel_id=1, source_target_pairs={{0,24},{8,0},{16,8},{24,16},{1,25},{9,1},{17,9},{25,17},{2,26},{10... | collective-permute-start | bytes 196616 | tf_op jit(solution)/shard_map/ppermute | solution.py:26
  7.0 9.2 %collective-permute-start.1 = (f32[2,2,16,128]{3,2,1,0:T(8,128)S(1)}, f32[2,2,16,128]{3,2,1,0:T(8,128)S(1)}, u32[]{:S(2)}, u32[]{:S(2)}) collective-permute-start(f32[2,2,16,128]{3,2,1,0:T(8,128)S(1)} %get-tuple-element.18), channel_id=1, source_target_pairs={{0,6},{2,0},{4,2},{6,4},{1,7},{3,1},{5,3},{7,5},{8,14},{10,8},{12,... | collective-permute-start | bytes 98312 | tf_op jit(solution)/shard_map/ppermute | solution.py:26
  10.6 5.6 %collective-permute-start.2 = (f32[32,128]{1,0:T(8,128)S(1)}, f32[32,128]{1,0:T(8,128)S(1)}, u32[]{:S(2)}, u32[]{:S(2)}) collective-permute-start(f32[32,128]{1,0:T(8,128)S(1)} %get-tuple-element.19), channel_id=1, source_target_pairs={{1,0},{3,2},{5,4},{7,6},{9,8},{11,10},{13,12},{15,14},{17,16},{19,... | collective-permute-start | bytes 49160 | tf_op jit(solution)/shard_map/ppermute | solution.py:31
  16.2 1.1 %copy-start.3 = (f32[3,16,32,128]{3,2,1,0:T(8,128)S(1)}, f32[3,16,32,128]{3,2,1,0:T(8,128)}, u32[]{:S(2)}) copy-start(f32[3,16,32,128]{3,2,1,0:T(8,128)} %hf.1) | copy-start | bytes 2359300
  17.4 1.1 %copy-start.4 = (f32[3,16,32,128]{3,2,1,0:T(8,128)S(1)}, f32[3,16,32,128]{3,2,1,0:T(8,128)}, u32[]{:S(2)}) copy-start(f32[3,16,32,128]{3,2,1,0:T(8,128)} %ha.1) | copy-start | bytes 2359300
  22.9 9.1 %collective-permute-start.3 = (f32[2,2,32,128]{3,2,1,0:T(8,128)S(1)}, f32[2,2,32,128]{3,2,1,0:T(8,128)S(1)}, u32[]{:S(2)}, u32[]{:S(2)}) collective-permute-start(f32[2,2,32,128]{3,2,1,0:T(8,128)S(1)} %get-tuple-element.22), channel_id=1, source_target_pairs={{0,8},{8,16},{16,24},{24,0},{1,9},{9,17},{17,25},{25,1},{2,10},{10... | collective-permute-start | bytes 196616 | tf_op jit(solution)/shard_map/ppermute | solution.py:26
  23.0 9.0 %collective-permute-start.4 = (f32[2,2,16,128]{3,2,1,0:T(8,128)S(1)}, f32[2,2,16,128]{3,2,1,0:T(8,128)S(1)}, u32[]{:S(2)}, u32[]{:S(2)}) collective-permute-start(f32[2,2,16,128]{3,2,1,0:T(8,128)S(1)} %get-tuple-element.23), channel_id=1, source_target_pairs={{0,2},{2,4},{4,6},{6,0},{1,3},{3,5},{5,7},{7,1},{8,10},{10,12},{12... | collective-permute-start | bytes 98312 | tf_op jit(solution)/shard_map/ppermute | solution.py:26
  23.1 8.9 %collective-permute-start.5 = (f32[32,128]{1,0:T(8,128)S(1)}, f32[32,128]{1,0:T(8,128)S(1)}, u32[]{:S(2)}, u32[]{:S(2)}) collective-permute-start(f32[32,128]{1,0:T(8,128)S(1)} %get-tuple-element.24), channel_id=1, source_target_pairs={{0,1},{2,3},{4,5},{6,7},{8,9},{10,11},{12,13},{14,15},{16,17},{18,... | collective-permute-start | bytes 49160 | tf_op jit(solution)/shard_map/ppermute | solution.py:31
  24.7 7.3 %copy-start.1 = (f32[3,16,32,128]{3,2,1,0:T(8,128)S(1)}, f32[3,16,32,128]{3,2,1,0:T(8,128)}, u32[]{:S(2)}) copy-start(f32[3,16,32,128]{3,2,1,0:T(8,128)} %ef.5) | copy-start | bytes 2359300
  24.7 7.3 %copy-start.5 = (f32[3,16,32,128]{3,2,1,0:T(8,128)S(1)}, f32[3,16,32,128]{3,2,1,0:T(8,128)}, u32[]{:S(2)}) copy-start(f32[3,16,32,128]{3,2,1,0:T(8,128)} %get-tuple-element.13.hf) | copy-start | bytes 2359300
  24.7 7.3 %copy-start.6 = (f32[3,16,32,128]{3,2,1,0:T(8,128)S(1)}, f32[3,16,32,128]{3,2,1,0:T(8,128)}, u32[]{:S(2)}) copy-start(f32[3,16,32,128]{3,2,1,0:T(8,128)} %get-tuple-element.15.ha) | copy-start | bytes 2359300
  24.8 7.3 %copy-start.7 = (s32[16,32,128]{2,1,0:T(8,128)S(1)}, s32[16,32,128]{2,1,0:T(8,128)}, u32[]{:S(2)}) copy-start(s32[16,32,128]{2,1,0:T(8,128)} %material.1) | copy-start | bytes 786436
  24.8 7.3 %copy-start.9 = (s32[96]{0:T(128)S(1)}, s32[96]{0:T(128)}, u32[]{:S(2)}) copy-start(s32[96]{0:T(128)} %param.17) | copy-start | bytes 1156
  37.2 3.8 %collective-permute-start.6 = (f32[8,512]{1,0:T(8,128)S(1)}, f32[8,512]{1,0:T(8,128)S(1)}, u32[]{:S(2)}, u32[]{:S(2)}) collective-permute-start(f32[8,512]{1,0:T(8,128)S(1)} %get-tuple-element.28), channel_id=1, source_target_pairs={{0,1},{1,0},{2,3},{3,2},{4,5},{5,4},{6,7},{7,6},{8,9},{9,8},{10,11... | collective-permute-start | bytes 49160 | tf_op jit(solution)/shard_map/ppermute | solution.py:26

commit v2 on v1

v2 whole, which is shorter than its diff:
```python
import functools

import jax
import jax.numpy as jnp
from jax import lax
from jax.experimental import pallas as pl
from jax.experimental.pallas import tpu as pltpu
from jax.sharding import PartitionSpec as P

LAYERS = 16
STEP = 40
PERMITTIVITIES = (1.0, 2.1, 4.0, 12.0)
COURANT = 0.5
LANES = 128
MIB = 1024 * 1024
ANY = pl.BlockSpec(memory_space=pl.ANY)
VMEM = pl.BlockSpec(memory_space=pltpu.VMEM)


def f32(*shape):
    return jax.ShapeDtypeStruct(shape, jnp.float32)


def vmem(*shape):
    return pltpu.VMEM(shape, jnp.float32)


def hbm(x):
    return pltpu.with_memory_space_constraint(x, pltpu.HBM)


def ring(x, axis, by):
    peers = lax.axis_size(axis)
    return lax.ppermute(x, axis, [(i, (i + by) % peers) for i in range(peers)])


def line(x, axis, by):
    peers = lax.axis_size(axis)
    return lax.ppermute(x, axis, [(i, i + by) for i in range(peers) if 0 <= i + by < peers])


def call(body, name, outs, out_specs, in_specs, scratch=(), nbytes=100000, limit=32):
    return pl.pallas_call(
        body,
        out_shape=outs,
        in_specs=in_specs,
        out_specs=out_specs,
        scratch_shapes=list(scratch),
        compiler_params=pltpu.CompilerParams(vmem_limit_bytes=limit * MIB),
        cost_estimate=pl.CostEstimate(flops=nbytes, bytes_accessed=nbytes, transcendentals=0),
        name=name,
    )


def lane_ids(rows):
    return lax.broadcasted_iota(jnp.int32, (rows, LANES), 1)


def row_ids(rows):
    return lax.broadcasted_iota(jnp.int32, (rows, LANES), 0)


def move(a, source, target):
    shift = (target - source) % LANES
    return pltpu.roll(a, shift, 1) if shift else a


def up_y(a, row):
    n = a.shape[0]
    return jnp.where(row_ids(n) == n - 1, jnp.broadcast_to(row, a.shape), pltpu.roll(a, n - 1, 0))


def down_y(a, row):
    return jnp.where(row_ids(a.shape[0]) == 0, jnp.broadcast_to(row, a.shape), pltpu.roll(a, 1, 0))


def up_z(a, packed, lane):
    n = a.shape[1]
    return jnp.where(lane_ids(a.shape[0]) == n - 1, move(packed, lane, n - 1), pltpu.roll(a, n - 1, 1))


def down_z(a, packed, lane):
    return jnp.where(lane_ids(a.shape[0]) == 0, move(packed, lane, 0), pltpu.roll(a, 1, 1))


def first_faces_body(ef, ea, xs, ys, zs, evf, eva, sems):
    fields = ((ef, evf), (ea, eva))
    _, nx, ny, _ = ef.shape
    copies = {}
    for c in range(3):
        for r, (e, v) in enumerate(fields):
            copies[c, r] = pltpu.make_async_copy(e.at[c], v.at[c], sems.at[r, c])
            copies[c, r].start()
    lane = lane_ids(ny)
    total = jnp.zeros((ny, LANES), jnp.float32)
    for c in range(3):
        for r, (_, v) in enumerate(fields):
            copies[c, r].wait()
            for x in range(nx):
                if c < 2:
                    to = (r * 2 + c) * nx + x
                    total = jnp.where(lane == to, move(v[c, x], 0, to), total)
                if c != 1:
                    ys[r, c // 2, x : x + 1, :] = v[c, x, 0:1, :]
            if c:
                xs[r, c - 1] = v[c, 0]
    zs[...] = total


def first_faces(ef, ea):
    _, nx, ny, nz = ef.shape
    field = vmem(3, nx, ny, nz)
    return call(
        first_faces_body,
        "first_faces",
        (vmem(2, 2, ny, nz), vmem(2, 2, nx, nz), vmem(ny, LANES), field, field),
        (VMEM,) * 5,
        [ANY, ANY],
        [pltpu.SemaphoreType.DMA((2, 3))],
        nbytes=1500000,
    )(hbm(ef), hbm(ea))


def transfer_body(n, *refs):
    sems = refs[-1]
    copies = []
    for k, (a, b) in enumerate(zip(refs[:n], refs[-1 - n : -1], strict=True)):
        for c in range(a.shape[0]):
            copies.append(pltpu.make_async_copy(a.at[c], b.at[c], sems.at[k, c]))
    for copy in copies:
        copy.start()
    for copy in copies:
        copy.wait()


def load(fields, after):
    n = len(fields)
    return call(
        functools.partial(transfer_body, n),
        "load",
        tuple(vmem(*f.shape) for f in fields),
        (VMEM,) * n,
        [ANY] * (n + 1),
        [pltpu.SemaphoreType.DMA((n, 3))],
        nbytes=1500000,
    )(*[hbm(f) for f in fields], after)


def store(fields, after):
    n = len(fields)
    return call(
        functools.partial(transfer_body, n),
        "store",
        tuple(f32(*f.shape) for f in fields),
        (ANY,) * n,
        [VMEM] * n + [ANY],
        [pltpu.SemaphoreType.DMA((n, 3))],
        nbytes=3000000,
    )(*fields, after)


def magnetic_body(ef, ea, hf, ha, xr, yr, zr, hfn, han, xs, ys, zs):
    runs = ((ef, hf, hfn), (ea, ha, han))
    _, nx, ny, nz = ef.shape
    packed = zr[...]
    for x in range(nx):
        for r, (e, h, hn) in enumerate(runs):
            ex, ey, ez = e[0, x], e[1, x], e[2, x]
            ey_x, ez_x = (e[1, x + 1], e[2, x + 1]) if x + 1 < nx else (xr[r, 0], xr[r, 1])
            ex_y = up_y(ex, yr[r, 0, x : x + 1, :])
            ez_y = up_y(ez, yr[r, 1, x : x + 1, :])
            ex_z = up_z(ex, packed, (r * 2 + 0) * nx + x)
            ey_z = up_z(ey, packed, (r * 2 + 1) * nx + x)
            hn[0, x] = h[0, x] - COURANT * ((ez_y - ez) - (ey_z - ey))
            hn[1, x] = h[1, x] - COURANT * ((ex_z - ex) - (ez_x - ez))
            hn[2, x] = h[2, x] - COURANT * ((ey_x - ey) - (ex_y - ex))
    lane = lane_ids(ny)
    total = jnp.zeros((ny, LANES), jnp.float32)
    for r, (_, _, hn) in enumerate(runs):
        for c in range(2):
            for x in range(nx):
                to = (r * 2 + c) * nx + x
                total = jnp.where(lane == to, move(hn[c, x], nz - 1, to), total)
                ys[r, c, x : x + 1, :] = hn[2 * c, x, ny - 1 : ny, :]
            xs[r, c] = hn[1 + c, nx - 1]
    zs[...] = total


def magnetic(ef, ea, hf, ha, xr, yr, zr):
    _, nx, ny, nz = ef.shape
    field = vmem(3, nx, ny, nz)
    return call(
        magnetic_body,
        "magnetic",
        (field, field, vmem(2, 2, ny, nz), vmem(2, 2, nx, nz), vmem(ny, LANES)),
        (VMEM,) * 5,
        [VMEM] * 7,
        nbytes=4800000,
    )(ef, ea, hf, ha, xr, yr, zr)


def slab_start(nz, half):
    return (1 - lax.axis_index("gz")) * (nz - half)


def spectra_body(half, nz, chunk, df, da, freq, after, out, dfv, dav, sems):
    freqs, nx, ny = df.shape[0], df.shape[3], df.shape[4]
    copies = {}
    for i in range(nx // chunk):
        part = pl.ds(i * chunk, chunk)
        for k, (d, v) in enumerate(((df, dfv), (da, dav))):
            copies[i, k] = pltpu.make_async_copy(d.at[:, :, :, part], v.at[:, :, :, part], sems.at[i, k])
            copies[i, k].start()
    phase = freq[...] * float(STEP)
    cos, sin = jnp.cos(phase), jnp.sin(phase)
    cs = [jnp.broadcast_to(cos[:, f : f + 1], (ny, half)) for f in range(freqs)]
    sn = [jnp.broadcast_to(sin[:, f : f + 1], (ny, half)) for f in range(freqs)]
    shift = slab_start(nz, half)
    blank = jnp.zeros((ny, LANES - half), jnp.float32)

    def place(a):
        return pltpu.roll(jnp.concatenate([a, blank], axis=1), shift, 1)

    for x in range(nx):
        if x % chunk == 0:
            copies[x // chunk, 0].wait()
            copies[x // chunk, 1].wait()
        base = jnp.zeros((ny, half), jnp.float32)
        for c in range(3):
            with_forward = jnp.zeros((ny, half), jnp.float32)
            with_adjoint = jnp.zeros((ny, half), jnp.float32)
            for f in range(freqs):
                rf, jf, ra, ja = dfv[f, 0, c, x], dfv[f, 1, c, x], dav[f, 0, c, x], dav[f, 1, c, x]
                base = base + (rf * ra - jf * ja)
                with_forward = with_forward + (cs[f] * ra + sn[f] * ja)
                with_adjoint = with_adjoint + (cs[f] * rf + sn[f] * jf)
            out[1 + c, x] = place(with_forward)
            out[4 + c, x] = place(with_adjoint)
        out[0, x] = place(base)


def spectra(df, da, freq, after, nz):
    freqs, _, _, nx, ny, half = df.shape
    chunk = 2
    held = vmem(*df.shape)
    return call(
        functools.partial(spectra_body, half, nz, chunk),
        "spectra",
        vmem(7, nx, ny, LANES),
        VMEM,
        [ANY, ANY, VMEM, ANY],
        [held, held, pltpu.SemaphoreType.DMA((nx // chunk, 2))],
        nbytes=11000000,
    )(hbm(df), hbm(da), freq, after)


def electric_body(half, owned, ef, ea, hf, ha, material, xr, yr, zr, spec, freq, layer_map, efn, ean, own, other):
    runs = ((ef, hf, efn), (ea, ha, ean))
    _, nx, ny, nz = ef.shape
    phase = freq[...] * float(STEP)
    cos, sin = jnp.cos(phase), jnp.sin(phase)
    both = jnp.sum(cos * cos - sin * sin, axis=1, keepdims=True)
    gz = lax.axis_index("gz")
    start = slab_start(nz, half)
    slab = layer_map.shape[1]
    cells = jnp.concatenate([layer_map[...], jnp.full((1, LANES - slab), -1, jnp.int32)], axis=1)
    cells = pltpu.roll(jnp.broadcast_to(cells, (8, LANES)), lax.rem(start + LANES - gz * half, LANES), 1)
    lane, layer = lane_ids(2 * owned), row_ids(2 * owned)
    inside = (lane >= start) & (lane < start + half)
    cells = jnp.broadcast_to(cells[0:1, :], (2 * owned, LANES))
    layer = lax.rem(layer + gz * owned, 2 * owned)
    hot = jnp.where(inside & (cells == layer), 1.0, 0.0).astype(jnp.bfloat16)
    packed = zr[...]
    dims = (((1,), (1,)), ((), ()))
    group = LANES // ny
    products = []
    for x in range(nx):
        m = material[x]
        coefficient = jnp.where(
            m == 0,
            COURANT / PERMITTIVITIES[0],
            jnp.where(
                m == 1,
                COURANT / PERMITTIVITIES[1],
                jnp.where(m == 2, COURANT / PERMITTIVITIES[2], COURANT / PERMITTIVITIES[3]),
            ),
        )
        news = []
        for r, (e, h, en) in enumerate(runs):
            hx, hy, hz = h[0, x], h[1, x], h[2, x]
            hy_x, hz_x = (h[1, x - 1], h[2, x - 1]) if x else (xr[r, 0], xr[r, 1])
            hx_y = down_y(hx, yr[r, 0, x : x + 1, :])
            hz_y = down_y(hz, yr[r, 1, x : x + 1, :])
            hx_z = down_z(hx, packed, (r * 2 + 0) * nx + x)
            hy_z = down_z(hy, packed, (r * 2 + 1) * nx + x)
            ex = e[0, x] + coefficient * ((hz - hz_y) - (hy - hy_z))
            ey = e[1, x] + coefficient * ((hx - hx_z) - (hz - hz_x))
            ez = e[2, x] + coefficient * ((hy - hy_x) - (hx - hx_y))
            en[0, x] = ex
            en[1, x] = ey
            en[2, x] = ez
            news.append((ex, ey, ez))
        total = spec[0, x]
        for c in range(3):
            f, a = news[0][c], news[1][c]
            total = total + (f * (spec[1 + c, x] + both * a) + a * spec[4 + c, x])
        products.append(total)
        if len(products) == group:
            block = jnp.concatenate(products, axis=0)
            products = []
            sums = jnp.zeros((2 * owned, group * ny), jnp.float32)
            for _ in range(3):
                part = block.astype(jnp.bfloat16)
                block = block - part.astype(jnp.float32)
                sums = sums + lax.dot_general(hot, part, dims, preferred_element_type=jnp.float32)
            where = pl.ds((x + 1 - group) * ny, group * ny)
            own[:, where] = sums[:owned]
            other[:, where] = sums[owned:]


def electric(ef, ea, hf, ha, material, xr, yr, zr, spec, freq, layer_map, half, owned):
    _, nx, ny, nz = ef.shape
    field = vmem(3, nx, ny, nz)
    return call(
        functools.partial(electric_body, half, owned),
        "electric",
        (field, field, vmem(owned, nx * ny), vmem(owned, nx * ny)),
        (VMEM,) * 4,
        [VMEM] * 11,
        nbytes=6700000,
    )(ef, ea, hf, ha, material, xr, yr, zr, spec, freq, layer_map)


def gradient_body(own, came, layer_map, out):
    owned, nx, ny = out.shape
    slab = layer_map.shape[1]
    layer = lax.broadcasted_iota(jnp.int32, (owned, slab), 0) + lax.axis_index("gz") * owned
    same = jnp.where(jnp.broadcast_to(layer_map[...], (owned, slab)) == layer, 1.0, 0.0)
    thickness = jnp.sum(same, axis=1, keepdims=True)
    result = (own[...] + came[...]) / (3.0 * thickness)
    for x in range(nx):
        out[:, x, :] = result[:, x * ny : (x + 1) * ny]


def gradient(own, came, layer_map, nx, ny):
    return call(gradient_body, "gradient", f32(own.shape[0], nx, ny), VMEM, [VMEM, VMEM, VMEM])(own, came, layer_map)


def shards(ef, hf, ea, ha, material, df, da, angular_freq, layer_map):
    _, nx, ny, nz = ef.shape
    half = df.shape[3]
    owned = LAYERS // lax.axis_size("gz")
    freq = angular_freq.reshape(1, -1)
    layer_map = layer_map.reshape(1, -1)
    df = jnp.transpose(df, (0, 1, 2, 4, 5, 3))
    da = jnp.transpose(da, (0, 1, 2, 4, 5, 3))
    xs, ys, zs, ef, ea = first_faces(ef, ea)
    yr = ring(ys, "gy", -1)
    xr = ring(xs, "gx", -1)
    zr = line(zs, "gz", -1)
    hf, ha = load((hf, ha), zs)
    hf, ha, xs, ys, zs = magnetic(ef, ea, hf, ha, xr, yr, zr)
    yr = ring(ys, "gy", 1)
    xr = ring(xs, "gx", 1)
    zr = line(zs, "gz", 1)
    spec = spectra(df, da, freq, zs, nz)
    ef, ea, own, other = electric(ef, ea, hf, ha, material, xr, yr, zr, spec, freq, layer_map, half, owned)
    came = ring(other, "gz", 1)
    ef, hf, ea, ha = store((ef, hf, ea, ha), own)
    return ef, hf, ea, ha, gradient(own, came, layer_map, nx, ny)


def solution(mesh):
    field = P(None, "gx", "gy", "gz")
    dft = P(None, None, None, "gz", "gx", "gy")
    return jax.shard_map(
        shards,
        mesh=mesh,
        in_specs=(field, field, field, field, P("gx", "gy", "gz"), dft, dft, P(), P()),
        out_specs=(field, field, field, field, P("gz", "gx", "gy")),
        check_vma=False,
    )
```

time: 42.3 us -> 26.8 us (0.63)
  Pallas kernels: 19.3 us -> 11.8 us
  local copies, waits for them, and re-layouts: 4.56 us -> 0.02 us
  waiting for transfers between devices: 8.09 us -> 4.93 us
    pallas_call x5 -> x7, Pallas kernels: 19.3 us -> 11.8 us  [the longest x1 4.07 us: spectra(): call(functools.partial(spectra_body, half, nz, chunk), 'spectra', vmem(7,...]
    unnamed x20 -> x6, local copies, waits for them, and re-layouts: 4.56 us -> 0.02 us
    ppermute x5, waiting for transfers between devices: 3.75 us -> 2 us  [ring(): return lax.ppermute(x, axis, [(i, (i + by) % peers) for i in range(peers)])]
    ppermute x2, waiting for transfers between devices: 4.34 us -> 2.93 us  [line(): lax.ppermute(x, axis, [(i, i + by) for i in range(peers) if 0 <= i + by <...]
  transfers between devices with their start and end apart: 7 -> 7, of which waited for: 2 -> 2; matrix products, arithmetic and copies ran while one was open for 0% -> 0% of each run, Pallas kernels for 17% -> 27%
where the time goes in v2:
time: 26.8 us; the launch traced here: 26.6 us
  Pallas kernels  11.8 us (44%)
  starting transfers between devices  9.07 us (34%)
  waiting for transfers between devices  4.93 us (18%)
  between operations  0.78 us (3%)
    ppermute x5, starting transfers between devices, ring(): return lax.ppermute(x, axis, [(i, (i + by) % peers) for i in range(peers)])  6.15 us
    pallas_call x1, Pallas kernels, spectra(): call(functools.partial(spectra_body, half, nz, chunk), 'spectra', vmem(7,...  4.07 us
    ppermute x2, waiting for transfers between devices, line(): lax.ppermute(x, axis, [(i, i + by) for i in range(peers) if 0 <= i + by <...  2.93 us
    ppermute x2, starting transfers between devices, line(): lax.ppermute(x, axis, [(i, i + by) for i in range(peers) if 0 <= i + by <...  2.92 us
    ppermute x5, waiting for transfers between devices, ring(): return lax.ppermute(x, axis, [(i, (i + by) % peers) for i in range(peers)])  2 us
    pallas_call x1, Pallas kernels, store(): call(functools.partial(transfer_body, n), 'store', tuple((f32(*f.shape) f...  1.78 us
    pallas_call x1, Pallas kernels, first_faces(): call(first_faces_body, 'first_faces', (vmem(2, 2, ny, nz), vmem(2, 2, nx,...  1.58 us
    pallas_call x1, Pallas kernels, load(): call(functools.partial(transfer_body, n), 'load', tuple((vmem(*f.shape) f...  1.4 us
  transfers between devices with their start and end apart: 7, of which 2 were waited for; matrix products, arithmetic and copies ran while one was open for 0% of the time, Pallas kernels for 27%

profile of v2, /device:TPU:0, one launch (start us, length us, event | category | flops | bytes accessed | tf_op | source)
XLA Modules:
  0.0 26.6 jit_solution(2898985234908200934)
XLA Ops:
  0.6 0.0 copy-start.1
  0.6 1.6 %first_faces.1 = (f32[2,2,32,128]{3,2,1,0:T(8,128)S(1)}, f32[2,2,16,128]{3,2,1,0:T(8,128)S(1)}, f32[32,128]{1,0:T(8,128)S(1)}, f32[3,16,32,128]{3,2,1,0:T(8,128)S(1)}, f32[3,16,32,128]{3,2,1,0:T(8,128)S(1)}) custom-call(f32[3,16,32,128]{3,2,1,0:T(8,128)} %ef.1, f32[3,16,32,128]{3,2,1,0:T(8,128)} %ea.1), custom_call_target="tpu_custom_call" | custom-call | flops 1500000 | bytes 1500000 | tf_op jit(solution)/shard_map/first_faces/pallas_call | solution.py:113
  2.2 2.4 %collective-permute-start = (f32[2,2,32,128]{3,2,1,0:T(8,128)S(1)}, f32[2,2,32,128]{3,2,1,0:T(8,128)S(1)}, u32[]{:S(2)}, u32[]{:S(2)}) collective-permute-start(f32[2,2,32,128]{3,2,1,0:T(8,128)S(1)} %get-tuple-element.30), channel_id=1, source_target_pairs={{0,24},{8,0},{16,8},{24,16},{1,25},{9,1},{17,9},{25,17},{2,26},{10... | collective-permute-start | bytes 196616 | tf_op jit(solution)/shard_map/ppermute | solution.py:34
  4.7 3.6 %collective-permute-start.1 = (f32[2,2,16,128]{3,2,1,0:T(8,128)S(1)}, f32[2,2,16,128]{3,2,1,0:T(8,128)S(1)}, u32[]{:S(2)}, u32[]{:S(2)}) collective-permute-start(f32[2,2,16,128]{3,2,1,0:T(8,128)S(1)} %get-tuple-element.31), channel_id=1, source_target_pairs={{0,6},{2,0},{4,2},{6,4},{1,7},{3,1},{5,3},{7,5},{8,14},{10,8},{12,... | collective-permute-start | bytes 98312 | tf_op jit(solution)/shard_map/ppermute | solution.py:34
  8.3 1.3 %collective-permute-start.2 = (f32[32,128]{1,0:T(8,128)S(1)}, f32[32,128]{1,0:T(8,128)S(1)}, u32[]{:S(2)}, u32[]{:S(2)}) collective-permute-start(f32[32,128]{1,0:T(8,128)S(1)} %get-tuple-element.27.refs_2_), channel_id=1, source_target_pairs={{1,0},{3,2},{5,4},{7,6},{9,8},{11,10},{13,12},{15,14},{17,16},{19,... | collective-permute-start | bytes 49160 | tf_op jit(solution)/shard_map/ppermute | solution.py:39
  9.6 1.4 %load.1 = (f32[3,16,32,128]{3,2,1,0:T(8,128)S(1)}, f32[3,16,32,128]{3,2,1,0:T(8,128)S(1)}) custom-call(f32[3,16,32,128]{3,2,1,0:T(8,128)} %refs_0_.1, f32[3,16,32,128]{3,2,1,0:T(8,128)} %refs_1_.1, f32[32,128]{1,0:T(8,128)S(1)} %get-tuple-element.27.refs_2_), custom_call_target="tpu_custom_call" | custom-call | flops 1500000 | bytes 1500000 | tf_op jit(solution)/shard_map/load/pallas_call | solution.py:138
  11.0 2.9 %collective-permute-done.2.zr = f32[32,128]{1,0:T(8,128)S(1)} collective-permute-done((f32[32,128]{1,0:T(8,128)S(1)}, f32[32,128]{1,0:T(8,128)S(1)}, u32[]{:S(2)}, u32[]{:S(2)}) %collective-permute-start.2) | collective-permute-done | bytes 16416 | tf_op jit(solution)/shard_map/ppermute | solution.py:39
  13.9 0.0 collective-permute-done.1.yr
  13.9 0.0 collective-permute-done.xr
  13.9 1.0 %magnetic.1 = (f32[3,16,32,128]{3,2,1,0:T(8,128)S(1)}, f32[3,16,32,128]{3,2,1,0:T(8,128)S(1)}, f32[2,2,32,128]{3,2,1,0:T(8,128)S(1)}, f32[2,2,16,128]{3,2,1,0:T(8,128)S(1)}, f32[32,128]{1,0:T(8,128)S(1)}) custom-call(f32[3,16,32,128]{3,2,1,0:T(8,128)S(1)} %get-tuple-element.25.ef, f32[3,16,32,128]{3,2,1,0:T(8,128)S(1)} %get-tuple-element.26.ea, ...), custom_call_target="tpu_custom_call" | custom-call | flops 4800000 | bytes 4800000 | tf_op jit(solution)/shard_map/magnetic/pallas_call | solution.py:192
  14.9 0.1 collective-permute-start.3
  15.0 0.1 collective-permute-start.4
  15.0 1.6 %collective-permute-start.5 = (f32[32,128]{1,0:T(8,128)S(1)}, f32[32,128]{1,0:T(8,128)S(1)}, u32[]{:S(2)}, u32[]{:S(2)}) collective-permute-start(f32[32,128]{1,0:T(8,128)S(1)} %get-tuple-element.36.after), channel_id=1, source_target_pairs={{0,1},{2,3},{4,5},{6,7},{8,9},{10,11},{12,13},{14,15},{16,17},{18,... | collective-permute-start | bytes 49160 | tf_op jit(solution)/shard_map/ppermute | solution.py:39
  16.7 0.0 copy-start
  16.7 0.0 copy-start.2
  16.7 4.1 %spectra.1.spec = f32[7,16,32,128]{3,2,1,0:T(8,128)S(1)} custom-call(f32[3,2,3,16,32,48]{5,4,3,2,1,0:T(8,128)} %bitcast.8, f32[3,2,3,16,32,48]{5,4,3,2,1,0:T(8,128)} %bitcast.9, f32[1,3]{1,0:T(1,128)S(1)} %bitcast.4, f32[32,128]{1,0:T(8,128)S(1)} %get-tuple-element.36.after), custom_call_target="tpu_custom_call" | custom-call | flops 11000000 | bytes 11000000 | tf_op jit(solution)/shard_map/spectra/pallas_call | solution.py:246
  20.8 0.0 collective-permute-done.5.zr
  20.8 0.0 collective-permute-done.4.yr
  20.8 0.0 collective-permute-done.3.xr
  20.8 1.1 %electric.1 = (f32[3,16,32,128]{3,2,1,0:T(8,128)S(1)}, f32[3,16,32,128]{3,2,1,0:T(8,128)S(1)}, f32[8,512]{1,0:T(8,128)S(1)}, f32[8,512]{1,0:T(8,128)S(1)}) custom-call(f32[3,16,32,128]{3,2,1,0:T(8,128)S(1)} %get-tuple-element.25.ef, f32[3,16,32,128]{3,2,1,0:T(8,128)S(1)} %get-tuple-element.26.ea, f32[3,16,32,128]{3,2,1,0:T(8,128)S(1)} %get-tuple-element.32.hf.refs_1_, ...), custom_call_target="tpu_custom_call" | custom-call | flops 6700000 | bytes 6700000 | tf_op jit(solution)/shard_map/electric/pallas_call | solution.py:324
  21.9 0.0 collective-permute-start.6
  21.9 1.8 %store.1 = (f32[3,16,32,128]{3,2,1,0:T(8,128)}, f32[3,16,32,128]{3,2,1,0:T(8,128)}, f32[3,16,32,128]{3,2,1,0:T(8,128)}, f32[3,16,32,128]{3,2,1,0:T(8,128)}) custom-call(f32[3,16,32,128]{3,2,1,0:T(8,128)S(1)} %get-tuple-element.37.refs_0_, f32[3,16,32,128]{3,2,1,0:T(8,128)S(1)} %get-tuple-element.32.hf.refs_1_, ...), custom_call_target="tpu_custom_call" | custom-call | flops 3000000 | bytes 3000000 | tf_op jit(solution)/shard_map/store/pallas_call | solution.py:151
  23.7 2.0 %collective-permute-done.6.came = f32[8,512]{1,0:T(8,128)S(1)} collective-permute-done((f32[8,512]{1,0:T(8,128)S(1)}, f32[8,512]{1,0:T(8,128)S(1)}, u32[]{:S(2)}, u32[]{:S(2)}) %collective-permute-start.6) | collective-permute-done | bytes 16416 | tf_op jit(solution)/shard_map/ppermute | solution.py:34
  25.7 0.9 %gradient.1 = f32[8,16,32]{2,1,0:T(8,128)} custom-call(f32[8,512]{1,0:T(8,128)S(1)} %get-tuple-element.39.refs_4_.own, f32[8,512]{1,0:T(8,128)S(1)} %collective-permute-done.6.came, s32[1,96]{1,0:T(1,128)S(1)} %bitcast.7), custom_call_target="tpu_custom_call" | custom-call | flops 100000 | bytes 100000 | tf_op jit(solution)/shard_map/gradient/pallas_call | solution.py:346
  (3 shorter events, 0.0 us)
Async XLA Ops:
  0.6 16.1 %copy-start.1 = (f32[3]{0:T(128)S(1)}, f32[3]{0:T(128)}, u32[]{:S(2)}) copy-start(f32[3]{0:T(128)} %param.16) | copy-start | bytes 40
  2.2 11.7 %collective-permute-start = (f32[2,2,32,128]{3,2,1,0:T(8,128)S(1)}, f32[2,2,32,128]{3,2,1,0:T(8,128)S(1)}, u32[]{:S(2)}, u32[]{:S(2)}) collective-permute-start(f32[2,2,32,128]{3,2,1,0:T(8,128)S(1)} %get-tuple-element.30), channel_id=1, source_target_pairs={{0,24},{8,0},{16,8},{24,16},{1,25},{9,1},{17,9},{25,17},{2,26},{10... | collective-permute-start | bytes 196616 | tf_op jit(solution)/shard_map/ppermute | solution.py:34
  4.7 9.2 %collective-permute-start.1 = (f32[2,2,16,128]{3,2,1,0:T(8,128)S(1)}, f32[2,2,16,128]{3,2,1,0:T(8,128)S(1)}, u32[]{:S(2)}, u32[]{:S(2)}) collective-permute-start(f32[2,2,16,128]{3,2,1,0:T(8,128)S(1)} %get-tuple-element.31), channel_id=1, source_target_pairs={{0,6},{2,0},{4,2},{6,4},{1,7},{3,1},{5,3},{7,5},{8,14},{10,8},{12,... | collective-permute-start | bytes 98312 | tf_op jit(solution)/shard_map/ppermute | solution.py:34
  8.3 5.6 %collective-permute-start.2 = (f32[32,128]{1,0:T(8,128)S(1)}, f32[32,128]{1,0:T(8,128)S(1)}, u32[]{:S(2)}, u32[]{:S(2)}) collective-permute-start(f32[32,128]{1,0:T(8,128)S(1)} %get-tuple-element.27.refs_2_), channel_id=1, source_target_pairs={{1,0},{3,2},{5,4},{7,6},{9,8},{11,10},{13,12},{15,14},{17,16},{19,... | collective-permute-start | bytes 49160 | tf_op jit(solution)/shard_map/ppermute | solution.py:39
  14.9 5.9 %collective-permute-start.3 = (f32[2,2,32,128]{3,2,1,0:T(8,128)S(1)}, f32[2,2,32,128]{3,2,1,0:T(8,128)S(1)}, u32[]{:S(2)}, u32[]{:S(2)}) collective-permute-start(f32[2,2,32,128]{3,2,1,0:T(8,128)S(1)} %get-tuple-element.34), channel_id=1, source_target_pairs={{0,8},{8,16},{16,24},{24,0},{1,9},{9,17},{17,25},{25,1},{2,10},{10... | collective-permute-start | bytes 196616 | tf_op jit(solution)/shard_map/ppermute | solution.py:34
  15.0 5.8 %collective-permute-start.4 = (f32[2,2,16,128]{3,2,1,0:T(8,128)S(1)}, f32[2,2,16,128]{3,2,1,0:T(8,128)S(1)}, u32[]{:S(2)}, u32[]{:S(2)}) collective-permute-start(f32[2,2,16,128]{3,2,1,0:T(8,128)S(1)} %get-tuple-element.35), channel_id=1, source_target_pairs={{0,2},{2,4},{4,6},{6,0},{1,3},{3,5},{5,7},{7,1},{8,10},{10,12},{12... | collective-permute-start | bytes 98312 | tf_op jit(solution)/shard_map/ppermute | solution.py:34
  15.0 5.8 %collective-permute-start.5 = (f32[32,128]{1,0:T(8,128)S(1)}, f32[32,128]{1,0:T(8,128)S(1)}, u32[]{:S(2)}, u32[]{:S(2)}) collective-permute-start(f32[32,128]{1,0:T(8,128)S(1)} %get-tuple-element.36.after), channel_id=1, source_target_pairs={{0,1},{2,3},{4,5},{6,7},{8,9},{10,11},{12,13},{14,15},{16,17},{18,... | collective-permute-start | bytes 49160 | tf_op jit(solution)/shard_map/ppermute | solution.py:39
  16.7 4.1 %copy-start = (s32[16,32,128]{2,1,0:T(8,128)S(1)}, s32[16,32,128]{2,1,0:T(8,128)}, u32[]{:S(2)}) copy-start(s32[16,32,128]{2,1,0:T(8,128)} %material.1) | copy-start | bytes 786436
  16.7 4.1 %copy-start.2 = (s32[96]{0:T(128)S(1)}, s32[96]{0:T(128)}, u32[]{:S(2)}) copy-start(s32[96]{0:T(128)} %param.17) | copy-start | bytes 1156
  21.9 3.8 %collective-permute-start.6 = (f32[8,512]{1,0:T(8,128)S(1)}, f32[8,512]{1,0:T(8,128)S(1)}, u32[]{:S(2)}, u32[]{:S(2)}) collective-permute-start(f32[8,512]{1,0:T(8,128)S(1)} %get-tuple-element.44), channel_id=1, source_target_pairs={{0,1},{1,0},{2,3},{3,2},{4,5},{5,4},{6,7},{7,6},{8,9},{9,8},{10,11... | collective-permute-start | bytes 49160 | tf_op jit(solution)/shard_map/ppermute | solution.py:34

commit v3 on v2

--- a/solution.py
+++ b/solution.py
@@ -32,11 +32,6 @@
 def ring(x, axis, by):
     peers = lax.axis_size(axis)
     return lax.ppermute(x, axis, [(i, (i + by) % peers) for i in range(peers)])
-
-
-def line(x, axis, by):
-    peers = lax.axis_size(axis)
-    return lax.ppermute(x, axis, [(i, i + by) for i in range(peers) if 0 <= i + by < peers])
 
 
 def call(body, name, outs, out_specs, in_specs, scratch=(), nbytes=100000, limit=32):
@@ -159,21 +154,55 @@
     )(*fields, after)
 
 
-def magnetic_body(ef, ea, hf, ha, xr, yr, zr, hfn, han, xs, ys, zs):
+def magnetic_update(e, h, x, rows, next_x, next_y, packed, r):
+    nx = e.shape[1]
+    ex, ey, ez = e[0, x, rows], e[1, x, rows], e[2, x, rows]
+    ey_x, ez_x = (e[1, x + 1, rows], e[2, x + 1, rows]) if x + 1 < nx else (next_x[r, 0, rows], next_x[r, 1, rows])
+    ex_y = up_y(ex, next_y[r, 0, x : x + 1, :])
+    ez_y = up_y(ez, next_y[r, 1, x : x + 1, :])
+    ex_z = up_z(ex, packed, (r * 2 + 0) * nx + x)
+    ey_z = up_z(ey, packed, (r * 2 + 1) * nx + x)
+    hx = h[0, x, rows] - COURANT * ((ez_y - ez) - (ey_z - ey))
+    hy = h[1, x, rows] - COURANT * ((ex_z - ex) - (ez_x - ez))
+    hz = h[2, x, rows] - COURANT * ((ey_x - ey) - (ex_y - ex))
+    return hx, hy, hz
+
+
+def within_upper_wall(zr):
+    return jnp.where(lax.axis_index("gz") == lax.axis_size("gz") - 1, 0.0, zr)
+
+
+def last_faces_body(ef, ea, hf, ha, xr, yr, zr, xs, ys):
+    _, nx, ny, _ = ef.shape
+    packed = within_upper_wall(zr[...])
+    last = slice(ny - 8, ny)
+    for r, (e, h) in enumerate(((ef, hf), (ea, ha))):
+        for x in range(nx):
+            hx, _, hz = magnetic_update(e, h, x, last, xr, yr, packed[last], r)
+            ys[r, 0, x : x + 1, :] = hx[7:8, :]
+            ys[r, 1, x : x + 1, :] = hz[7:8, :]
+        _, xs[r, 0], xs[r, 1] = magnetic_update(e, h, nx - 1, slice(0, ny), xr, yr, packed, r)
+
+
+def last_faces(ef, ea, hf, ha, xr, yr, zr):
+    _, nx, ny, nz = ef.shape
+    return call(
+        last_faces_body,
+        "last_faces",
+        (vmem(2, 2, ny, nz), vmem(2, 2, nx, nz)),
+        (VMEM,) * 2,
+        [VMEM] * 7,
+        nbytes=500000,
+    )(ef, ea, hf, ha, xr, yr, zr)
+
+
+def magnetic_body(ef, ea, hf, ha, xr, yr, zr, after, hfn, han, zs):
     runs = ((ef, hf, hfn), (ea, ha, han))
     _, nx, ny, nz = ef.shape
-    packed = zr[...]
+    packed = within_upper_wall(zr[...])
     for x in range(nx):
         for r, (e, h, hn) in enumerate(runs):
-            ex, ey, ez = e[0, x], e[1, x], e[2, x]
-            ey_x, ez_x = (e[1, x + 1], e[2, x + 1]) if x + 1 < nx else (xr[r, 0], xr[r, 1])
-            ex_y = up_y(ex, yr[r, 0, x : x + 1, :])
-            ez_y = up_y(ez, yr[r, 1, x : x + 1, :])
-            ex_z = up_z(ex, packed, (r * 2 + 0) * nx + x)
-            ey_z = up_z(ey, packed, (r * 2 + 1) * nx + x)
-            hn[0, x] = h[0, x] - COURANT * ((ez_y - ez) - (ey_z - ey))
-            hn[1, x] = h[1, x] - COURANT * ((ex_z - ex) - (ez_x - ez))
-            hn[2, x] = h[2, x] - COURANT * ((ey_x - ey) - (ex_y - ex))
+            hn[0, x], hn[1, x], hn[2, x] = magnetic_update(e, h, x, slice(0, ny), xr, yr, packed, r)
     lane = lane_ids(ny)
     total = jnp.zeros((ny, LANES), jnp.float32)
     for r, (_, _, hn) in enumerate(runs):
@@ -181,36 +210,33 @@
             for x in range(nx):
                 to = (r * 2 + c) * nx + x
                 total = jnp.where(lane == to, move(hn[c, x], nz - 1, to), total)
-                ys[r, c, x : x + 1, :] = hn[2 * c, x, ny - 1 : ny, :]
-            xs[r, c] = hn[1 + c, nx - 1]
     zs[...] = total
 
 
-def magnetic(ef, ea, hf, ha, xr, yr, zr):
+def magnetic(ef, ea, hf, ha, xr, yr, zr, after):
     _, nx, ny, nz = ef.shape
     field = vmem(3, nx, ny, nz)
     return call(
         magnetic_body,
         "magnetic",
-        (field, field, vmem(2, 2, ny, nz), vmem(2, 2, nx, nz), vmem(ny, LANES)),
-        (VMEM,) * 5,
-        [VMEM] * 7,
+        (field, field, vmem(ny, LANES)),
+        (VMEM,) * 3,
+        [VMEM] * 7 + [ANY],
         nbytes=4800000,
-    )(ef, ea, hf, ha, xr, yr, zr)
+    )(ef, ea, hf, ha, xr, yr, zr, after)
 
 
 def slab_start(nz, half):
     return (1 - lax.axis_index("gz")) * (nz - half)
 
 
-def spectra_body(half, nz, chunk, df, da, freq, after, out, dfv, dav, sems):
+def spectra_body(half, nz, chunk, df, dav, freq, after, out, dfv, sems):
     freqs, nx, ny = df.shape[0], df.shape[3], df.shape[4]
     copies = {}
     for i in range(nx // chunk):
         part = pl.ds(i * chunk, chunk)
-        for k, (d, v) in enumerate(((df, dfv), (da, dav))):
-            copies[i, k] = pltpu.make_async_copy(d.at[:, :, :, part], v.at[:, :, :, part], sems.at[i, k])
-            copies[i, k].start()
+        copies[i] = pltpu.make_async_copy(df.at[:, :, :, part], dfv.at[:, :, :, part], sems.at[i])
+        copies[i].start()
     phase = freq[...] * float(STEP)
     cos, sin = jnp.cos(phase), jnp.sin(phase)
     cs = [jnp.broadcast_to(cos[:, f : f + 1], (ny, half)) for f in range(freqs)]
@@ -223,8 +249,7 @@
 
     for x in range(nx):
         if x % chunk == 0:
-            copies[x // chunk, 0].wait()
-            copies[x // chunk, 1].wait()
+            copies[x // chunk].wait()
         base = jnp.zeros((ny, half), jnp.float32)
         for c in range(3):
             with_forward = jnp.zeros((ny, half), jnp.float32)
@@ -248,10 +273,10 @@
         "spectra",
         vmem(7, nx, ny, LANES),
         VMEM,
-        [ANY, ANY, VMEM, ANY],
-        [held, held, pltpu.SemaphoreType.DMA((nx // chunk, 2))],
+        [ANY, VMEM, VMEM, ANY],
+        [held, pltpu.SemaphoreType.DMA((nx // chunk,))],
         nbytes=11000000,
-    )(hbm(df), hbm(da), freq, after)
+    )(hbm(df), da, freq, after)
 
 
 def electric_body(half, owned, ef, ea, hf, ha, material, xr, yr, zr, spec, freq, layer_map, efn, ean, own, other):
@@ -270,7 +295,9 @@
     cells = jnp.broadcast_to(cells[0:1, :], (2 * owned, LANES))
     layer = lax.rem(layer + gz * owned, 2 * owned)
     hot = jnp.where(inside & (cells == layer), 1.0, 0.0).astype(jnp.bfloat16)
-    packed = zr[...]
+    owner = jnp.broadcast_to(layer_map[...], (2 * owned, slab)) == layer[:, :slab]
+    share = 1.0 / (3.0 * jnp.sum(jnp.where(owner, 1.0, 0.0), axis=1, keepdims=True))
+    packed = jnp.where(gz == 0, 0.0, zr[...])
     dims = (((1,), (1,)), ((), ()))
     group = LANES // ny
     products = []
@@ -314,6 +341,7 @@
                 block = block - part.astype(jnp.float32)
                 sums = sums + lax.dot_general(hot, part, dims, preferred_element_type=jnp.float32)
             where = pl.ds((x + 1 - group) * ny, group * ny)
+            sums = sums * share
             own[:, where] = sums[:owned]
             other[:, where] = sums[owned:]
 
@@ -331,19 +359,15 @@
     )(ef, ea, hf, ha, material, xr, yr, zr, spec, freq, layer_map)
 
 
-def gradient_body(own, came, layer_map, out):
-    owned, nx, ny = out.shape
-    slab = layer_map.shape[1]
-    layer = lax.broadcasted_iota(jnp.int32, (owned, slab), 0) + lax.axis_index("gz") * owned
-    same = jnp.where(jnp.broadcast_to(layer_map[...], (owned, slab)) == layer, 1.0, 0.0)
-    thickness = jnp.sum(same, axis=1, keepdims=True)
-    result = (own[...] + came[...]) / (3.0 * thickness)
+def gradient_body(own, came, out):
+    _, nx, ny = out.shape
+    result = own[...] + came[...]
     for x in range(nx):
         out[:, x, :] = result[:, x * ny : (x + 1) * ny]
 
 
-def gradient(own, came, layer_map, nx, ny):
-    return call(gradient_body, "gradient", f32(own.shape[0], nx, ny), VMEM, [VMEM, VMEM, VMEM])(own, came, layer_map)
+def gradient(own, came, nx, ny):
+    return call(gradient_body, "gradient", f32(own.shape[0], nx, ny), VMEM, [VMEM, VMEM])(own, came)
 
 
 def shards(ef, hf, ea, ha, material, df, da, angular_freq, layer_map):
@@ -357,17 +381,18 @@
     xs, ys, zs, ef, ea = first_faces(ef, ea)
     yr = ring(ys, "gy", -1)
     xr = ring(xs, "gx", -1)
-    zr = line(zs, "gz", -1)
+    zr = ring(zs, "gz", -1)
     hf, ha = load((hf, ha), zs)
-    hf, ha, xs, ys, zs = magnetic(ef, ea, hf, ha, xr, yr, zr)
+    xs, ys = last_faces(ef, ea, hf, ha, xr, yr, zr)
+    hf, ha, zs = magnetic(ef, ea, hf, ha, xr, yr, zr, ys)
     yr = ring(ys, "gy", 1)
     xr = ring(xs, "gx", 1)
-    zr = line(zs, "gz", 1)
+    zr = ring(zs, "gz", 1)
     spec = spectra(df, da, freq, zs, nz)
     ef, ea, own, other = electric(ef, ea, hf, ha, material, xr, yr, zr, spec, freq, layer_map, half, owned)
     came = ring(other, "gz", 1)
     ef, hf, ea, ha = store((ef, hf, ea, ha), own)
-    return ef, hf, ea, ha, gradient(own, came, layer_map, nx, ny)
+    return ef, hf, ea, ha, gradient(own, came, nx, ny)
 
 
 def solution(mesh):

time: 26.8 us -> 24 us (0.90)
  waiting for transfers between devices: 4.93 us -> 1.74 us
  starting transfers between devices: 9.07 us -> 10.8 us
  Pallas kernels: 11.8 us -> 10.6 us
    ppermute x5 -> x7, starting transfers between devices: 6.15 us -> 10.8 us  [ring(): return lax.ppermute(x, axis, [(i, (i + by) % peers) for i in range(peers)])]
    ppermute x2 -> x0, waiting for transfers between devices: 2.93 us -> none  [line(): lax.ppermute(x, axis, [(i, i + by) for i in range(peers) if 0 <= i + by <...]
    ppermute x2 -> x0, starting transfers between devices: 2.92 us -> none  [line(): lax.ppermute(x, axis, [(i, i + by) for i in range(peers) if 0 <= i + by <...]
    pallas_call x1, Pallas kernels: 4.07 us -> 2.74 us  [spectra(): call(functools.partial(spectra_body, half, nz, chunk), 'spectra', vmem(7,...]
    ppermute x5 -> x7, waiting for transfers between devices: 2 us -> 1.74 us  [ring(): return lax.ppermute(x, axis, [(i, (i + by) % peers) for i in range(peers)])]
    pallas_call x1 -> x2, Pallas kernels: 1.01 us -> 1.12 us  [the longest x1 0.94 us: magnetic(): call(magnetic_body, 'magnetic', (field, field, vmem(ny, LANES)), (VMEM,)...]
  transfers between devices with their start and end apart: 7 -> 7, of which waited for: 2 -> 3; matrix products, arithmetic and copies ran while one was open for 0% -> 0% of each run, Pallas kernels for 27% -> 29%
where the time goes in v3:
time: 24 us; the launch traced here: 23.9 us
  starting transfers between devices  10.8 us (45%)
  Pallas kernels  10.6 us (44%)
  waiting for transfers between devices  1.74 us (7%)
  between operations  0.73 us (3%)
    ppermute x7, starting transfers between devices, ring(): return lax.ppermute(x, axis, [(i, (i + by) % peers) for i in range(peers)])  10.8 us
    pallas_call x1, Pallas kernels, spectra(): call(functools.partial(spectra_body, half, nz, chunk), 'spectra', vmem(7,...  2.74 us
    pallas_call x1, Pallas kernels, store(): call(functools.partial(transfer_body, n), 'store', tuple((f32(*f.shape) f...  1.75 us
    ppermute x7, waiting for transfers between devices, ring(): return lax.ppermute(x, axis, [(i, (i + by) % peers) for i in range(peers)])  1.74 us
    pallas_call x1, Pallas kernels, first_faces(): call(first_faces_body, 'first_faces', (vmem(2, 2, ny, nz), vmem(2, 2, nx,...  1.73 us
    pallas_call x1, Pallas kernels, load(): call(functools.partial(transfer_body, n), 'load', tuple((vmem(*f.shape) f...  1.39 us
    pallas_call x1, Pallas kernels, electric(): call(functools.partial(electric_body, half, owned), 'electric', (field, f...  1.04 us
    pallas_call x1, Pallas kernels, magnetic(): call(magnetic_body, 'magnetic', (field, field, vmem(ny, LANES)), (VMEM,)...  0.94 us
  transfers between devices with their start and end apart: 7, of which 3 were waited for; matrix products, arithmetic and copies ran while one was open for 0% of the time, Pallas kernels for 29%

profile of v3, /device:TPU:0, one launch (start us, length us, event | category | flops | bytes accessed | tf_op | source)
XLA Modules:
  0.0 23.9 jit_solution(13504357154578316137)
XLA Ops:
  0.6 0.0 copy-start.2
  0.7 1.7 %first_faces.1 = (f32[2,2,32,128]{3,2,1,0:T(8,128)S(1)}, f32[2,2,16,128]{3,2,1,0:T(8,128)S(1)}, f32[32,128]{1,0:T(8,128)S(1)}, f32[3,16,32,128]{3,2,1,0:T(8,128)S(1)}, f32[3,16,32,128]{3,2,1,0:T(8,128)S(1)}) custom-call(f32[3,16,32,128]{3,2,1,0:T(8,128)} %ef.1, f32[3,16,32,128]{3,2,1,0:T(8,128)} %ea.1), custom_call_target="tpu_custom_call" | custom-call | flops 1500000 | bytes 1500000 | tf_op jit(solution)/shard_map/first_faces/pallas_call | solution.py:108
  2.4 2.4 %collective-permute-start = (f32[2,2,32,128]{3,2,1,0:T(8,128)S(1)}, f32[2,2,32,128]{3,2,1,0:T(8,128)S(1)}, u32[]{:S(2)}, u32[]{:S(2)}) collective-permute-start(f32[2,2,32,128]{3,2,1,0:T(8,128)S(1)} %get-tuple-element.30), channel_id=1, source_target_pairs={{0,24},{8,0},{16,8},{24,16},{1,25},{9,1},{17,9},{25,17},{2,26},{10... | collective-permute-start | bytes 196616 | tf_op jit(solution)/shard_map/ppermute | solution.py:34
  4.8 3.6 %collective-permute-start.1 = (f32[2,2,16,128]{3,2,1,0:T(8,128)S(1)}, f32[2,2,16,128]{3,2,1,0:T(8,128)S(1)}, u32[]{:S(2)}, u32[]{:S(2)}) collective-permute-start(f32[2,2,16,128]{3,2,1,0:T(8,128)S(1)} %get-tuple-element.31), channel_id=1, source_target_pairs={{0,6},{2,0},{4,2},{6,4},{1,7},{3,1},{5,3},{7,5},{8,14},{10,8},{12,... | collective-permute-start | bytes 98312 | tf_op jit(solution)/shard_map/ppermute | solution.py:34
  8.4 1.5 %collective-permute-start.2 = (f32[32,128]{1,0:T(8,128)S(1)}, f32[32,128]{1,0:T(8,128)S(1)}, u32[]{:S(2)}, u32[]{:S(2)}) collective-permute-start(f32[32,128]{1,0:T(8,128)S(1)} %get-tuple-element.27.refs_2_), channel_id=1, source_target_pairs={{0,1},{1,0},{2,3},{3,2},{4,5},{5,4},{6,7},{7,6},{8,9},{9,8},{10,11... | collective-permute-start | bytes 49160 | tf_op jit(solution)/shard_map/ppermute | solution.py:34
  9.9 1.4 %load.1 = (f32[3,16,32,128]{3,2,1,0:T(8,128)S(1)}, f32[3,16,32,128]{3,2,1,0:T(8,128)S(1)}) custom-call(f32[3,16,32,128]{3,2,1,0:T(8,128)} %refs_0_.1, f32[3,16,32,128]{3,2,1,0:T(8,128)} %refs_1_.1, f32[32,128]{1,0:T(8,128)S(1)} %get-tuple-element.27.refs_2_), custom_call_target="tpu_custom_call" | custom-call | flops 1500000 | bytes 1500000 | tf_op jit(solution)/shard_map/load/pallas_call | solution.py:133
  11.3 0.8 %collective-permute-done.2.zr = f32[32,128]{1,0:T(8,128)S(1)} collective-permute-done((f32[32,128]{1,0:T(8,128)S(1)}, f32[32,128]{1,0:T(8,128)S(1)}, u32[]{:S(2)}, u32[]{:S(2)}) %collective-permute-start.2) | collective-permute-done | bytes 16416 | tf_op jit(solution)/shard_map/ppermute | solution.py:34
  12.2 0.0 collective-permute-done.1.yr
  12.2 0.0 collective-permute-done.xr
  12.2 0.2 last_faces.1
  12.3 0.1 collective-permute-start.3
  12.4 0.1 collective-permute-start.4
  12.5 0.9 %magnetic.1 = (f32[3,16,32,128]{3,2,1,0:T(8,128)S(1)}, f32[3,16,32,128]{3,2,1,0:T(8,128)S(1)}, f32[32,128]{1,0:T(8,128)S(1)}) custom-call(f32[3,16,32,128]{3,2,1,0:T(8,128)S(1)} %get-tuple-element.25.ef, f32[3,16,32,128]{3,2,1,0:T(8,128)S(1)} %get-tuple-element.26.ea, f32[3,16,32,128]{3,2,1,0:T(8,128)S(1)} %get-tuple-element.28.hf, ...), custom_call_target="tpu_custom_call" | custom-call | flops 4800000 | bytes 4800000 | tf_op jit(solution)/shard_map/magnetic/pallas_call | solution.py:219
  13.4 1.6 %collective-permute-start.5 = (f32[32,128]{1,0:T(8,128)S(1)}, f32[32,128]{1,0:T(8,128)S(1)}, u32[]{:S(2)}, u32[]{:S(2)}) collective-permute-start(f32[32,128]{1,0:T(8,128)S(1)} %get-tuple-element.36.after), channel_id=1, source_target_pairs={{0,1},{1,0},{2,3},{3,2},{4,5},{5,4},{6,7},{7,6},{8,9},{9,8},{10,11... | collective-permute-start | bytes 49160 | tf_op jit(solution)/shard_map/ppermute | solution.py:34
  15.0 2.7 %spectra.1.spec = f32[7,16,32,128]{3,2,1,0:T(8,128)S(1)} custom-call(f32[3,2,3,16,32,48]{5,4,3,2,1,0:T(8,128)} %bitcast.8, f32[3,2,3,16,32,48]{5,4,3,2,1,0:T(8,128)S(1)} %bitcast.4, f32[1,3]{1,0:T(1,128)S(1)} %bitcast.5, f32[32,128]{1,0:T(8,128)S(1)} %get-tuple-element.36.after), custom_call_target="tpu_custom_call" | custom-call | flops 11000000 | bytes 11000000 | tf_op jit(solution)/shard_map/spectra/pallas_call | solution.py:271
  17.8 0.0 collective-permute-done.5.zr
  17.8 0.5 %collective-permute-done.4.yr = f32[2,2,16,128]{3,2,1,0:T(8,128)S(1)} collective-permute-done((f32[2,2,16,128]{3,2,1,0:T(8,128)S(1)}, f32[2,2,16,128]{3,2,1,0:T(8,128)S(1)}, u32[]{:S(2)}, u32[]{:S(2)}) %collective-permute-start.4) | collective-permute-done | bytes 32800 | tf_op jit(solution)/shard_map/ppermute | solution.py:34
  18.2 0.0 collective-permute-done.3.xr
  18.2 0.0 copy-done.1
  18.2 1.0 %electric.1 = (f32[3,16,32,128]{3,2,1,0:T(8,128)S(1)}, f32[3,16,32,128]{3,2,1,0:T(8,128)S(1)}, f32[8,512]{1,0:T(8,128)S(1)}, f32[8,512]{1,0:T(8,128)S(1)}) custom-call(f32[3,16,32,128]{3,2,1,0:T(8,128)S(1)} %get-tuple-element.25.ef, f32[3,16,32,128]{3,2,1,0:T(8,128)S(1)} %get-tuple-element.26.ea, f32[3,16,32,128]{3,2,1,0:T(8,128)S(1)} %get-tuple-element.33.hf.refs_1_, ...), custom_call_target="tpu_custom_call" | custom-call | flops 6700000 | bytes 6700000 | tf_op jit(solution)/shard_map/electric/pallas_call | solution.py:352
  19.3 1.6 %collective-permute-start.6 = (f32[8,512]{1,0:T(8,128)S(1)}, f32[8,512]{1,0:T(8,128)S(1)}, u32[]{:S(2)}, u32[]{:S(2)}) collective-permute-start(f32[8,512]{1,0:T(8,128)S(1)} %get-tuple-element.44), channel_id=1, source_target_pairs={{0,1},{1,0},{2,3},{3,2},{4,5},{5,4},{6,7},{7,6},{8,9},{9,8},{10,11... | collective-permute-start | bytes 49160 | tf_op jit(solution)/shard_map/ppermute | solution.py:34
  20.8 1.8 %store.1 = (f32[3,16,32,128]{3,2,1,0:T(8,128)}, f32[3,16,32,128]{3,2,1,0:T(8,128)}, f32[3,16,32,128]{3,2,1,0:T(8,128)}, f32[3,16,32,128]{3,2,1,0:T(8,128)}) custom-call(f32[3,16,32,128]{3,2,1,0:T(8,128)S(1)} %get-tuple-element.37.refs_0_, f32[3,16,32,128]{3,2,1,0:T(8,128)S(1)} %get-tuple-element.33.hf.refs_1_, ...), custom_call_target="tpu_custom_call" | custom-call | flops 3000000 | bytes 3000000 | tf_op jit(solution)/shard_map/store/pallas_call | solution.py:146
  22.6 0.5 %collective-permute-done.6.came = f32[8,512]{1,0:T(8,128)S(1)} collective-permute-done((f32[8,512]{1,0:T(8,128)S(1)}, f32[8,512]{1,0:T(8,128)S(1)}, u32[]{:S(2)}, u32[]{:S(2)}) %collective-permute-start.6) | collective-permute-done | bytes 16416 | tf_op jit(solution)/shard_map/ppermute | solution.py:34
  23.1 0.8 %gradient.1 = f32[8,16,32]{2,1,0:T(8,128)} custom-call(f32[8,512]{1,0:T(8,128)S(1)} %get-tuple-element.39.refs_4_.own, f32[8,512]{1,0:T(8,128)S(1)} %collective-permute-done.6.came), custom_call_target="tpu_custom_call" | custom-call | flops 100000 | bytes 100000 | tf_op jit(solution)/shard_map/gradient/pallas_call | solution.py:370
  (6 shorter events, 0.0 us)
Async XLA Ops:
  0.6 14.4 %copy-start.2 = (f32[3]{0:T(128)S(1)}, f32[3]{0:T(128)}, u32[]{:S(2)}) copy-start(f32[3]{0:T(128)} %param.16) | copy-start | bytes 40
  0.6 14.4 %copy-start = (f32[3,2,3,48,16,32]{3,5,4,2,1,0:T(8,128)S(1)}, f32[3,2,3,48,16,32]{3,5,4,2,1,0:T(8,128)}, u32[]{:S(2)}) copy-start(f32[3,2,3,48,16,32]{3,5,4,2,1,0:T(8,128)} %param.15) | copy-start | bytes 5308420
  2.4 9.8 %collective-permute-start = (f32[2,2,32,128]{3,2,1,0:T(8,128)S(1)}, f32[2,2,32,128]{3,2,1,0:T(8,128)S(1)}, u32[]{:S(2)}, u32[]{:S(2)}) collective-permute-start(f32[2,2,32,128]{3,2,1,0:T(8,128)S(1)} %get-tuple-element.30), channel_id=1, source_target_pairs={{0,24},{8,0},{16,8},{24,16},{1,25},{9,1},{17,9},{25,17},{2,26},{10... | collective-permute-start | bytes 196616 | tf_op jit(solution)/shard_map/ppermute | solution.py:34
  4.8 7.3 %collective-permute-start.1 = (f32[2,2,16,128]{3,2,1,0:T(8,128)S(1)}, f32[2,2,16,128]{3,2,1,0:T(8,128)S(1)}, u32[]{:S(2)}, u32[]{:S(2)}) collective-permute-start(f32[2,2,16,128]{3,2,1,0:T(8,128)S(1)} %get-tuple-element.31), channel_id=1, source_target_pairs={{0,6},{2,0},{4,2},{6,4},{1,7},{3,1},{5,3},{7,5},{8,14},{10,8},{12,... | collective-permute-start | bytes 98312 | tf_op jit(solution)/shard_map/ppermute | solution.py:34
  8.4 3.7 %collective-permute-start.2 = (f32[32,128]{1,0:T(8,128)S(1)}, f32[32,128]{1,0:T(8,128)S(1)}, u32[]{:S(2)}, u32[]{:S(2)}) collective-permute-start(f32[32,128]{1,0:T(8,128)S(1)} %get-tuple-element.27.refs_2_), channel_id=1, source_target_pairs={{0,1},{1,0},{2,3},{3,2},{4,5},{5,4},{6,7},{7,6},{8,9},{9,8},{10,11... | collective-permute-start | bytes 49160 | tf_op jit(solution)/shard_map/ppermute | solution.py:34
  12.3 5.9 %collective-permute-start.3 = (f32[2,2,32,128]{3,2,1,0:T(8,128)S(1)}, f32[2,2,32,128]{3,2,1,0:T(8,128)S(1)}, u32[]{:S(2)}, u32[]{:S(2)}) collective-permute-start(f32[2,2,32,128]{3,2,1,0:T(8,128)S(1)} %get-tuple-element.35), channel_id=1, source_target_pairs={{0,8},{8,16},{16,24},{24,0},{1,9},{9,17},{17,25},{25,1},{2,10},{10... | collective-permute-start | bytes 196616 | tf_op jit(solution)/shard_map/ppermute | solution.py:34
  12.4 5.8 %collective-permute-start.4 = (f32[2,2,16,128]{3,2,1,0:T(8,128)S(1)}, f32[2,2,16,128]{3,2,1,0:T(8,128)S(1)}, u32[]{:S(2)}, u32[]{:S(2)}) collective-permute-start(f32[2,2,16,128]{3,2,1,0:T(8,128)S(1)} %get-tuple-element.32.after), channel_id=1, source_target_pairs={{0,2},{2,4},{4,6},{6,0},{1,3},{3,5},{5,7},{7,1},{8,10},{10,12},{12... | collective-permute-start | bytes 98312 | tf_op jit(solution)/shard_map/ppermute | solution.py:34
  13.4 4.3 %collective-permute-start.5 = (f32[32,128]{1,0:T(8,128)S(1)}, f32[32,128]{1,0:T(8,128)S(1)}, u32[]{:S(2)}, u32[]{:S(2)}) collective-permute-start(f32[32,128]{1,0:T(8,128)S(1)} %get-tuple-element.36.after), channel_id=1, source_target_pairs={{0,1},{1,0},{2,3},{3,2},{4,5},{5,4},{6,7},{7,6},{8,9},{9,8},{10,11... | collective-permute-start | bytes 49160 | tf_op jit(solution)/shard_map/ppermute | solution.py:34
  15.0 3.2 %copy-start.1 = (s32[16,32,128]{2,1,0:T(8,128)S(1)}, s32[16,32,128]{2,1,0:T(8,128)}, u32[]{:S(2)}) copy-start(s32[16,32,128]{2,1,0:T(8,128)} %material.1) | copy-start | bytes 786436
  15.0 3.2 %copy-start.3 = (s32[96]{0:T(128)S(1)}, s32[96]{0:T(128)}, u32[]{:S(2)}) copy-start(s32[96]{0:T(128)} %param.17) | copy-start | bytes 1156
  19.3 3.8 %collective-permute-start.6 = (f32[8,512]{1,0:T(8,128)S(1)}, f32[8,512]{1,0:T(8,128)S(1)}, u32[]{:S(2)}, u32[]{:S(2)}) collective-permute-start(f32[8,512]{1,0:T(8,128)S(1)} %get-tuple-element.44), channel_id=1, source_target_pairs={{0,1},{1,0},{2,3},{3,2},{4,5},{5,4},{6,7},{7,6},{8,9},{9,8},{10,11... | collective-permute-start | bytes 49160 | tf_op jit(solution)/shard_map/ppermute | solution.py:34

commit v4 on v3

v4 whole, which is shorter than its diff:
```python
import functools

import jax
import jax.numpy as jnp
from jax import lax
from jax.experimental import pallas as pl
from jax.experimental.pallas import tpu as pltpu
from jax.sharding import PartitionSpec as P

LAYERS = 16
STEP = 40
PERMITTIVITIES = (1.0, 2.1, 4.0, 12.0)
COURANT = 0.5
LANES = 128
MIB = 1024 * 1024
ANY = pl.BlockSpec(memory_space=pl.ANY)
VMEM = pl.BlockSpec(memory_space=pltpu.VMEM)


def f32(*shape):
    return jax.ShapeDtypeStruct(shape, jnp.float32)


def vmem(*shape):
    return pltpu.VMEM(shape, jnp.float32)


def hbm(x):
    return pltpu.with_memory_space_constraint(x, pltpu.HBM)


def ring(x, axis, by):
    peers = lax.axis_size(axis)
    return lax.ppermute(x, axis, [(i, (i + by) % peers) for i in range(peers)])


def call(body, name, outs, out_specs, in_specs, scratch=(), nbytes=100000, limit=32):
    return pl.pallas_call(
        body,
        out_shape=outs,
        in_specs=in_specs,
        out_specs=out_specs,
        scratch_shapes=list(scratch),
        compiler_params=pltpu.CompilerParams(vmem_limit_bytes=limit * MIB),
        cost_estimate=pl.CostEstimate(flops=nbytes, bytes_accessed=nbytes, transcendentals=0),
        name=name,
    )


def lane_ids(rows):
    return lax.broadcasted_iota(jnp.int32, (rows, LANES), 1)


def row_ids(rows):
    return lax.broadcasted_iota(jnp.int32, (rows, LANES), 0)


def move(a, source, target):
    shift = (target - source) % LANES
    return pltpu.roll(a, shift, 1) if shift else a


def up_y(a, row):
    n = a.shape[0]
    return jnp.where(row_ids(n) == n - 1, jnp.broadcast_to(row, a.shape), pltpu.roll(a, n - 1, 0))


def down_y(a, row):
    return jnp.where(row_ids(a.shape[0]) == 0, jnp.broadcast_to(row, a.shape), pltpu.roll(a, 1, 0))


def up_z(a):
    n = a.shape[1]
    return jnp.where(lane_ids(a.shape[0]) == n - 1, 0.0, pltpu.roll(a, n - 1, 1))


def down_z(a, packed, lane):
    return jnp.where(lane_ids(a.shape[0]) == 0, move(packed, lane, 0), pltpu.roll(a, 1, 1))


def first_faces_body(ef, ea, xs, ys, evf, eva, sems):
    fields = ((ef, evf), (ea, eva))
    nx = ef.shape[1]
    copies = {}
    for c in range(3):
        for r, (e, v) in enumerate(fields):
            copies[c, r] = pltpu.make_async_copy(e.at[c], v.at[c], sems.at[r, c])
            copies[c, r].start()
    for c in range(3):
        for r, (_, v) in enumerate(fields):
            copies[c, r].wait()
            if c != 1:
                for x in range(nx):
                    ys[r, c // 2, x : x + 1, :] = v[c, x, 0:1, :]
            if c:
                xs[r, c - 1] = v[c, 0]


def first_faces(ef, ea):
    _, nx, ny, nz = ef.shape
    field = vmem(3, nx, ny, nz)
    return call(
        first_faces_body,
        "first_faces",
        (vmem(2, 2, ny, nz), vmem(2, 2, nx, nz), field, field),
        (VMEM,) * 4,
        [ANY, ANY],
        [pltpu.SemaphoreType.DMA((2, 3))],
        nbytes=1500000,
    )(hbm(ef), hbm(ea))


def load_body(hf, ha, ef, ea, after, hvf, hva, along_x, along_y, sems):
    _, nx, ny, _ = ef.shape
    copies = []
    for r, (h, v) in enumerate(((hf, hvf), (ha, hva))):
        for c in range(3):
            copies.append(pltpu.make_async_copy(h.at[c], v.at[c], sems.at[r, c]))
    for copy in copies:
        copy.start()
    lane, lane_8 = lane_ids(ny), lane_ids(8)
    by_x = jnp.zeros((ny, LANES), jnp.float32)
    by_y = jnp.zeros((8, LANES), jnp.float32)
    for r, e in enumerate((ef, ea)):
        by_x = jnp.where(lane == r * nx, move(e[0, nx - 1], 0, r * nx), by_x)
        for x in range(nx):
            by_y = jnp.where(lane_8 == r * nx + x, move(e[1, x, ny - 8 : ny, :], 0, r * nx + x), by_y)
    along_x[...] = by_x
    along_y[...] = jnp.where(row_ids(8) == 0, pltpu.roll(by_y, 1, 0), 0.0)
    for copy in copies:
        copy.wait()


def load(hf, ha, ef, ea, after):
    _, nx, ny, nz = ef.shape
    field = vmem(3, nx, ny, nz)
    return call(
        load_body,
        "load",
        (field, field, vmem(ny, LANES), vmem(8, LANES)),
        (VMEM,) * 4,
        [ANY, ANY, VMEM, VMEM, ANY],
        [pltpu.SemaphoreType.DMA((2, 3))],
        nbytes=1500000,
    )(hbm(hf), hbm(ha), ef, ea, after)


def magnetic_update(e, h, x, rows, next_x, next_y, r):
    nx = e.shape[1]
    ex, ey, ez = e[0, x, rows], e[1, x, rows], e[2, x, rows]
    ey_x, ez_x = (e[1, x + 1, rows], e[2, x + 1, rows]) if x + 1 < nx else (next_x[r, 0, rows], next_x[r, 1, rows])
    ex_y = up_y(ex, next_y[r, 0, x : x + 1, :])
    ez_y = up_y(ez, next_y[r, 1, x : x + 1, :])
    ex_z = up_z(ex)
    ey_z = up_z(ey)
    hx = h[0, x, rows] - COURANT * ((ez_y - ez) - (ey_z - ey))
    hy = h[1, x, rows] - COURANT * ((ex_z - ex) - (ez_x - ez))
    hz = h[2, x, rows] - COURANT * ((ey_x - ey) - (ex_y - ex))
    return hx, hy, hz


def last_faces_body(ef, ea, hf, ha, xr, yr, along_x, along_y, xs, ys):
    _, nx, ny, _ = ef.shape
    last = slice(ny - 8, ny)
    for r, (e, h) in enumerate(((ef, hf), (ea, ha))):
        for x in range(nx):
            hx, _, hz = magnetic_update(e, h, x, last, xr, yr, r)
            for c, a in enumerate((hx, hz)):
                at = packed_lane(r, c, x, nx)
                ys[at : at + 1, :] = a[7:8, :]
        _, xs[r * 2], xs[r * 2 + 1] = magnetic_update(e, h, nx - 1, slice(0, ny), xr, yr, r)
    xs[4] = along_x[...]
    ys[4 * nx : 4 * nx + 8, :] = along_y[...]


def last_faces(ef, ea, hf, ha, xr, yr, along_x, along_y):
    _, nx, ny, nz = ef.shape
    return call(
        last_faces_body,
        "last_faces",
        (vmem(5, ny, nz), vmem(4 * nx + 8, nz)),
        (VMEM,) * 2,
        [VMEM] * 8,
        nbytes=500000,
    )(ef, ea, hf, ha, xr, yr, along_x, along_y)


def magnetic_body(ef, ea, hf, ha, xr, yr, after, hfn, han, layer, zs):
    _, nx, ny, nz = ef.shape
    for x in range(nx):
        for r, (e, h, hn) in enumerate(((ef, hf, hfn), (ea, ha, han))):
            hn[0, x], hn[1, x], hn[2, x] = magnetic_update(e, h, x, slice(0, ny), xr, yr, r)
    first = pack_layer((ef, ea), nx, ny, 0)
    layer[...] = first
    zs[...] = jnp.where(lax.axis_index("gz") == 0, pack_layer((hfn, han), nx, ny, nz - 1), first)


def magnetic(ef, ea, hf, ha, xr, yr, after):
    _, nx, ny, nz = ef.shape
    field = vmem(3, nx, ny, nz)
    return call(
        magnetic_body,
        "magnetic",
        (field, field, vmem(ny, LANES), vmem(ny, LANES)),
        (VMEM,) * 4,
        [VMEM] * 6 + [ANY],
        nbytes=4800000,
    )(ef, ea, hf, ha, xr, yr, after)


def packed_lane(r, c, x, nx):
    return (r * 2 + c) * nx + x


def pack_layer(fields, nx, ny, z):
    lane = lane_ids(ny)
    total = jnp.zeros((ny, LANES), jnp.float32)
    for r, f in enumerate(fields):
        for c in range(2):
            for x in range(nx):
                to = packed_lane(r, c, x, nx)
                total = jnp.where(lane == to, move(f[c, x], z, to), total)
    return total


def from_layer_above(tile, nx):
    first = lax.rem(lane_ids(tile.shape[0]) // nx, 2) == 0
    return COURANT * jnp.where(first, pltpu.roll(tile, LANES - nx, 1), -pltpu.roll(tile, nx, 1))


def pack_open(planes, z):
    ny = planes[0].shape[0]
    lane_8 = lane_ids(8)
    first = jnp.where(lane_ids(ny) == 0, move(planes[0], z, 0), 0.0)
    top = first[0:8, :]
    for x in range(1, len(planes)):
        top = jnp.where(lane_8 == x, move(planes[x], z, x), top)
    return jnp.concatenate([top, first[8:, :]], axis=0)


def update_coefficient(m):
    return jnp.where(
        m == 0,
        COURANT / PERMITTIVITIES[0],
        jnp.where(
            m == 1,
            COURANT / PERMITTIVITIES[1],
            jnp.where(m == 2, COURANT / PERMITTIVITIES[2], COURANT / PERMITTIVITIES[3]),
        ),
    )


def slab_start(nz, half):
    return (1 - lax.axis_index("gz")) * (nz - half)


def spectra_body(half, nz, chunk, df, dav, freq, material, after, out, still, dfv, sems):
    freqs, nx, ny = df.shape[0], df.shape[3], df.shape[4]
    copies = {}
    for i in range(nx // chunk):
        part = pl.ds(i * chunk, chunk)
        copies[i] = pltpu.make_async_copy(df.at[:, :, :, part], dfv.at[:, :, :, part], sems.at[i])
        copies[i].start()
    phase = freq[...] * float(STEP)
    cos, sin = jnp.cos(phase), jnp.sin(phase)
    cs = [jnp.broadcast_to(cos[:, f : f + 1], (ny, half)) for f in range(freqs)]
    sn = [jnp.broadcast_to(sin[:, f : f + 1], (ny, half)) for f in range(freqs)]
    shift = slab_start(nz, half)
    blank = jnp.zeros((ny, LANES - half), jnp.float32)

    def place(a):
        return pltpu.roll(jnp.concatenate([a, blank], axis=1), shift, 1)

    for x in range(nx):
        if x % chunk == 0:
            copies[x // chunk].wait()
        base = jnp.zeros((ny, half), jnp.float32)
        for c in range(3):
            with_forward = jnp.zeros((ny, half), jnp.float32)
            with_adjoint = jnp.zeros((ny, half), jnp.float32)
            for f in range(freqs):
                rf, jf, ra, ja = dfv[f, 0, c, x], dfv[f, 1, c, x], dav[f, 0, c, x], dav[f, 1, c, x]
                base = base + (rf * ra - jf * ja)
                with_forward = with_forward + (cs[f] * ra + sn[f] * ja)
                with_adjoint = with_adjoint + (cs[f] * rf + sn[f] * jf)
            out[1 + c, x] = place(with_forward)
            out[4 + c, x] = place(with_adjoint)
        out[0, x] = place(base)

    def cells(planes):
        return pack_open([planes(x, slice(0, 8 if x else ny)) for x in range(nx)], nz - 1)

    still[0] = cells(lambda x, rows: out[3, x, rows])
    still[1] = cells(lambda x, rows: out[6, x, rows])
    still[2] = cells(lambda x, rows: update_coefficient(material[x, rows]))


def spectra(df, da, freq, material, after, nz):
    freqs, _, _, nx, ny, half = df.shape
    chunk = 2
    held = vmem(*df.shape)
    return call(
        functools.partial(spectra_body, half, nz, chunk),
        "spectra",
        (vmem(7, nx, ny, LANES), vmem(3, ny, LANES)),
        (VMEM,) * 2,
        [ANY, VMEM, VMEM, VMEM, ANY],
        [held, pltpu.SemaphoreType.DMA((nx // chunk,))],
        nbytes=11000000,
    )(hbm(df), da, freq, material, after)


def complete_body(hf, ha, zr, layer, hfn, han, below):
    _, nx, ny, nz = hf.shape
    lower = lax.axis_index("gz") == 0
    came = zr[...]
    above = jnp.where(lower, from_layer_above(came, nx), 0.0)
    below[...] = jnp.where(lower, 0.0, came + from_layer_above(layer[...], nx))
    top = lane_ids(ny) == nz - 1
    for r, (h, hn) in enumerate(((hf, hfn), (ha, han))):
        for c in range(2):
            for x in range(nx):
                hn[c, x] = h[c, x] + jnp.where(top, move(above, packed_lane(r, c, x, nx), nz - 1), 0.0)


def complete(hf, ha, zr, layer):
    _, nx, ny, nz = hf.shape
    part = vmem(2, nx, ny, nz)
    return call(
        complete_body,
        "complete",
        (part, part, vmem(ny, LANES)),
        (VMEM,) * 3,
        [VMEM] * 4,
        nbytes=2000000,
    )(hf, ha, zr, layer)


def electric_body(
    half, owned, ef, ea, hf, ha, hzf, hza, material, xr, yr, zr, spec, still, freq, layer_map, efn, ean, own, other, tile
):
    runs = ((ef, hf, hzf, efn), (ea, ha, hza, ean))
    _, nx, ny, nz = ef.shape
    phase = freq[...] * float(STEP)
    cos, sin = jnp.cos(phase), jnp.sin(phase)
    both = jnp.sum(cos * cos - sin * sin, axis=1, keepdims=True)
    gz = lax.axis_index("gz")
    lower = gz == 0
    start = slab_start(nz, half)
    slab = layer_map.shape[1]
    cells = jnp.concatenate([layer_map[...], jnp.full((1, LANES - slab), -1, jnp.int32)], axis=1)
    cells = pltpu.roll(jnp.broadcast_to(cells, (8, LANES)), lax.rem(start + LANES - gz * half, LANES), 1)
    lane, row = lane_ids(2 * owned), row_ids(2 * owned)
    inside = (lane >= start) & (lane < start + half)
    cells = jnp.broadcast_to(cells[0:1, :], (2 * owned, LANES))
    ids = lax.rem(row + gz * owned, 2 * owned)
    hot = jnp.where(inside & (cells == ids), 1.0, 0.0).astype(jnp.bfloat16)
    owner = jnp.broadcast_to(layer_map[...], (2 * owned, slab)) == ids[:, :slab]
    share = 1.0 / (3.0 * jnp.sum(jnp.where(owner, 1.0, 0.0), axis=1, keepdims=True))
    middle = jnp.broadcast_to(layer_map[0:1, half - 1 : half], (2 * owned, 1)) == ids[:, 0:1]
    middle_share = jnp.sum(jnp.where(middle, share, 0.0), axis=0, keepdims=True)
    below = zr[...]
    dims = (((1,), (1,)), ((), ()))
    group = LANES // ny
    products = []
    for x in range(nx):
        coefficient = update_coefficient(material[x])
        news = []
        for r, (e, h, hz, en) in enumerate(runs):
            at_x, at_y = packed_lane(r, 0, x, nx), packed_lane(r, 1, x, nx)
            hx, hy, hz_here = h[0, x], h[1, x], hz[2, x]
            hy_x, hz_x = (h[1, x - 1], hz[2, x - 1]) if x else (xr[2 * r], xr[2 * r + 1])
            hx_y = down_y(hx, yr[at_x : at_x + 1, :])
            hz_y = down_y(hz_here, yr[at_y : at_y + 1, :])
            hx_z = down_z(hx, below, at_x)
            hy_z = down_z(hy, below, at_y)
            ex = e[0, x] + coefficient * ((hz_here - hz_y) - (hy - hy_z))
            ey = e[1, x] + coefficient * ((hx - hx_z) - (hz_here - hz_x))
            ez = e[2, x] + coefficient * ((hy - hy_x) - (hx - hx_y))
            en[0, x] = ex
            en[1, x] = ey
            en[2, x] = ez
            news.append((ex, ey, ez))
        total = spec[0, x]
        for c in range(3):
            f, a = news[0][c], news[1][c]
            total = total + (f * (spec[1 + c, x] + both * a) + a * spec[4 + c, x])
        products.append(total)
        if len(products) == group:
            block = jnp.concatenate(products, axis=0)
            products = []
            sums = jnp.zeros((2 * owned, group * ny), jnp.float32)
            for _ in range(3):
                part = block.astype(jnp.bfloat16)
                block = block - part.astype(jnp.float32)
                sums = sums + lax.dot_general(hot, part, dims, preferred_element_type=jnp.float32)
            sums = sums * share
            where = pl.ds(x // group * owned, owned)
            own[where, :] = sums[:owned]
            other[where, :] = sums[owned:]
    f, a = (pack_open([e[2, x, 0 : 8 if x else ny, :] for x in range(nx)], nz - 1) for e in (efn, ean))
    ratio = COURANT * still[2]
    scaled = ratio * middle_share
    rest = scaled * (still[0] + both * a)
    rest = rest + pltpu.roll(scaled * (still[1] + both * f), nx, 1)
    rest = rest + pltpu.roll(scaled * ratio * both, 2 * nx, 1)
    rest = rest + pltpu.roll(ratio, 3 * nx, 1)
    along = xr[4]
    along = along + jnp.concatenate([yr[4 * nx : 4 * nx + 8, :], jnp.zeros((ny - 8, LANES), jnp.float32)], axis=0)
    rest = jnp.where(lower, rest, along)
    tile[...] = rest
    other[nx // group * owned :, :] = rest


def electric(ef, ea, hf, ha, hzf, hza, material, xr, yr, zr, spec, still, freq, layer_map, half, owned):
    _, nx, ny, nz = ef.shape
    field = vmem(3, nx, ny, nz)
    rows = nx * ny // LANES * owned
    return call(
        functools.partial(electric_body, half, owned),
        "electric",
        (field, field, vmem(rows, LANES), vmem(rows + ny, LANES), vmem(ny, LANES)),
        (VMEM,) * 5,
        [VMEM] * 14,
        nbytes=6700000,
    )(ef, ea, hf, ha, hzf, hza, material, xr, yr, zr, spec, still, freq, layer_map)


def store_body(ef, ea, hf, ha, hzf, hza, after, efn, ean, hfn, han, sems):
    copies = []
    for r, (e, h, hz, en, hn) in enumerate(((ef, hf, hzf, efn, hfn), (ea, ha, hza, ean, han))):
        for c in range(3):
            copies.append(pltpu.make_async_copy(e.at[c], en.at[c], sems.at[r, c]))
            copies.append(pltpu.make_async_copy((h if c < 2 else hz).at[c], hn.at[c], sems.at[r, 3 + c]))
    for copy in copies:
        copy.start()
    for copy in copies:
        copy.wait()


def store(ef, ea, hf, ha, hzf, hza, after):
    field = f32(*ef.shape)
    return call(
        store_body,
        "store",
        (field,) * 4,
        (ANY,) * 4,
        [VMEM] * 6 + [ANY],
        [pltpu.SemaphoreType.DMA((2, 6))],
        nbytes=3000000,
    )(ef, ea, hf, ha, hzf, hza, after)


def gradient_body(ef, ea, own, tile, came, layer_map, _f, _a, out, efn, ean, plane, rows, result, sems):
    owned, nx, ny = out.shape
    nz = ef.shape[3]
    half = layer_map.shape[1] // 2
    gz = lax.axis_index("gz")
    lower = gz == 0
    sums = own.shape[0]
    mine, theirs = tile[...], came[sums:, :]
    change, cells = jnp.where(lower, mine, theirs), jnp.where(lower, theirs, mine)
    cell = [cells, pltpu.roll(cells, LANES - nx, 1)]
    ratio = jnp.where(lower, pltpu.roll(change, LANES - 3 * nx, 1), 0.0)
    copies = []
    for r, (e, en) in enumerate(((ef, efn), (ea, ean))):
        add = ratio * cell[r]
        plane[r] = e[2, 0] + jnp.where(lane_ids(ny) == nz - 1, move(add, 0, nz - 1), 0.0)
        corner = (lane_ids(8) == nz - 1) & (row_ids(8) == 0)
        for x in range(1, nx):
            rows[r, x - 1] = e[2, x, 0:8, :] + jnp.where(corner, move(add[0:8, :], x, nz - 1), 0.0)
        copies.append(pltpu.make_async_copy(plane.at[r], en.at[2, 0], sems.at[r, 0]))
        copies.append(pltpu.make_async_copy(rows.at[r], en.at[2, 1:nx, 0:8], sems.at[r, 1]))
    for copy in copies:
        copy.start()
    by_a, by_both = pltpu.roll(change, LANES - nx, 1), pltpu.roll(change, LANES - 2 * nx, 1)
    missing = change * cell[0] + by_a * cell[1] + by_both * (cell[0] * cell[1])
    missing = jnp.transpose(missing)[0:nx, 0:ny]
    share = own[...] + came[0:sums, :]
    group = nx * owned // sums
    for x in range(nx):
        block = share[x // group * owned : (x // group + 1) * owned]
        at = x % group * ny
        result[:, x, :] = block[:, at : at + ny]
    middle = layer_map[0:1, half - 1 : half]
    for k in range(owned):
        mine = jnp.broadcast_to(middle == gz * owned + k, (nx, ny))
        result[k] = result[k] + jnp.where(mine, missing, 0.0)
    last = pltpu.make_async_copy(result, out, sems.at[0, 2])
    last.start()
    for copy in copies:
        copy.wait()
    last.wait()


def gradient(ef, ea, own, tile, came, layer_map, efn, ean, owned):
    _, nx, ny, nz = ef.shape
    return pl.pallas_call(
        gradient_body,
        out_shape=(f32(owned, nx, ny), f32(*efn.shape), f32(*ean.shape)),
        in_specs=[VMEM] * 6 + [ANY] * 2,
        out_specs=(ANY,) * 3,
        scratch_shapes=[
            pltpu.VMEM((2, ny, nz), jnp.float32),
            pltpu.VMEM((2, nx - 1, 8, nz), jnp.float32),
            pltpu.VMEM((owned, nx, ny), jnp.float32),
            pltpu.SemaphoreType.DMA((2, 3)),
        ],
        input_output_aliases={6: 1, 7: 2},
        compiler_params=pltpu.CompilerParams(vmem_limit_bytes=32 * MIB),
        cost_estimate=pl.CostEstimate(flops=100000, bytes_accessed=400000, transcendentals=0),
        name="gradient",
    )(ef, ea, own, tile, came, layer_map, efn, ean)


def shards(ef, hf, ea, ha, material, df, da, angular_freq, layer_map):
    _, nx, ny, nz = ef.shape
    half = df.shape[3]
    owned = LAYERS // lax.axis_size("gz")
    freq = angular_freq.reshape(1, -1)
    layer_map = layer_map.reshape(1, -1)
    df = jnp.transpose(df, (0, 1, 2, 4, 5, 3))
    da = jnp.transpose(da, (0, 1, 2, 4, 5, 3))
    xs, ys, ef, ea = first_faces(ef, ea)
    yr = ring(ys, "gy", -1)
    xr = ring(xs, "gx", -1)
    hf, ha, along_x, along_y = load(hf, ha, ef, ea, ys)
    xs, ys = last_faces(ef, ea, hf, ha, xr, yr, along_x, along_y)
    hf, ha, layer, zs = magnetic(ef, ea, hf, ha, xr, yr, ys)
    yr = ring(ys, "gy", 1)
    xr = ring(xs, "gx", 1)
    zr = ring(zs, "gz", 1)
    spec, still = spectra(df, da, freq, material, zs, nz)
    hxyf, hxya, below = complete(hf, ha, zr, layer)
    ef, ea, own, other, tile = electric(
        ef, ea, hxyf, hxya, hf, ha, material, xr, yr, below, spec, still, freq, layer_map, half, owned
    )
    came = ring(other, "gz", 1)
    efn, ean, hfn, han = store(ef, ea, hxyf, hxya, hf, ha, own)
    out, efn, ean = gradient(ef, ea, own, tile, came, layer_map, efn, ean, owned)
    return efn, hfn, ean, han, out


def solution(mesh):
    field = P(None, "gx", "gy", "gz")
    dft = P(None, None, None, "gz", "gx", "gy")
    return jax.shard_map(
        shards,
        mesh=mesh,
        in_specs=(field, field, field, field, P("gx", "gy", "gz"), dft, dft, P(), P()),
        out_specs=(field, field, field, field, P("gz", "gx", "gy")),
        check_vma=False,
    )
```

time: 24 us -> 22.6 us (0.942)
  starting transfers between devices: 10.8 us -> 9.55 us
  waiting for transfers between devices: 1.74 us -> 0.98 us
  Pallas kernels: 10.6 us -> 11.1 us
    ppermute x7 -> x6, starting transfers between devices: 10.8 us -> 9.55 us  [ring(): return lax.ppermute(x, axis, [(i, (i + by) % peers) for i in range(peers)])]
    pallas_call x6 -> x7, Pallas kernels: 7.81 us -> 8.65 us  [the longest x1 2.78 us: spectra(): call(functools.partial(spectra_body, half, nz, chunk), 'spectra', (vmem(7...]
    ppermute x7 -> x6, waiting for transfers between devices: 1.74 us -> 0.98 us  [ring(): return lax.ppermute(x, axis, [(i, (i + by) % peers) for i in range(peers)])]
    pallas_call x1, Pallas kernels: 1.73 us -> 1.41 us  [first_faces(): call(first_faces_body, 'first_faces', (vmem(2, 2, ny, nz), vmem(2, 2, nx,...]
  transfers between devices with their start and end apart: 7 -> 6, of which waited for: 3 -> 2; matrix products, arithmetic and copies ran while one was open for 0% -> 0% of each run, Pallas kernels for 29% -> 33%
where the time goes in v4:
time: 22.6 us; the launch traced here: 22.4 us
  Pallas kernels  11.1 us (49%)
  starting transfers between devices  9.55 us (42%)
  waiting for transfers between devices  0.98 us (4%)
  between operations  0.71 us (3%)
    ppermute x6, starting transfers between devices, ring(): return lax.ppermute(x, axis, [(i, (i + by) % peers) for i in range(peers)])  9.55 us
    pallas_call x1, Pallas kernels, spectra(): call(functools.partial(spectra_body, half, nz, chunk), 'spectra', (vmem(7...  2.78 us
    pallas_call x1, Pallas kernels, store(): call(store_body, 'store', (field,) * 4, (ANY,) * 4, [VMEM] * 6 + [ANY], [...  1.75 us
    pallas_call x1, Pallas kernels, load(): call(load_body, 'load', (field, field, vmem(ny, LANES), vmem(8, LANES)),...  1.56 us
    pallas_call x1, Pallas kernels, first_faces(): call(first_faces_body, 'first_faces', (vmem(2, 2, ny, nz), vmem(2, 2, nx,...  1.41 us
    pallas_call x1, Pallas kernels, electric(): call(functools.partial(electric_body, half, owned), 'electric', (field, f...  1.09 us
    pallas_call x1, Pallas kernels, gradient(): pl.pallas_call(gradient_body, out_shape=(f32(owned, nx, ny), f32(*efn.sha...  1.01 us
    pallas_call x1, Pallas kernels, magnetic(): call(magnetic_body, 'magnetic', (field, field, vmem(ny, LANES), vmem(ny,...  1 us
  transfers between devices with their start and end apart: 6, of which 2 were waited for; matrix products, arithmetic and copies ran while one was open for 0% of the time, Pallas kernels for 33%

profile of v4, /device:TPU:0, one launch (start us, length us, event | category | flops | bytes accessed | tf_op | source)
XLA Modules:
  0.0 22.4 jit_solution(16493867546646562254)
XLA Ops:
  0.6 1.4 %first_faces.1 = (f32[2,2,32,128]{3,2,1,0:T(8,128)S(1)}, f32[2,2,16,128]{3,2,1,0:T(8,128)S(1)}, f32[3,16,32,128]{3,2,1,0:T(8,128)S(1)}, f32[3,16,32,128]{3,2,1,0:T(8,128)S(1)}) custom-call(f32[3,16,32,128]{3,2,1,0:T(8,128)} %ef.1, f32[3,16,32,128]{3,2,1,0:T(8,128)} %ea.1), custom_call_target="tpu_custom_call" | custom-call | flops 1500000 | bytes 1500000 | tf_op jit(solution)/shard_map/first_faces/pallas_call | solution.py:102
  2.0 2.4 %collective-permute-start = (f32[2,2,32,128]{3,2,1,0:T(8,128)S(1)}, f32[2,2,32,128]{3,2,1,0:T(8,128)S(1)}, u32[]{:S(2)}, u32[]{:S(2)}) collective-permute-start(f32[2,2,32,128]{3,2,1,0:T(8,128)S(1)} %get-tuple-element.41), channel_id=1, source_target_pairs={{0,24},{8,0},{16,8},{24,16},{1,25},{9,1},{17,9},{25,17},{2,26},{10... | collective-permute-start | bytes 196616 | tf_op jit(solution)/shard_map/ppermute | solution.py:34
  4.5 3.6 %collective-permute-start.1 = (f32[2,2,16,128]{3,2,1,0:T(8,128)S(1)}, f32[2,2,16,128]{3,2,1,0:T(8,128)S(1)}, u32[]{:S(2)}, u32[]{:S(2)}) collective-permute-start(f32[2,2,16,128]{3,2,1,0:T(8,128)S(1)} %get-tuple-element.38.after), channel_id=1, source_target_pairs={{0,6},{2,0},{4,2},{6,4},{1,7},{3,1},{5,3},{7,5},{8,14},{10,8},{12,... | collective-permute-start | bytes 98312 | tf_op jit(solution)/shard_map/ppermute | solution.py:34
  8.1 1.6 %load.1 = (f32[3,16,32,128]{3,2,1,0:T(8,128)S(1)}, f32[3,16,32,128]{3,2,1,0:T(8,128)S(1)}, f32[32,128]{1,0:T(8,128)S(1)}, f32[8,128]{1,0:T(8,128)S(1)}) custom-call(f32[3,16,32,128]{3,2,1,0:T(8,128)} %hf.1, f32[3,16,32,128]{3,2,1,0:T(8,128)} %ha.1, f32[3,16,32,128]{3,2,1,0:T(8,128)S(1)} %get-tuple-element.36.ef, ...), custom_call_target="tpu_custom_call" | custom-call | flops 1500000 | bytes 1500000 | tf_op jit(solution)/shard_map/load/pallas_call | solution.py:137
  9.6 0.0 collective-permute-done.1.yr
  9.7 0.0 collective-permute-done.xr
  9.7 0.1 last_faces.1
  9.8 0.1 collective-permute-start.3
  9.9 0.3 %collective-permute-start.4 = (f32[72,128]{1,0:T(8,128)S(1)}, f32[72,128]{1,0:T(8,128)S(1)}, u32[]{:S(2)}, u32[]{:S(2)}) collective-permute-start(f32[72,128]{1,0:T(8,128)S(1)} %get-tuple-element.44.after), channel_id=1, source_target_pairs={{0,2},{2,4},{4,6},{6,0},{1,3},{3,5},{5,7},{7,1},{8,10},{10,12},{12... | collective-permute-start | bytes 110600 | tf_op jit(solution)/shard_map/ppermute | solution.py:34
  10.2 1.0 %magnetic.1 = (f32[3,16,32,128]{3,2,1,0:T(8,128)S(1)}, f32[3,16,32,128]{3,2,1,0:T(8,128)S(1)}, f32[32,128]{1,0:T(8,128)S(1)}, f32[32,128]{1,0:T(8,128)S(1)}) custom-call(f32[3,16,32,128]{3,2,1,0:T(8,128)S(1)} %get-tuple-element.36.ef, f32[3,16,32,128]{3,2,1,0:T(8,128)S(1)} %get-tuple-element.37.ea, f32[3,16,32,128]{3,2,1,0:T(8,128)S(1)} %get-tuple-element.39.hf, ...), custom_call_target="tpu_custom_call" | custom-call | flops 4800000 | bytes 4800000 | tf_op jit(solution)/shard_map/magnetic/pallas_call | solution.py:201
  11.2 1.6 %collective-permute-start.2 = (f32[32,128]{1,0:T(8,128)S(1)}, f32[32,128]{1,0:T(8,128)S(1)}, u32[]{:S(2)}, u32[]{:S(2)}) collective-permute-start(f32[32,128]{1,0:T(8,128)S(1)} %get-tuple-element.47.after), channel_id=1, source_target_pairs={{0,1},{1,0},{2,3},{3,2},{4,5},{5,4},{6,7},{7,6},{8,9},{9,8},{10,11... | collective-permute-start | bytes 49160 | tf_op jit(solution)/shard_map/ppermute | solution.py:34
  12.8 0.0 copy-done
  12.8 0.0 copy-done.1
  12.8 0.0 copy-done.2
  12.8 2.8 %spectra.1 = (f32[7,16,32,128]{3,2,1,0:T(8,128)S(1)}, f32[3,32,128]{2,1,0:T(8,128)S(1)}) custom-call(f32[3,2,3,16,32,48]{5,4,3,2,1,0:T(8,128)} %bitcast.9, f32[3,2,3,16,32,48]{5,4,3,2,1,0:T(8,128)S(1)} %bitcast.4, f32[1,3]{1,0:T(1,128)S(1)} %bitcast.5, s32[16,32,128]{2,1,0:T(8,128)S(1)} %copy-done.1, f32[32,128]{1,0:T(8,128)S(1)} %get-tuple-element.47.after), custom_call_target="tpu_custom_call" | custom-call | flops 11000000 | bytes 11000000 | tf_op jit(solution)/shard_map/spectra/pallas_call | solution.py:302
  15.6 0.0 collective-permute-done.2.zr
  15.6 0.4 %complete.1 = (f32[2,16,32,128]{3,2,1,0:T(8,128)S(1)}, f32[2,16,32,128]{3,2,1,0:T(8,128)S(1)}, f32[32,128]{1,0:T(8,128)S(1)}) custom-call(f32[3,16,32,128]{3,2,1,0:T(8,128)S(1)} %get-tuple-element.45.hf.hzf, f32[3,16,32,128]{3,2,1,0:T(8,128)S(1)} %get-tuple-element.46.ha.hza, f32[32,128]{1,0:T(8,128)S(1)} %collective-permute-done.2.zr, ...), custom_call_target="tpu_custom_call" | custom-call | flops 2000000 | bytes 2000000 | tf_op jit(solution)/shard_map/complete/pallas_call | solution.py:329
  16.1 0.3 %collective-permute-done.4.yr = f32[72,128]{1,0:T(8,128)S(1)} collective-permute-done((f32[72,128]{1,0:T(8,128)S(1)}, f32[72,128]{1,0:T(8,128)S(1)}, u32[]{:S(2)}, u32[]{:S(2)}) %collective-permute-start.4) | collective-permute-done | bytes 36896 | tf_op jit(solution)/shard_map/ppermute | solution.py:34
  16.4 0.0 collective-permute-done.3.xr
  16.4 1.1 %electric.1 = (f32[3,16,32,128]{3,2,1,0:T(8,128)S(1)}, f32[3,16,32,128]{3,2,1,0:T(8,128)S(1)}, f32[32,128]{1,0:T(8,128)S(1)}, f32[64,128]{1,0:T(8,128)S(1)}, f32[32,128]{1,0:T(8,128)S(1)}) custom-call(f32[3,16,32,128]{3,2,1,0:T(8,128)S(1)} %get-tuple-element.36.ef, f32[3,16,32,128]{3,2,1,0:T(8,128)S(1)} %get-tuple-element.37.ea, ...), custom_call_target="tpu_custom_call" | custom-call | flops 6700000 | bytes 6700000 | tf_op jit(solution)/shard_map/electric/pallas_call | solution.py:419
  17.5 1.5 %collective-permute-start.5 = (f32[64,128]{1,0:T(8,128)S(1)}, f32[64,128]{1,0:T(8,128)S(1)}, u32[]{:S(2)}, u32[]{:S(2)}) collective-permute-start(f32[64,128]{1,0:T(8,128)S(1)} %get-tuple-element.59), channel_id=1, source_target_pairs={{0,1},{1,0},{2,3},{3,2},{4,5},{5,4},{6,7},{7,6},{8,9},{9,8},{10,11... | collective-permute-start | bytes 98312 | tf_op jit(solution)/shard_map/ppermute | solution.py:34
  19.0 1.8 %store.1 = (f32[3,16,32,128]{3,2,1,0:T(8,128)}, f32[3,16,32,128]{3,2,1,0:T(8,128)}, f32[3,16,32,128]{3,2,1,0:T(8,128)}, f32[3,16,32,128]{3,2,1,0:T(8,128)}) custom-call(f32[3,16,32,128]{3,2,1,0:T(8,128)S(1)} %get-tuple-element.55.ef, f32[3,16,32,128]{3,2,1,0:T(8,128)S(1)} %get-tuple-element.56.ea, f32[2,16,32,128]{3,2,1,0:T(8,128)S(1)} %get-tuple-element.49.hf, ...), custom_call_target="tpu_custom_call" | custom-call | flops 3000000 | bytes 3000000 | tf_op jit(solution)/shard_map/store/pallas_call | solution.py:443
  20.8 0.6 %collective-permute-done.5.came = f32[64,128]{1,0:T(8,128)S(1)} collective-permute-done((f32[64,128]{1,0:T(8,128)S(1)}, f32[64,128]{1,0:T(8,128)S(1)}, u32[]{:S(2)}, u32[]{:S(2)}) %collective-permute-start.5) | collective-permute-done | bytes 32800 | tf_op jit(solution)/shard_map/ppermute | solution.py:34
  21.4 1.0 %gradient.1 = (f32[8,16,32]{2,1,0:T(8,128)}, f32[3,16,32,128]{3,2,1,0:T(8,128)}, f32[3,16,32,128]{3,2,1,0:T(8,128)}) custom-call(f32[3,16,32,128]{3,2,1,0:T(8,128)S(1)} %get-tuple-element.55.ef, f32[3,16,32,128]{3,2,1,0:T(8,128)S(1)} %get-tuple-element.56.ea, ...), custom_call_target="tpu_custom_call", output_to_operand_aliasing={{1}: (6, {}), {2}: (7, {})} | custom-call | flops 100000 | bytes 400000 | tf_op jit(solution)/shard_map/gradient/pallas_call | solution.py:498
  (5 shorter events, 0.0 us)
Async XLA Ops:
  2.0 7.6 %collective-permute-start = (f32[2,2,32,128]{3,2,1,0:T(8,128)S(1)}, f32[2,2,32,128]{3,2,1,0:T(8,128)S(1)}, u32[]{:S(2)}, u32[]{:S(2)}) collective-permute-start(f32[2,2,32,128]{3,2,1,0:T(8,128)S(1)} %get-tuple-element.41), channel_id=1, source_target_pairs={{0,24},{8,0},{16,8},{24,16},{1,25},{9,1},{17,9},{25,17},{2,26},{10... | collective-permute-start | bytes 196616 | tf_op jit(solution)/shard_map/ppermute | solution.py:34
  4.5 5.2 %collective-permute-start.1 = (f32[2,2,16,128]{3,2,1,0:T(8,128)S(1)}, f32[2,2,16,128]{3,2,1,0:T(8,128)S(1)}, u32[]{:S(2)}, u32[]{:S(2)}) collective-permute-start(f32[2,2,16,128]{3,2,1,0:T(8,128)S(1)} %get-tuple-element.38.after), channel_id=1, source_target_pairs={{0,6},{2,0},{4,2},{6,4},{1,7},{3,1},{5,3},{7,5},{8,14},{10,8},{12,... | collective-permute-start | bytes 98312 | tf_op jit(solution)/shard_map/ppermute | solution.py:34
  8.1 4.7 %copy-start = (f32[3,2,3,48,16,32]{3,5,4,2,1,0:T(8,128)S(1)}, f32[3,2,3,48,16,32]{3,5,4,2,1,0:T(8,128)}, u32[]{:S(2)}) copy-start(f32[3,2,3,48,16,32]{3,5,4,2,1,0:T(8,128)} %param.15) | copy-start | bytes 5308420
  8.1 4.7 %copy-start.1 = (s32[16,32,128]{2,1,0:T(8,128)S(1)}, s32[16,32,128]{2,1,0:T(8,128)}, u32[]{:S(2)}) copy-start(s32[16,32,128]{2,1,0:T(8,128)} %material.3) | copy-start | bytes 786436
  8.1 4.7 %copy-start.2 = (f32[3]{0:T(128)S(1)}, f32[3]{0:T(128)}, u32[]{:S(2)}) copy-start(f32[3]{0:T(128)} %param.16) | copy-start | bytes 40
  9.8 6.6 %collective-permute-start.3 = (f32[5,32,128]{2,1,0:T(8,128)S(1)}, f32[5,32,128]{2,1,0:T(8,128)S(1)}, u32[]{:S(2)}, u32[]{:S(2)}) collective-permute-start(f32[5,32,128]{2,1,0:T(8,128)S(1)} %get-tuple-element.51), channel_id=1, source_target_pairs={{0,8},{8,16},{16,24},{24,0},{1,9},{9,17},{17,25},{25,1},{2,10},{10... | collective-permute-start | bytes 245768 | tf_op jit(solution)/shard_map/ppermute | solution.py:34
  9.9 6.5 %collective-permute-start.4 = (f32[72,128]{1,0:T(8,128)S(1)}, f32[72,128]{1,0:T(8,128)S(1)}, u32[]{:S(2)}, u32[]{:S(2)}) collective-permute-start(f32[72,128]{1,0:T(8,128)S(1)} %get-tuple-element.44.after), channel_id=1, source_target_pairs={{0,2},{2,4},{4,6},{6,0},{1,3},{3,5},{5,7},{7,1},{8,10},{10,12},{12... | collective-permute-start | bytes 110600 | tf_op jit(solution)/shard_map/ppermute | solution.py:34
  11.2 4.4 %collective-permute-start.2 = (f32[32,128]{1,0:T(8,128)S(1)}, f32[32,128]{1,0:T(8,128)S(1)}, u32[]{:S(2)}, u32[]{:S(2)}) collective-permute-start(f32[32,128]{1,0:T(8,128)S(1)} %get-tuple-element.47.after), channel_id=1, source_target_pairs={{0,1},{1,0},{2,3},{3,2},{4,5},{5,4},{6,7},{7,6},{8,9},{9,8},{10,11... | collective-permute-start | bytes 49160 | tf_op jit(solution)/shard_map/ppermute | solution.py:34
  12.8 3.5 %copy-start.3 = (s32[96]{0:T(128)S(1)}, s32[96]{0:T(128)}, u32[]{:S(2)}) copy-start(s32[96]{0:T(128)} %param.17) | copy-start | bytes 1156
  17.5 3.9 %collective-permute-start.5 = (f32[64,128]{1,0:T(8,128)S(1)}, f32[64,128]{1,0:T(8,128)S(1)}, u32[]{:S(2)}, u32[]{:S(2)}) collective-permute-start(f32[64,128]{1,0:T(8,128)S(1)} %get-tuple-element.59), channel_id=1, source_target_pairs={{0,1},{1,0},{2,3},{3,2},{4,5},{5,4},{6,7},{7,6},{8,9},{9,8},{10,11... | collective-permute-start | bytes 98312 | tf_op jit(solution)/shard_map/ppermute | solution.py:34

commit v5 on v4

--- a/solution.py
+++ b/solution.py
@@ -78,79 +78,57 @@
     return jnp.where(lane_ids(a.shape[0]) == 0, move(packed, lane, 0), pltpu.roll(a, 1, 1))
 
 
-def first_faces_body(ef, ea, xs, ys, evf, eva, sems):
-    fields = ((ef, evf), (ea, eva))
-    nx = ef.shape[1]
+def first_faces_body(ef, ea, hf, ha, xs, ys, evf, eva, hvf, hva, along_x, along_y, sems):
+    fields = (evf, eva)
+    _, nx, ny, _ = ef.shape
     copies = {}
+    for k, (pair, held) in enumerate((((ef, ea), (evf, eva)), ((hf, ha), (hvf, hva)))):
+        for c in range(3):
+            for r in range(2):
+                copies[k, c, r] = pltpu.make_async_copy(pair[r].at[c], held[r].at[c], sems.at[k, r, c])
+                copies[k, c, r].start()
     for c in range(3):
-        for r, (e, v) in enumerate(fields):
-            copies[c, r] = pltpu.make_async_copy(e.at[c], v.at[c], sems.at[r, c])
-            copies[c, r].start()
-    for c in range(3):
-        for r, (_, v) in enumerate(fields):
-            copies[c, r].wait()
+        for r, v in enumerate(fields):
+            copies[0, c, r].wait()
             if c != 1:
                 for x in range(nx):
                     ys[r, c // 2, x : x + 1, :] = v[c, x, 0:1, :]
             if c:
                 xs[r, c - 1] = v[c, 0]
-
-
-def first_faces(ef, ea):
-    _, nx, ny, nz = ef.shape
-    field = vmem(3, nx, ny, nz)
-    return call(
-        first_faces_body,
-        "first_faces",
-        (vmem(2, 2, ny, nz), vmem(2, 2, nx, nz), field, field),
-        (VMEM,) * 4,
-        [ANY, ANY],
-        [pltpu.SemaphoreType.DMA((2, 3))],
-        nbytes=1500000,
-    )(hbm(ef), hbm(ea))
-
-
-def load_body(hf, ha, ef, ea, after, hvf, hva, along_x, along_y, sems):
-    _, nx, ny, _ = ef.shape
-    copies = []
-    for r, (h, v) in enumerate(((hf, hvf), (ha, hva))):
-        for c in range(3):
-            copies.append(pltpu.make_async_copy(h.at[c], v.at[c], sems.at[r, c]))
-    for copy in copies:
-        copy.start()
     lane, lane_8 = lane_ids(ny), lane_ids(8)
     by_x = jnp.zeros((ny, LANES), jnp.float32)
     by_y = jnp.zeros((8, LANES), jnp.float32)
-    for r, e in enumerate((ef, ea)):
+    for r, e in enumerate(fields):
         by_x = jnp.where(lane == r * nx, move(e[0, nx - 1], 0, r * nx), by_x)
         for x in range(nx):
             by_y = jnp.where(lane_8 == r * nx + x, move(e[1, x, ny - 8 : ny, :], 0, r * nx + x), by_y)
     along_x[...] = by_x
     along_y[...] = jnp.where(row_ids(8) == 0, pltpu.roll(by_y, 1, 0), 0.0)
-    for copy in copies:
-        copy.wait()
-
-
-def load(hf, ha, ef, ea, after):
+    for c in range(3):
+        for r in range(2):
+            copies[1, c, r].wait()
+
+
+def first_faces(ef, ea, hf, ha):
     _, nx, ny, nz = ef.shape
     field = vmem(3, nx, ny, nz)
     return call(
-        load_body,
-        "load",
-        (field, field, vmem(ny, LANES), vmem(8, LANES)),
-        (VMEM,) * 4,
-        [ANY, ANY, VMEM, VMEM, ANY],
-        [pltpu.SemaphoreType.DMA((2, 3))],
-        nbytes=1500000,
-    )(hbm(hf), hbm(ha), ef, ea, after)
+        first_faces_body,
+        "first_faces",
+        (vmem(2, 2, ny, nz), vmem(2, 2, nx, nz)) + (field,) * 4 + (vmem(ny, LANES), vmem(8, LANES)),
+        (VMEM,) * 8,
+        [ANY] * 4,
+        [pltpu.SemaphoreType.DMA((2, 2, 3))],
+        nbytes=3000000,
+    )(hbm(ef), hbm(ea), hbm(hf), hbm(ha))
 
 
 def magnetic_update(e, h, x, rows, next_x, next_y, r):
     nx = e.shape[1]
     ex, ey, ez = e[0, x, rows], e[1, x, rows], e[2, x, rows]
     ey_x, ez_x = (e[1, x + 1, rows], e[2, x + 1, rows]) if x + 1 < nx else (next_x[r, 0, rows], next_x[r, 1, rows])
-    ex_y = up_y(ex, next_y[r, 0, x : x + 1, :])
-    ez_y = up_y(ez, next_y[r, 1, x : x + 1, :])
+    ex_y = up_y(ex, 0.0 if next_y is None else next_y[r, 0, x : x + 1, :])
+    ez_y = up_y(ez, 0.0 if next_y is None else next_y[r, 1, x : x + 1, :])
     ex_z = up_z(ex)
     ey_z = up_z(ey)
     hx = h[0, x, rows] - COURANT * ((ez_y - ez) - (ey_z - ey))
@@ -159,30 +137,47 @@
     return hx, hy, hz
 
 
-def last_faces_body(ef, ea, hf, ha, xr, yr, along_x, along_y, xs, ys):
+def last_y_body(ef, ea, hf, ha, xr, along_y, ys):
     _, nx, ny, _ = ef.shape
     last = slice(ny - 8, ny)
     for r, (e, h) in enumerate(((ef, hf), (ea, ha))):
         for x in range(nx):
-            hx, _, hz = magnetic_update(e, h, x, last, xr, yr, r)
+            hx, _, hz = magnetic_update(e, h, x, last, xr, None, r)
             for c, a in enumerate((hx, hz)):
                 at = packed_lane(r, c, x, nx)
                 ys[at : at + 1, :] = a[7:8, :]
+    ys[4 * nx : 4 * nx + 8, :] = along_y[...]
+
+
+def last_y(ef, ea, hf, ha, xr, along_y):
+    _, nx, ny, nz = ef.shape
+    return call(
+        last_y_body,
+        "last_y",
+        vmem(4 * nx + 112, nz),
+        VMEM,
+        [VMEM] * 6,
+        nbytes=500000,
+    )(ef, ea, hf, ha, xr, along_y)
+
+
+def last_x_body(ef, ea, hf, ha, xr, yr, along_x, after, xs):
+    _, nx, ny, _ = ef.shape
+    for r, (e, h) in enumerate(((ef, hf), (ea, ha))):
         _, xs[r * 2], xs[r * 2 + 1] = magnetic_update(e, h, nx - 1, slice(0, ny), xr, yr, r)
     xs[4] = along_x[...]
-    ys[4 * nx : 4 * nx + 8, :] = along_y[...]
-
-
-def last_faces(ef, ea, hf, ha, xr, yr, along_x, along_y):
-    _, nx, ny, nz = ef.shape
-    return call(
-        last_faces_body,
-        "last_faces",
-        (vmem(5, ny, nz), vmem(4 * nx + 8, nz)),
-        (VMEM,) * 2,
-        [VMEM] * 8,
+
+
+def last_x(ef, ea, hf, ha, xr, yr, along_x, after):
+    _, nx, ny, nz = ef.shape
+    return call(
+        last_x_body,
+        "last_x",
+        vmem(5, ny, nz),
+        VMEM,
+        [VMEM] * 7 + [ANY],
         nbytes=500000,
-    )(ef, ea, hf, ha, xr, yr, along_x, along_y)
+    )(ef, ea, hf, ha, xr, yr, along_x, after)
 
 
 def magnetic_body(ef, ea, hf, ha, xr, yr, after, hfn, han, layer, zs):
@@ -254,13 +249,8 @@
     return (1 - lax.axis_index("gz")) * (nz - half)
 
 
-def spectra_body(half, nz, chunk, df, dav, freq, material, after, out, still, dfv, sems):
-    freqs, nx, ny = df.shape[0], df.shape[3], df.shape[4]
-    copies = {}
-    for i in range(nx // chunk):
-        part = pl.ds(i * chunk, chunk)
-        copies[i] = pltpu.make_async_copy(df.at[:, :, :, part], dfv.at[:, :, :, part], sems.at[i])
-        copies[i].start()
+def spectra_body(half, nz, dfv, dav, freq, material, after, out, still):
+    freqs, nx, ny = dfv.shape[0], dfv.shape[3], dfv.shape[4]
     phase = freq[...] * float(STEP)
     cos, sin = jnp.cos(phase), jnp.sin(phase)
     cs = [jnp.broadcast_to(cos[:, f : f + 1], (ny, half)) for f in range(freqs)]
@@ -272,8 +262,6 @@
         return pltpu.roll(jnp.concatenate([a, blank], axis=1), shift, 1)
 
     for x in range(nx):
-        if x % chunk == 0:
-            copies[x // chunk].wait()
         base = jnp.zeros((ny, half), jnp.float32)
         for c in range(3):
             with_forward = jnp.zeros((ny, half), jnp.float32)
@@ -296,18 +284,15 @@
 
 
 def spectra(df, da, freq, material, after, nz):
-    freqs, _, _, nx, ny, half = df.shape
-    chunk = 2
-    held = vmem(*df.shape)
-    return call(
-        functools.partial(spectra_body, half, nz, chunk),
+    _, _, _, nx, ny, half = df.shape
+    return call(
+        functools.partial(spectra_body, half, nz),
         "spectra",
         (vmem(7, nx, ny, LANES), vmem(3, ny, LANES)),
         (VMEM,) * 2,
-        [ANY, VMEM, VMEM, VMEM, ANY],
-        [held, pltpu.SemaphoreType.DMA((nx // chunk,))],
+        [VMEM] * 4 + [ANY],
         nbytes=11000000,
-    )(hbm(df), da, freq, material, after)
+    )(df, da, freq, material, after)
 
 
 def complete_body(hf, ha, zr, layer, hfn, han, below):
@@ -337,7 +322,7 @@
 
 
 def electric_body(
-    half, owned, ef, ea, hf, ha, hzf, hza, material, xr, yr, zr, spec, still, freq, layer_map, efn, ean, own, other, tile
+    half, owned, ef, ea, hf, ha, hzf, hza, material, xr, yr, zr, first_y, spec, still, freq, layer_map, efn, ean, own, other, tile
 ):
     runs = ((ef, hf, hzf, efn), (ea, ha, hza, ean))
     _, nx, ny, nz = ef.shape
@@ -360,6 +345,8 @@
     middle = jnp.broadcast_to(layer_map[0:1, half - 1 : half], (2 * owned, 1)) == ids[:, 0:1]
     middle_share = jnp.sum(jnp.where(middle, share, 0.0), axis=0, keepdims=True)
     below = zr[...]
+    hx_below = [yr[2 * r * nx : (2 * r + 1) * nx, :] - COURANT * first_y[r, 1] for r in range(2)]
+    hz_below = [yr[(2 * r + 1) * nx : (2 * r + 2) * nx, :] + COURANT * first_y[r, 0] for r in range(2)]
     dims = (((1,), (1,)), ((), ()))
     group = LANES // ny
     products = []
@@ -370,8 +357,8 @@
             at_x, at_y = packed_lane(r, 0, x, nx), packed_lane(r, 1, x, nx)
             hx, hy, hz_here = h[0, x], h[1, x], hz[2, x]
             hy_x, hz_x = (h[1, x - 1], hz[2, x - 1]) if x else (xr[2 * r], xr[2 * r + 1])
-            hx_y = down_y(hx, yr[at_x : at_x + 1, :])
-            hz_y = down_y(hz_here, yr[at_y : at_y + 1, :])
+            hx_y = down_y(hx, hx_below[r][x : x + 1, :])
+            hz_y = down_y(hz_here, hz_below[r][x : x + 1, :])
             hx_z = down_z(hx, below, at_x)
             hy_z = down_z(hy, below, at_y)
             ex = e[0, x] + coefficient * ((hz_here - hz_y) - (hy - hy_z))
@@ -412,7 +399,7 @@
     other[nx // group * owned :, :] = rest
 
 
-def electric(ef, ea, hf, ha, hzf, hza, material, xr, yr, zr, spec, still, freq, layer_map, half, owned):
+def electric(ef, ea, hf, ha, hzf, hza, material, xr, yr, zr, first_y, spec, still, freq, layer_map, half, owned):
     _, nx, ny, nz = ef.shape
     field = vmem(3, nx, ny, nz)
     rows = nx * ny // LANES * owned
@@ -421,9 +408,9 @@
         "electric",
         (field, field, vmem(rows, LANES), vmem(rows + ny, LANES), vmem(ny, LANES)),
         (VMEM,) * 5,
-        [VMEM] * 14,
+        [VMEM] * 15,
         nbytes=6700000,
-    )(ef, ea, hf, ha, hzf, hza, material, xr, yr, zr, spec, still, freq, layer_map)
+    )(ef, ea, hf, ha, hzf, hza, material, xr, yr, zr, first_y, spec, still, freq, layer_map)
 
 
 def store_body(ef, ea, hf, ha, hzf, hza, after, efn, ean, hfn, han, sems):
@@ -521,19 +508,19 @@
     layer_map = layer_map.reshape(1, -1)
     df = jnp.transpose(df, (0, 1, 2, 4, 5, 3))
     da = jnp.transpose(da, (0, 1, 2, 4, 5, 3))
-    xs, ys, ef, ea = first_faces(ef, ea)
-    yr = ring(ys, "gy", -1)
+    xs, first_y, ef, ea, hf, ha, along_x, along_y = first_faces(ef, ea, hf, ha)
+    yr = ring(first_y, "gy", -1)
     xr = ring(xs, "gx", -1)
-    hf, ha, along_x, along_y = load(hf, ha, ef, ea, ys)
-    xs, ys = last_faces(ef, ea, hf, ha, xr, yr, along_x, along_y)
-    hf, ha, layer, zs = magnetic(ef, ea, hf, ha, xr, yr, ys)
+    ys = last_y(ef, ea, hf, ha, xr, along_y)
+    xs = last_x(ef, ea, hf, ha, xr, yr, along_x, ys)
+    hf, ha, layer, zs = magnetic(ef, ea, hf, ha, xr, yr, xs)
     yr = ring(ys, "gy", 1)
     xr = ring(xs, "gx", 1)
     zr = ring(zs, "gz", 1)
     spec, still = spectra(df, da, freq, material, zs, nz)
     hxyf, hxya, below = complete(hf, ha, zr, layer)
     ef, ea, own, other, tile = electric(
-        ef, ea, hxyf, hxya, hf, ha, material, xr, yr, below, spec, still, freq, layer_map, half, owned
+        ef, ea, hxyf, hxya, hf, ha, material, xr, yr, below, first_y, spec, still, freq, layer_map, half, owned
     )
     came = ring(other, "gz", 1)
     efn, ean, hfn, han = store(ef, ea, hxyf, hxya, hf, ha, own)

time: 22.6 us -> 21.9 us (0.969)
  Pallas kernels: 11.1 us -> 8.6 us
  waiting for transfers between devices: 0.98 us -> 3.17 us
  starting transfers between devices: 9.55 us -> 9.26 us
    pallas_call x3, Pallas kernels: 4.48 us -> 1.43 us  [the longest x1 1.22 us: spectra(): call(functools.partial(spectra_body, half, nz), 'spectra', (vmem(7, nx, n...]
    ppermute x6, waiting for transfers between devices: 0.98 us -> 3.17 us  [ring(): return lax.ppermute(x, axis, [(i, (i + by) % peers) for i in range(peers)])]
    pallas_call x1, Pallas kernels: 1.41 us -> 1.93 us  [first_faces(): call(first_faces_body, 'first_faces', (vmem(2, 2, ny, nz), vmem(2, 2, nx,...]
    ppermute x6, starting transfers between devices: 9.55 us -> 9.26 us  [ring(): return lax.ppermute(x, axis, [(i, (i + by) % peers) for i in range(peers)])]
  transfers between devices with their start and end apart: 6 -> 6, of which waited for: 2 -> 3; matrix products, arithmetic and copies ran while one was open for 0% -> 0% of each run, Pallas kernels for 33% -> 21%
where the time goes in v5:
time: 21.9 us; the launch traced here: 21.8 us
  starting transfers between devices  9.26 us (42%)
  Pallas kernels  8.6 us (39%)
  waiting for transfers between devices  3.17 us (14%)
  between operations  0.74 us (3%)
    ppermute x6, starting transfers between devices, ring(): return lax.ppermute(x, axis, [(i, (i + by) % peers) for i in range(peers)])  9.26 us
    ppermute x6, waiting for transfers between devices, ring(): return lax.ppermute(x, axis, [(i, (i + by) % peers) for i in range(peers)])  3.17 us
    pallas_call x1, Pallas kernels, first_faces(): call(first_faces_body, 'first_faces', (vmem(2, 2, ny, nz), vmem(2, 2, nx,...  1.93 us
    pallas_call x1, Pallas kernels, store(): call(store_body, 'store', (field,) * 4, (ANY,) * 4, [VMEM] * 6 + [ANY], [...  1.75 us
    pallas_call x1, Pallas kernels, spectra(): call(functools.partial(spectra_body, half, nz), 'spectra', (vmem(7, nx, n...  1.22 us
    pallas_call x1, Pallas kernels, electric(): call(functools.partial(electric_body, half, owned), 'electric', (field, f...  1.07 us
    pallas_call x1, Pallas kernels, gradient(): pl.pallas_call(gradient_body, out_shape=(f32(owned, nx, ny), f32(*efn.sha...  1.02 us
    pallas_call x1, Pallas kernels, magnetic(): call(magnetic_body, 'magnetic', (field, field, vmem(ny, LANES), vmem(ny,...  1.01 us
  transfers between devices with their start and end apart: 6, of which 3 were waited for; matrix products, arithmetic and copies ran while one was open for 0% of the time, Pallas kernels for 21%

profile of v5, /device:TPU:0, one launch (start us, length us, event | category | flops | bytes accessed | tf_op | source)
XLA Modules:
  0.0 21.8 jit_solution(2462110017173878306)
XLA Ops:
  0.6 1.9 %first_faces.1 = (f32[2,2,32,128]{3,2,1,0:T(8,128)S(1)}, f32[2,2,16,128]{3,2,1,0:T(8,128)S(1)}, f32[3,16,32,128]{3,2,1,0:T(8,128)S(1)}, f32[3,16,32,128]{3,2,1,0...) custom-call(f32[3,16,32,128]{3,2,1,0:T(8,128)} %ef.1, ...), custom_call_target="tpu_custom_call" | custom-call | flops 3000000 | bytes 3000000 | tf_op jit(solution)/shard_map/first_faces/pallas_call | solution.py:115
  2.6 2.4 %collective-permute-start = (f32[2,2,32,128]{3,2,1,0:T(8,128)S(1)}, f32[2,2,32,128]{3,2,1,0:T(8,128)S(1)}, u32[]{:S(2)}, u32[]{:S(2)}) collective-permute-start(f32[2,2,32,128]{3,2,1,0:T(8,128)S(1)} %get-tuple-element.38), channel_id=1, source_target_pairs={{0,24},{8,0},{16,8},{24,16},{1,25},{9,1},{17,9},{25,17},{2,26},{10... | collective-permute-start | bytes 196616 | tf_op jit(solution)/shard_map/ppermute | solution.py:34
  5.0 3.6 %collective-permute-start.1 = (f32[2,2,16,128]{3,2,1,0:T(8,128)S(1)}, f32[2,2,16,128]{3,2,1,0:T(8,128)S(1)}, u32[]{:S(2)}, u32[]{:S(2)}) collective-permute-start(f32[2,2,16,128]{3,2,1,0:T(8,128)S(1)} %get-tuple-element.39.first_y), channel_id=1, source_target_pairs={{0,6},{2,0},{4,2},{6,4},{1,7},{3,1},{5,3},{7,5},{8,14},{10,8},{12,... | collective-permute-start | bytes 98312 | tf_op jit(solution)/shard_map/ppermute | solution.py:34
  8.6 0.0 collective-permute-done.xr
  8.6 0.0 copy-start.3
  8.6 0.1 last_y.1.after
  8.8 0.1 collective-permute-start.4
  8.8 1.6 %collective-permute-done.1.yr = f32[2,2,16,128]{3,2,1,0:T(8,128)S(1)} collective-permute-done((f32[2,2,16,128]{3,2,1,0:T(8,128)S(1)}, f32[2,2,16,128]{3,2,1,0:T(8,128)S(1)}, u32[]{:S(2)}, u32[]{:S(2)}) %collective-permute-start.1) | collective-permute-done | bytes 32800 | tf_op jit(solution)/shard_map/ppermute | solution.py:34
  10.4 0.1 last_x.1.after
  10.5 0.1 collective-permute-start.3
  10.5 1.0 %magnetic.1 = (f32[3,16,32,128]{3,2,1,0:T(8,128)S(1)}, f32[3,16,32,128]{3,2,1,0:T(8,128)S(1)}, f32[32,128]{1,0:T(8,128)S(1)}, f32[32,128]{1,0:T(8,128)S(1)}) custom-call(f32[3,16,32,128]{3,2,1,0:T(8,128)S(1)} %get-tuple-element.34.ef, f32[3,16,32,128]{3,2,1,0:T(8,128)S(1)} %get-tuple-element.35.ea, f32[3,16,32,128]{3,2,1,0:T(8,128)S(1)} %get-tuple-element.36.hf, ...), custom_call_target="tpu_custom_call" | custom-call | flops 4800000 | bytes 4800000 | tf_op jit(solution)/shard_map/magnetic/pallas_call | solution.py:196
  11.5 1.6 %collective-permute-start.2 = (f32[32,128]{1,0:T(8,128)S(1)}, f32[32,128]{1,0:T(8,128)S(1)}, u32[]{:S(2)}, u32[]{:S(2)}) collective-permute-start(f32[32,128]{1,0:T(8,128)S(1)} %get-tuple-element.44.after), channel_id=1, source_target_pairs={{0,1},{1,0},{2,3},{3,2},{4,5},{5,4},{6,7},{7,6},{8,9},{9,8},{10,11... | collective-permute-start | bytes 49160 | tf_op jit(solution)/shard_map/ppermute | solution.py:34
  13.1 0.0 copy-done.2
  13.1 0.0 copy-start.4
  13.2 1.2 %spectra.1 = (f32[7,16,32,128]{3,2,1,0:T(8,128)S(1)}, f32[3,32,128]{2,1,0:T(8,128)S(1)}) custom-call(f32[3,2,3,16,32,48]{5,4,3,2,1,0:T(8,128)S(1)} %bitcast.4, f32[3,2,3,16,32,48]{5,4,3,2,1,0:T(8,128)S(1)} %bitcast.5, f32[1,3]{1,0:T(1,128)S(1)} %bitcast.6, s32[16,32,128]{2,1,0:T(8,128)S(1)} %copy-done.2, f32[32,128]{1,0:T(8,128)S(1)} %get-tuple-element.44.after), custom_call_target="tpu_custom_call" | custom-call | flops 11000000 | bytes 11000000 | tf_op jit(solution)/shard_map/spectra/pallas_call | solution.py:288
  14.4 1.0 %collective-permute-done.2.zr = f32[32,128]{1,0:T(8,128)S(1)} collective-permute-done((f32[32,128]{1,0:T(8,128)S(1)}, f32[32,128]{1,0:T(8,128)S(1)}, u32[]{:S(2)}, u32[]{:S(2)}) %collective-permute-start.2) | collective-permute-done | bytes 16416 | tf_op jit(solution)/shard_map/ppermute | solution.py:34
  15.3 0.4 %complete.1 = (f32[2,16,32,128]{3,2,1,0:T(8,128)S(1)}, f32[2,16,32,128]{3,2,1,0:T(8,128)S(1)}, f32[32,128]{1,0:T(8,128)S(1)}) custom-call(f32[3,16,32,128]{3,2,1,0:T(8,128)S(1)} %get-tuple-element.42.hf.hzf, f32[3,16,32,128]{3,2,1,0:T(8,128)S(1)} %get-tuple-element.43.ha.hza, f32[32,128]{1,0:T(8,128)S(1)} %collective-permute-done.2.zr, ...), custom_call_target="tpu_custom_call" | custom-call | flops 2000000 | bytes 2000000 | tf_op jit(solution)/shard_map/complete/pallas_call | solution.py:314
  15.8 0.0 collective-permute-done.3.xr
  15.8 0.0 collective-permute-done.4.yr
  15.8 1.1 %electric.1 = (f32[3,16,32,128]{3,2,1,0:T(8,128)S(1)}, f32[3,16,32,128]{3,2,1,0:T(8,128)S(1)}, f32[32,128]{1,0:T(8,128)S(1)}, f32[64,128]{1,0:T(8,128)S(1)}, f32[32,128]{1,0:T(8,128)S(1)}) custom-call(f32[3,16,32,128]{3,2,1,0:T(8,128)S(1)} %get-tuple-element.34.ef, f32[3,16,32,128]{3,2,1,0:T(8,128)S(1)} %get-tuple-element.35.ea, ...), custom_call_target="tpu_custom_call" | custom-call | flops 6700000 | bytes 6700000 | tf_op jit(solution)/shard_map/electric/pallas_call | solution.py:406
  16.9 1.5 %collective-permute-start.5 = (f32[64,128]{1,0:T(8,128)S(1)}, f32[64,128]{1,0:T(8,128)S(1)}, u32[]{:S(2)}, u32[]{:S(2)}) collective-permute-start(f32[64,128]{1,0:T(8,128)S(1)} %get-tuple-element.55), channel_id=1, source_target_pairs={{0,1},{1,0},{2,3},{3,2},{4,5},{5,4},{6,7},{7,6},{8,9},{9,8},{10,11... | collective-permute-start | bytes 98312 | tf_op jit(solution)/shard_map/ppermute | solution.py:34
  18.4 1.8 %store.1 = (f32[3,16,32,128]{3,2,1,0:T(8,128)}, f32[3,16,32,128]{3,2,1,0:T(8,128)}, f32[3,16,32,128]{3,2,1,0:T(8,128)}, f32[3,16,32,128]{3,2,1,0:T(8,128)}) custom-call(f32[3,16,32,128]{3,2,1,0:T(8,128)S(1)} %get-tuple-element.51.ef, f32[3,16,32,128]{3,2,1,0:T(8,128)S(1)} %get-tuple-element.52.ea, f32[2,16,32,128]{3,2,1,0:T(8,128)S(1)} %get-tuple-element.46.hf, ...), custom_call_target="tpu_custom_call" | custom-call | flops 3000000 | bytes 3000000 | tf_op jit(solution)/shard_map/store/pallas_call | solution.py:430
  20.1 0.6 %collective-permute-done.5.came = f32[64,128]{1,0:T(8,128)S(1)} collective-permute-done((f32[64,128]{1,0:T(8,128)S(1)}, f32[64,128]{1,0:T(8,128)S(1)}, u32[]{:S(2)}, u32[]{:S(2)}) %collective-permute-start.5) | collective-permute-done | bytes 32800 | tf_op jit(solution)/shard_map/ppermute | solution.py:34
  20.8 1.0 %gradient.1 = (f32[8,16,32]{2,1,0:T(8,128)}, f32[3,16,32,128]{3,2,1,0:T(8,128)}, f32[3,16,32,128]{3,2,1,0:T(8,128)}) custom-call(f32[3,16,32,128]{3,2,1,0:T(8,128)S(1)} %get-tuple-element.51.ef, f32[3,16,32,128]{3,2,1,0:T(8,128)S(1)} %get-tuple-element.52.ea, ...), custom_call_target="tpu_custom_call", output_to_operand_aliasing={{1}: (6, {}), {2}: (7, {})} | custom-call | flops 100000 | bytes 400000 | tf_op jit(solution)/shard_map/gradient/pallas_call | solution.py:485
  (7 shorter events, 0.0 us)
Async XLA Ops:
  2.6 6.0 %collective-permute-start = (f32[2,2,32,128]{3,2,1,0:T(8,128)S(1)}, f32[2,2,32,128]{3,2,1,0:T(8,128)S(1)}, u32[]{:S(2)}, u32[]{:S(2)}) collective-permute-start(f32[2,2,32,128]{3,2,1,0:T(8,128)S(1)} %get-tuple-element.38), channel_id=1, source_target_pairs={{0,24},{8,0},{16,8},{24,16},{1,25},{9,1},{17,9},{25,17},{2,26},{10... | collective-permute-start | bytes 196616 | tf_op jit(solution)/shard_map/ppermute | solution.py:34
  5.0 5.4 %collective-permute-start.1 = (f32[2,2,16,128]{3,2,1,0:T(8,128)S(1)}, f32[2,2,16,128]{3,2,1,0:T(8,128)S(1)}, u32[]{:S(2)}, u32[]{:S(2)}) collective-permute-start(f32[2,2,16,128]{3,2,1,0:T(8,128)S(1)} %get-tuple-element.39.first_y), channel_id=1, source_target_pairs={{0,6},{2,0},{4,2},{6,4},{1,7},{3,1},{5,3},{7,5},{8,14},{10,8},{12,... | collective-permute-start | bytes 98312 | tf_op jit(solution)/shard_map/ppermute | solution.py:34
  8.6 4.5 %copy-start = (f32[3,2,3,48,16,32]{3,5,4,2,1,0:T(8,128)S(1)}, f32[3,2,3,48,16,32]{3,5,4,2,1,0:T(8,128)}, u32[]{:S(2)}) copy-start(f32[3,2,3,48,16,32]{3,5,4,2,1,0:T(8,128)} %param.14) | copy-start | bytes 5308420
  8.6 4.5 %copy-start.1 = (f32[3,2,3,48,16,32]{3,5,4,2,1,0:T(8,128)S(1)}, f32[3,2,3,48,16,32]{3,5,4,2,1,0:T(8,128)}, u32[]{:S(2)}) copy-start(f32[3,2,3,48,16,32]{3,5,4,2,1,0:T(8,128)} %param.15) | copy-start | bytes 5308420
  8.6 4.5 %copy-start.2 = (s32[16,32,128]{2,1,0:T(8,128)S(1)}, s32[16,32,128]{2,1,0:T(8,128)}, u32[]{:S(2)}) copy-start(s32[16,32,128]{2,1,0:T(8,128)} %material.3) | copy-start | bytes 786436
  8.6 4.5 %copy-start.3 = (f32[3]{0:T(128)S(1)}, f32[3]{0:T(128)}, u32[]{:S(2)}) copy-start(f32[3]{0:T(128)} %param.16) | copy-start | bytes 40
  8.8 7.0 %collective-permute-start.4 = (f32[176,128]{1,0:T(8,128)S(1)}, f32[176,128]{1,0:T(8,128)S(1)}, u32[]{:S(2)}, u32[]{:S(2)}) collective-permute-start(f32[176,128]{1,0:T(8,128)S(1)} %last_y.1.after), channel_id=1, source_target_pairs={{0,2},{2,4},{4,6},{6,0},{1,3},{3,5},{5,7},{7,1},{8,10},{10,12},{12... | collective-permute-start | bytes 270344 | tf_op jit(solution)/shard_map/ppermute | solution.py:34
  10.5 5.3 %collective-permute-start.3 = (f32[5,32,128]{2,1,0:T(8,128)S(1)}, f32[5,32,128]{2,1,0:T(8,128)S(1)}, u32[]{:S(2)}, u32[]{:S(2)}) collective-permute-start(f32[5,32,128]{2,1,0:T(8,128)S(1)} %last_x.1.after), channel_id=1, source_target_pairs={{0,8},{8,16},{16,24},{24,0},{1,9},{9,17},{17,25},{25,1},{2,10},{10... | collective-permute-start | bytes 245768 | tf_op jit(solution)/shard_map/ppermute | solution.py:34
  11.5 3.8 %collective-permute-start.2 = (f32[32,128]{1,0:T(8,128)S(1)}, f32[32,128]{1,0:T(8,128)S(1)}, u32[]{:S(2)}, u32[]{:S(2)}) collective-permute-start(f32[32,128]{1,0:T(8,128)S(1)} %get-tuple-element.44.after), channel_id=1, source_target_pairs={{0,1},{1,0},{2,3},{3,2},{4,5},{5,4},{6,7},{7,6},{8,9},{9,8},{10,11... | collective-permute-start | bytes 49160 | tf_op jit(solution)/shard_map/ppermute | solution.py:34
  13.1 2.6 %copy-start.4 = (s32[96]{0:T(128)S(1)}, s32[96]{0:T(128)}, u32[]{:S(2)}) copy-start(s32[96]{0:T(128)} %param.17) | copy-start | bytes 1156
  16.9 3.9 %collective-permute-start.5 = (f32[64,128]{1,0:T(8,128)S(1)}, f32[64,128]{1,0:T(8,128)S(1)}, u32[]{:S(2)}, u32[]{:S(2)}) collective-permute-start(f32[64,128]{1,0:T(8,128)S(1)} %get-tuple-element.55), channel_id=1, source_target_pairs={{0,1},{1,0},{2,3},{3,2},{4,5},{5,4},{6,7},{7,6},{8,9},{9,8},{10,11... | collective-permute-start | bytes 98312 | tf_op jit(solution)/shard_map/ppermute | solution.py:34

commit v6 on v5

--- a/solution.py
+++ b/solution.py
@@ -60,9 +60,9 @@
     return pltpu.roll(a, shift, 1) if shift else a
 
 
-def up_y(a, row):
+def up_y(a):
     n = a.shape[0]
-    return jnp.where(row_ids(n) == n - 1, jnp.broadcast_to(row, a.shape), pltpu.roll(a, n - 1, 0))
+    return jnp.where(row_ids(n) == n - 1, 0.0, pltpu.roll(a, n - 1, 0))
 
 
 def down_y(a, row):
@@ -99,10 +99,11 @@
     by_x = jnp.zeros((ny, LANES), jnp.float32)
     by_y = jnp.zeros((8, LANES), jnp.float32)
     for r, e in enumerate(fields):
-        by_x = jnp.where(lane == r * nx, move(e[0, nx - 1], 0, r * nx), by_x)
+        by_x = jnp.where(lane == r, move(e[0, nx - 1], 0, r), by_x)
         for x in range(nx):
             by_y = jnp.where(lane_8 == r * nx + x, move(e[1, x, ny - 8 : ny, :], 0, r * nx + x), by_y)
-    along_x[...] = by_x
+    turned = jnp.transpose(by_x)[0:8, :]
+    along_x[...] = jnp.concatenate([turned, jnp.zeros((8, LANES - ny), jnp.float32)], axis=1)
     along_y[...] = jnp.where(row_ids(8) == 0, pltpu.roll(by_y, 1, 0), 0.0)
     for c in range(3):
         for r in range(2):
@@ -115,7 +116,7 @@
     return call(
         first_faces_body,
         "first_faces",
-        (vmem(2, 2, ny, nz), vmem(2, 2, nx, nz)) + (field,) * 4 + (vmem(ny, LANES), vmem(8, LANES)),
+        (vmem(2, 2, ny, nz), vmem(2, 2, nx, nz)) + (field,) * 4 + (vmem(8, LANES), vmem(8, LANES)),
         (VMEM,) * 8,
         [ANY] * 4,
         [pltpu.SemaphoreType.DMA((2, 2, 3))],
@@ -123,12 +124,12 @@
     )(hbm(ef), hbm(ea), hbm(hf), hbm(ha))
 
 
-def magnetic_update(e, h, x, rows, next_x, next_y, r):
+def magnetic_update(e, h, x, rows, next_x, r):
     nx = e.shape[1]
     ex, ey, ez = e[0, x, rows], e[1, x, rows], e[2, x, rows]
     ey_x, ez_x = (e[1, x + 1, rows], e[2, x + 1, rows]) if x + 1 < nx else (next_x[r, 0, rows], next_x[r, 1, rows])
-    ex_y = up_y(ex, 0.0 if next_y is None else next_y[r, 0, x : x + 1, :])
-    ez_y = up_y(ez, 0.0 if next_y is None else next_y[r, 1, x : x + 1, :])
+    ex_y = up_y(ex)
+    ez_y = up_y(ez)
     ex_z = up_z(ex)
     ey_z = up_z(ey)
     hx = h[0, x, rows] - COURANT * ((ez_y - ez) - (ey_z - ey))
@@ -142,7 +143,7 @@
     last = slice(ny - 8, ny)
     for r, (e, h) in enumerate(((ef, hf), (ea, ha))):
         for x in range(nx):
-            hx, _, hz = magnetic_update(e, h, x, last, xr, None, r)
+            hx, _, hz = magnetic_update(e, h, x, last, xr, r)
             for c, a in enumerate((hx, hz)):
                 at = packed_lane(r, c, x, nx)
                 ys[at : at + 1, :] = a[7:8, :]
@@ -154,43 +155,23 @@
     return call(
         last_y_body,
         "last_y",
-        vmem(4 * nx + 112, nz),
+        vmem(4 * nx + 80, nz),
         VMEM,
         [VMEM] * 6,
         nbytes=500000,
     )(ef, ea, hf, ha, xr, along_y)
 
 
-def last_x_body(ef, ea, hf, ha, xr, yr, along_x, after, xs):
-    _, nx, ny, _ = ef.shape
-    for r, (e, h) in enumerate(((ef, hf), (ea, ha))):
-        _, xs[r * 2], xs[r * 2 + 1] = magnetic_update(e, h, nx - 1, slice(0, ny), xr, yr, r)
-    xs[4] = along_x[...]
-
-
-def last_x(ef, ea, hf, ha, xr, yr, along_x, after):
-    _, nx, ny, nz = ef.shape
-    return call(
-        last_x_body,
-        "last_x",
-        vmem(5, ny, nz),
-        VMEM,
-        [VMEM] * 7 + [ANY],
-        nbytes=500000,
-    )(ef, ea, hf, ha, xr, yr, along_x, after)
-
-
-def magnetic_body(ef, ea, hf, ha, xr, yr, after, hfn, han, layer, zs):
+def magnetic_body(ef, ea, hf, ha, xr, after, hfn, han, layer, top):
     _, nx, ny, nz = ef.shape
     for x in range(nx):
         for r, (e, h, hn) in enumerate(((ef, hf, hfn), (ea, ha, han))):
-            hn[0, x], hn[1, x], hn[2, x] = magnetic_update(e, h, x, slice(0, ny), xr, yr, r)
-    first = pack_layer((ef, ea), nx, ny, 0)
-    layer[...] = first
-    zs[...] = jnp.where(lax.axis_index("gz") == 0, pack_layer((hfn, han), nx, ny, nz - 1), first)
-
-
-def magnetic(ef, ea, hf, ha, xr, yr, after):
+            hn[0, x], hn[1, x], hn[2, x] = magnetic_update(e, h, x, slice(0, ny), xr, r)
+    layer[...] = pack_layer((ef, ea), nx, ny, 0)
+    top[...] = pack_layer((hfn, han), nx, ny, nz - 1)
+
+
+def magnetic(ef, ea, hf, ha, xr, after):
     _, nx, ny, nz = ef.shape
     field = vmem(3, nx, ny, nz)
     return call(
@@ -198,9 +179,47 @@
         "magnetic",
         (field, field, vmem(ny, LANES), vmem(ny, LANES)),
         (VMEM,) * 4,
-        [VMEM] * 6 + [ANY],
+        [VMEM] * 5 + [ANY],
         nbytes=4800000,
-    )(ef, ea, hf, ha, xr, yr, after)
+    )(ef, ea, hf, ha, xr, after)
+
+
+def last_faces_body(hf, ha, yr, along_x, layer, top, hfn, han, xs, zs):
+    _, nx, ny, nz = hf.shape
+    last = slice(ny - 8, ny)
+    edge, lane = row_ids(8) == 7, lane_ids(8)
+    rows = top[last, :]
+    for r, (h, hn) in enumerate(((hf, hfn), (ha, han))):
+        for x in range(nx):
+            hx = h[0, x, last, :] - COURANT * jnp.where(edge, jnp.broadcast_to(yr[r, 1, x : x + 1, :], (8, nz)), 0.0)
+            hz = h[2, x, last, :] + COURANT * jnp.where(edge, jnp.broadcast_to(yr[r, 0, x : x + 1, :], (8, nz)), 0.0)
+            hn[0, x, last, :] = hx
+            hn[2, x, last, :] = hz
+            to = packed_lane(r, 0, x, nx)
+            rows = jnp.where(lane == to, move(hx, nz - 1, to), rows)
+        at = r * 2 * ny
+        xs[at : at + ny, :] = h[1, nx - 1]
+        xs[at + ny : at + 2 * ny - 8, :] = h[2, nx - 1, 0 : ny - 8, :]
+        xs[at + 2 * ny - 8 : at + 2 * ny, :] = hz
+    xs[4 * ny :, :] = along_x[...]
+    lower = lax.axis_index("gz") == 0
+    zs[...] = jnp.where(lower, top[...], layer[...])
+    zs[last, :] = jnp.where(lower, rows, layer[last, :])
+
+
+def last_faces(hf, ha, yr, along_x, layer, top):
+    _, nx, ny, nz = hf.shape
+    field = vmem(3, nx, ny, nz)
+    return pl.pallas_call(
+        last_faces_body,
+        out_shape=(field, field, vmem(4 * ny + 8, nz), vmem(ny, LANES)),
+        in_specs=[VMEM] * 6,
+        out_specs=(VMEM,) * 4,
+        input_output_aliases={0: 0, 1: 1},
+        compiler_params=pltpu.CompilerParams(vmem_limit_bytes=32 * MIB),
+        cost_estimate=pl.CostEstimate(flops=500000, bytes_accessed=500000, transcendentals=0),
+        name="last_faces",
+    )(hf, ha, yr, along_x, layer, top)
 
 
 def packed_lane(r, c, x, nx):
@@ -356,7 +375,7 @@
         for r, (e, h, hz, en) in enumerate(runs):
             at_x, at_y = packed_lane(r, 0, x, nx), packed_lane(r, 1, x, nx)
             hx, hy, hz_here = h[0, x], h[1, x], hz[2, x]
-            hy_x, hz_x = (h[1, x - 1], hz[2, x - 1]) if x else (xr[2 * r], xr[2 * r + 1])
+            hy_x, hz_x = (h[1, x - 1], hz[2, x - 1]) if x else (xr[2 * r * ny : (2 * r + 1) * ny, :], xr[(2 * r + 1) * ny : (2 * r + 2) * ny, :])
             hx_y = down_y(hx, hx_below[r][x : x + 1, :])
             hz_y = down_y(hz_here, hz_below[r][x : x + 1, :])
             hx_z = down_z(hx, below, at_x)
@@ -392,7 +411,11 @@
     rest = rest + pltpu.roll(scaled * (still[1] + both * f), nx, 1)
     rest = rest + pltpu.roll(scaled * ratio * both, 2 * nx, 1)
     rest = rest + pltpu.roll(ratio, 3 * nx, 1)
-    along = xr[4]
+    turned = jnp.concatenate([xr[4 * ny :, :], jnp.zeros((ny - 8, LANES), jnp.float32)], axis=0)
+    turned = jnp.transpose(turned)[0:ny, :]
+    turned = jnp.concatenate([turned, jnp.zeros((ny, LANES - ny), jnp.float32)], axis=1)
+    lane = lane_ids(ny)
+    along = jnp.where(lane == 0, turned, jnp.where(lane == nx, move(turned, 1, nx), 0.0))
     along = along + jnp.concatenate([yr[4 * nx : 4 * nx + 8, :], jnp.zeros((ny - 8, LANES), jnp.float32)], axis=0)
     rest = jnp.where(lower, rest, along)
     tile[...] = rest
@@ -512,8 +535,8 @@
     yr = ring(first_y, "gy", -1)
     xr = ring(xs, "gx", -1)
     ys = last_y(ef, ea, hf, ha, xr, along_y)
-    xs = last_x(ef, ea, hf, ha, xr, yr, along_x, ys)
-    hf, ha, layer, zs = magnetic(ef, ea, hf, ha, xr, yr, xs)
+    hf, ha, layer, top = magnetic(ef, ea, hf, ha, xr, ys)
+    hf, ha, xs, zs = last_faces(hf, ha, yr, along_x, layer, top)
     yr = ring(ys, "gy", 1)
     xr = ring(xs, "gx", 1)
     zr = ring(zs, "gz", 1)

time: 21.9 us -> 21.3 us (0.973)
  waiting for transfers between devices: 3.17 us -> 2.24 us
  Pallas kernels: 8.6 us -> 8.83 us
    ppermute x6, waiting for transfers between devices: 3.17 us -> 2.24 us  [ring(): return lax.ppermute(x, axis, [(i, (i + by) % peers) for i in range(peers)])]
  transfers between devices with their start and end apart: 6 -> 6, of which waited for: 3 -> 4; matrix products, arithmetic and copies ran while one was open for 0% -> 0% of each run, Pallas kernels for 21% -> 22%
where the time goes in v6:
time: 21.3 us; the launch traced here: 21.1 us
  starting transfers between devices  9.26 us (43%)
  Pallas kernels  8.83 us (41%)
  waiting for transfers between devices  2.24 us (11%)
  between operations  0.76 us (4%)
    ppermute x6, starting transfers between devices, ring(): return lax.ppermute(x, axis, [(i, (i + by) % peers) for i in range(peers)])  9.26 us
    ppermute x6, waiting for transfers between devices, ring(): return lax.ppermute(x, axis, [(i, (i + by) % peers) for i in range(peers)])  2.24 us
    pallas_call x1, Pallas kernels, first_faces(): call(first_faces_body, 'first_faces', (vmem(2, 2, ny, nz), vmem(2, 2, nx,...  2.07 us
    pallas_call x1, Pallas kernels, store(): call(store_body, 'store', (field,) * 4, (ANY,) * 4, [VMEM] * 6 + [ANY], [...  1.75 us
    pallas_call x1, Pallas kernels, spectra(): call(functools.partial(spectra_body, half, nz), 'spectra', (vmem(7, nx, n...  1.22 us
    pallas_call x1, Pallas kernels, electric(): call(functools.partial(electric_body, half, owned), 'electric', (field, f...  1.06 us
    pallas_call x1, Pallas kernels, gradient(): pl.pallas_call(gradient_body, out_shape=(f32(owned, nx, ny), f32(*efn.sha...  1.01 us
    pallas_call x1, Pallas kernels, magnetic(): call(magnetic_body, 'magnetic', (field, field, vmem(ny, LANES), vmem(ny,...  0.99 us
  transfers between devices with their start and end apart: 6, of which 4 were waited for; matrix products, arithmetic and copies ran while one was open for 0% of the time, Pallas kernels for 22%

profile of v6, /device:TPU:0, one launch (start us, length us, event | category | flops | bytes accessed | tf_op | source)
XLA Modules:
  0.0 21.1 jit_solution(10717581556211713783)
XLA Ops:
  0.6 0.0 slice-start
  0.6 2.1 %first_faces.1 = (f32[2,2,32,128]{3,2,1,0:T(8,128)S(1)}, f32[2,2,16,128]{3,2,1,0:T(8,128)S(1)}, f32[3,16,32,128]{3,2,1,0:T(8,128)S(1)}, f32[3,16,32,128]{3,2,1,0...) custom-call(f32[3,16,32,128]{3,2,1,0:T(8,128)} %ef.1, ...), custom_call_target="tpu_custom_call" | custom-call | flops 3000000 | bytes 3000000 | tf_op jit(solution)/shard_map/first_faces/pallas_call | solution.py:116
  2.7 0.0 copy-start
  2.7 0.0 copy-start.1
  2.7 0.0 copy-start.2
  2.8 2.4 %collective-permute-start = (f32[2,2,32,128]{3,2,1,0:T(8,128)S(1)}, f32[2,2,32,128]{3,2,1,0:T(8,128)S(1)}, u32[]{:S(2)}, u32[]{:S(2)}) collective-permute-start(f32[2,2,32,128]{3,2,1,0:T(8,128)S(1)} %get-tuple-element.42), channel_id=1, source_target_pairs={{0,24},{8,0},{16,8},{24,16},{1,25},{9,1},{17,9},{25,17},{2,26},{10... | collective-permute-start | bytes 196616 | tf_op jit(solution)/shard_map/ppermute | solution.py:34
  5.2 3.6 %collective-permute-start.1 = (f32[2,2,16,128]{3,2,1,0:T(8,128)S(1)}, f32[2,2,16,128]{3,2,1,0:T(8,128)S(1)}, u32[]{:S(2)}, u32[]{:S(2)}) collective-permute-start(f32[2,2,16,128]{3,2,1,0:T(8,128)S(1)} %get-tuple-element.46.first_y), channel_id=1, source_target_pairs={{0,6},{2,0},{4,2},{6,4},{1,7},{3,1},{5,3},{7,5},{8,14},{10,8},{12,... | collective-permute-start | bytes 98312 | tf_op jit(solution)/shard_map/ppermute | solution.py:34
  8.8 0.1 last_y.1.after
  8.9 0.1 collective-permute-start.4
  9.0 1.0 %magnetic.1 = (f32[3,16,32,128]{3,2,1,0:T(8,128)S(1)}, f32[3,16,32,128]{3,2,1,0:T(8,128)S(1)}, f32[32,128]{1,0:T(8,128)S(1)}, f32[32,128]{1,0:T(8,128)S(1)}) custom-call(f32[3,16,32,128]{3,2,1,0:T(8,128)S(1)} %get-tuple-element.38.ef, f32[3,16,32,128]{3,2,1,0:T(8,128)S(1)} %get-tuple-element.39.ea, f32[3,16,32,128]{3,2,1,0:T(8,128)S(1)} %get-tuple-element.40.hf, ...), custom_call_target="tpu_custom_call" | custom-call | flops 4800000 | bytes 4800000 | tf_op jit(solution)/shard_map/magnetic/pallas_call | solution.py:177
  10.0 0.6 %collective-permute-done.1.yr = f32[2,2,16,128]{3,2,1,0:T(8,128)S(1)} collective-permute-done((f32[2,2,16,128]{3,2,1,0:T(8,128)S(1)}, f32[2,2,16,128]{3,2,1,0:T(8,128)S(1)}, u32[]{:S(2)}, u32[]{:S(2)}) %collective-permute-start.1) | collective-permute-done | bytes 32800 | tf_op jit(solution)/shard_map/ppermute | solution.py:34
  10.6 0.2 last_faces.1
  10.8 0.1 collective-permute-start.3
  10.8 1.6 %collective-permute-start.2 = (f32[32,128]{1,0:T(8,128)S(1)}, f32[32,128]{1,0:T(8,128)S(1)}, u32[]{:S(2)}, u32[]{:S(2)}) collective-permute-start(f32[32,128]{1,0:T(8,128)S(1)} %get-tuple-element.52.after), channel_id=1, source_target_pairs={{0,1},{1,0},{2,3},{3,2},{4,5},{5,4},{6,7},{7,6},{8,9},{9,8},{10,11... | collective-permute-start | bytes 49160 | tf_op jit(solution)/shard_map/ppermute | solution.py:34
  12.4 0.0 copy-start.3
  12.5 1.2 %spectra.1 = (f32[7,16,32,128]{3,2,1,0:T(8,128)S(1)}, f32[3,32,128]{2,1,0:T(8,128)S(1)}) custom-call(f32[3,2,3,16,32,48]{5,4,3,2,1,0:T(8,128)S(1)} %bitcast.6, f32[3,2,3,16,32,48]{5,4,3,2,1,0:T(8,128)S(1)} %bitcast.7, f32[1,3]{1,0:T(1,128)S(1)} %bitcast.8, s32[16,32,128]{2,1,0:T(8,128)S(1)} %copy-done.1, f32[32,128]{1,0:T(8,128)S(1)} %get-tuple-element.52.after), custom_call_target="tpu_custom_call" | custom-call | flops 11000000 | bytes 11000000 | tf_op jit(solution)/shard_map/spectra/pallas_call | solution.py:307
  13.7 0.9 %collective-permute-done.2.zr = f32[32,128]{1,0:T(8,128)S(1)} collective-permute-done((f32[32,128]{1,0:T(8,128)S(1)}, f32[32,128]{1,0:T(8,128)S(1)}, u32[]{:S(2)}, u32[]{:S(2)}) %collective-permute-start.2) | collective-permute-done | bytes 16416 | tf_op jit(solution)/shard_map/ppermute | solution.py:34
  14.6 0.4 %complete.1 = (f32[2,16,32,128]{3,2,1,0:T(8,128)S(1)}, f32[2,16,32,128]{3,2,1,0:T(8,128)S(1)}, f32[32,128]{1,0:T(8,128)S(1)}) custom-call(f32[3,16,32,128]{3,2,1,0:T(8,128)S(1)} %get-tuple-element.50.hf.hzf, f32[3,16,32,128]{3,2,1,0:T(8,128)S(1)} %get-tuple-element.51.ha.hza, f32[32,128]{1,0:T(8,128)S(1)} %collective-permute-done.2.zr, ...), custom_call_target="tpu_custom_call" | custom-call | flops 2000000 | bytes 2000000 | tf_op jit(solution)/shard_map/complete/pallas_call | solution.py:333
  15.1 0.1 collective-permute-done.4.yr
  15.1 1.1 %electric.1 = (f32[3,16,32,128]{3,2,1,0:T(8,128)S(1)}, f32[3,16,32,128]{3,2,1,0:T(8,128)S(1)}, f32[32,128]{1,0:T(8,128)S(1)}, f32[64,128]{1,0:T(8,128)S(1)}, f32[32,128]{1,0:T(8,128)S(1)}) custom-call(f32[3,16,32,128]{3,2,1,0:T(8,128)S(1)} %get-tuple-element.38.ef, f32[3,16,32,128]{3,2,1,0:T(8,128)S(1)} %get-tuple-element.39.ea, ...), custom_call_target="tpu_custom_call" | custom-call | flops 6700000 | bytes 6700000 | tf_op jit(solution)/shard_map/electric/pallas_call | solution.py:429
  16.2 1.5 %collective-permute-start.5 = (f32[64,128]{1,0:T(8,128)S(1)}, f32[64,128]{1,0:T(8,128)S(1)}, u32[]{:S(2)}, u32[]{:S(2)}) collective-permute-start(f32[64,128]{1,0:T(8,128)S(1)} %get-tuple-element.63), channel_id=1, source_target_pairs={{0,1},{1,0},{2,3},{3,2},{4,5},{5,4},{6,7},{7,6},{8,9},{9,8},{10,11... | collective-permute-start | bytes 98312 | tf_op jit(solution)/shard_map/ppermute | solution.py:34
  17.7 1.8 %store.1 = (f32[3,16,32,128]{3,2,1,0:T(8,128)}, f32[3,16,32,128]{3,2,1,0:T(8,128)}, f32[3,16,32,128]{3,2,1,0:T(8,128)}, f32[3,16,32,128]{3,2,1,0:T(8,128)}) custom-call(f32[3,16,32,128]{3,2,1,0:T(8,128)S(1)} %get-tuple-element.59.ef, f32[3,16,32,128]{3,2,1,0:T(8,128)S(1)} %get-tuple-element.60.ea, f32[2,16,32,128]{3,2,1,0:T(8,128)S(1)} %get-tuple-element.53.hf, ...), custom_call_target="tpu_custom_call" | custom-call | flops 3000000 | bytes 3000000 | tf_op jit(solution)/shard_map/store/pallas_call | solution.py:453
  19.5 0.6 %collective-permute-done.5.came = f32[64,128]{1,0:T(8,128)S(1)} collective-permute-done((f32[64,128]{1,0:T(8,128)S(1)}, f32[64,128]{1,0:T(8,128)S(1)}, u32[]{:S(2)}, u32[]{:S(2)}) %collective-permute-start.5) | collective-permute-done | bytes 32800 | tf_op jit(solution)/shard_map/ppermute | solution.py:34
  20.1 1.0 %gradient.1 = (f32[8,16,32]{2,1,0:T(8,128)}, f32[3,16,32,128]{3,2,1,0:T(8,128)}, f32[3,16,32,128]{3,2,1,0:T(8,128)}) custom-call(f32[3,16,32,128]{3,2,1,0:T(8,128)S(1)} %get-tuple-element.59.ef, f32[3,16,32,128]{3,2,1,0:T(8,128)S(1)} %get-tuple-element.60.ea, ...), custom_call_target="tpu_custom_call", output_to_operand_aliasing={{1}: (6, {}), {2}: (7, {})} | custom-call | flops 100000 | bytes 400000 | tf_op jit(solution)/shard_map/gradient/pallas_call | solution.py:508
  (10 shorter events, 0.0 us)
Async XLA Ops:
  0.6 11.8 %slice-start = ((s8[4718592]{0:T(1024)(128)(4,1)}), s8[4194304]{0:T(1024)(128)(4,1)S(1)}, s32[]{:S(2)}) async-start(s8[4718592]{0:T(1024)(128)(4,1)} %bitcast.4), calls=%async_computation | async-start | bytes 8388608
  2.7 9.7 %copy-start = (f32[3,2,3,48,16,32]{3,5,4,2,1,0:T(8,128)S(1)}, f32[3,2,3,48,16,32]{3,5,4,2,1,0:T(8,128)}, u32[]{:S(2)}) copy-start(f32[3,2,3,48,16,32]{3,5,4,2,1,0:T(8,128)} %param.15) | copy-start | bytes 5308420
  2.7 9.7 %copy-start.1 = (s32[16,32,128]{2,1,0:T(8,128)S(1)}, s32[16,32,128]{2,1,0:T(8,128)}, u32[]{:S(2)}) copy-start(s32[16,32,128]{2,1,0:T(8,128)} %material.3) | copy-start | bytes 786436
  2.7 9.7 %copy-start.2 = (f32[3]{0:T(128)S(1)}, f32[3]{0:T(128)}, u32[]{:S(2)}) copy-start(f32[3]{0:T(128)} %param.16) | copy-start | bytes 40
  2.8 6.0 %collective-permute-start = (f32[2,2,32,128]{3,2,1,0:T(8,128)S(1)}, f32[2,2,32,128]{3,2,1,0:T(8,128)S(1)}, u32[]{:S(2)}, u32[]{:S(2)}) collective-permute-start(f32[2,2,32,128]{3,2,1,0:T(8,128)S(1)} %get-tuple-element.42), channel_id=1, source_target_pairs={{0,24},{8,0},{16,8},{24,16},{1,25},{9,1},{17,9},{25,17},{2,26},{10... | collective-permute-start | bytes 196616 | tf_op jit(solution)/shard_map/ppermute | solution.py:34
  5.2 5.4 %collective-permute-start.1 = (f32[2,2,16,128]{3,2,1,0:T(8,128)S(1)}, f32[2,2,16,128]{3,2,1,0:T(8,128)S(1)}, u32[]{:S(2)}, u32[]{:S(2)}) collective-permute-start(f32[2,2,16,128]{3,2,1,0:T(8,128)S(1)} %get-tuple-element.46.first_y), channel_id=1, source_target_pairs={{0,6},{2,0},{4,2},{6,4},{1,7},{3,1},{5,3},{7,5},{8,14},{10,8},{12,... | collective-permute-start | bytes 98312 | tf_op jit(solution)/shard_map/ppermute | solution.py:34
  8.8 3.6 %slice-start.1 = ((s8[4718592]{0:T(1024)(128)(4,1)}), s8[524288]{0:T(1024)(128)(4,1)S(1)}, s32[]{:S(2)}) async-start(s8[4718592]{0:T(1024)(128)(4,1)} %bitcast.4), calls=%async_computation.1 | async-start | bytes 1048576
  8.9 6.2 %collective-permute-start.4 = (f32[144,128]{1,0:T(8,128)S(1)}, f32[144,128]{1,0:T(8,128)S(1)}, u32[]{:S(2)}, u32[]{:S(2)}) collective-permute-start(f32[144,128]{1,0:T(8,128)S(1)} %last_y.1.after), channel_id=1, source_target_pairs={{0,2},{2,4},{4,6},{6,0},{1,3},{3,5},{5,7},{7,1},{8,10},{10,12},{12... | collective-permute-start | bytes 221192 | tf_op jit(solution)/shard_map/ppermute | solution.py:34
  10.8 4.3 %collective-permute-start.3 = (f32[136,128]{1,0:T(8,128)S(1)}, f32[136,128]{1,0:T(8,128)S(1)}, u32[]{:S(2)}, u32[]{:S(2)}) collective-permute-start(f32[136,128]{1,0:T(8,128)S(1)} %get-tuple-element.55), channel_id=1, source_target_pairs={{0,8},{8,16},{16,24},{24,0},{1,9},{9,17},{17,25},{25,1},{2,10},{10... | collective-permute-start | bytes 208904 | tf_op jit(solution)/shard_map/ppermute | solution.py:34
  10.8 3.8 %collective-permute-start.2 = (f32[32,128]{1,0:T(8,128)S(1)}, f32[32,128]{1,0:T(8,128)S(1)}, u32[]{:S(2)}, u32[]{:S(2)}) collective-permute-start(f32[32,128]{1,0:T(8,128)S(1)} %get-tuple-element.52.after), channel_id=1, source_target_pairs={{0,1},{1,0},{2,3},{3,2},{4,5},{5,4},{6,7},{7,6},{8,9},{9,8},{10,11... | collective-permute-start | bytes 49160 | tf_op jit(solution)/shard_map/ppermute | solution.py:34
  12.4 2.7 %copy-start.3 = (s32[96]{0:T(128)S(1)}, s32[96]{0:T(128)}, u32[]{:S(2)}) copy-start(s32[96]{0:T(128)} %param.17) | copy-start | bytes 1156
  16.2 3.9 %collective-permute-start.5 = (f32[64,128]{1,0:T(8,128)S(1)}, f32[64,128]{1,0:T(8,128)S(1)}, u32[]{:S(2)}, u32[]{:S(2)}) collective-permute-start(f32[64,128]{1,0:T(8,128)S(1)} %get-tuple-element.63), channel_id=1, source_target_pairs={{0,1},{1,0},{2,3},{3,2},{4,5},{5,4},{6,7},{7,6},{8,9},{9,8},{10,11... | collective-permute-start | bytes 98312 | tf_op jit(solution)/shard_map/ppermute | solution.py:34

commit v7 on v6

--- a/solution.py
+++ b/solution.py
@@ -148,6 +148,7 @@
                 at = packed_lane(r, c, x, nx)
                 ys[at : at + 1, :] = a[7:8, :]
     ys[4 * nx : 4 * nx + 8, :] = along_y[...]
+    ys[4 * nx + 8 :, :] = jnp.zeros((ys.shape[0] - 4 * nx - 8, ys.shape[1]), jnp.float32)
 
 
 def last_y(ef, ea, hf, ha, xr, along_y):
@@ -155,7 +156,7 @@
     return call(
         last_y_body,
         "last_y",
-        vmem(4 * nx + 80, nz),
+        vmem(max(4 * nx, 4 * ny + 8) + 8, nz),
         VMEM,
         [VMEM] * 6,
         nbytes=500000,

time: 21.3 us -> 21.3 us (level)
  no operation moved by 1% of the time
where the time goes in v7:
time: 21.3 us; the launch traced here: 21.1 us
  starting transfers between devices  9.26 us (43%)
  Pallas kernels  8.83 us (41%)
  waiting for transfers between devices  2.24 us (11%)
  between operations  0.76 us (4%)
    ppermute x6, starting transfers between devices, ring(): return lax.ppermute(x, axis, [(i, (i + by) % peers) for i in range(peers)])  9.26 us
    ppermute x6, waiting for transfers between devices, ring(): return lax.ppermute(x, axis, [(i, (i + by) % peers) for i in range(peers)])  2.24 us
    pallas_call x1, Pallas kernels, first_faces(): call(first_faces_body, 'first_faces', (vmem(2, 2, ny, nz), vmem(2, 2, nx,...  2.07 us
    pallas_call x1, Pallas kernels, store(): call(store_body, 'store', (field,) * 4, (ANY,) * 4, [VMEM] * 6 + [ANY], [...  1.75 us
    pallas_call x1, Pallas kernels, spectra(): call(functools.partial(spectra_body, half, nz), 'spectra', (vmem(7, nx, n...  1.22 us
    pallas_call x1, Pallas kernels, electric(): call(functools.partial(electric_body, half, owned), 'electric', (field, f...  1.06 us
    pallas_call x1, Pallas kernels, gradient(): pl.pallas_call(gradient_body, out_shape=(f32(owned, nx, ny), f32(*efn.sha...  1.01 us
    pallas_call x1, Pallas kernels, magnetic(): call(magnetic_body, 'magnetic', (field, field, vmem(ny, LANES), vmem(ny,...  0.99 us
  transfers between devices with their start and end apart: 6, of which 4 were waited for; matrix products, arithmetic and copies ran while one was open for 0% of the time, Pallas kernels for 22%

profile of v7, /device:TPU:0, one launch (start us, length us, event | category | flops | bytes accessed | tf_op | source)
XLA Modules:
  0.0 21.1 jit_solution(1723651477297549850)
XLA Ops:
  0.6 0.0 slice-start
  0.6 2.1 %first_faces.1 = (f32[2,2,32,128]{3,2,1,0:T(8,128)S(1)}, f32[2,2,16,128]{3,2,1,0:T(8,128)S(1)}, f32[3,16,32,128]{3,2,1,0:T(8,128)S(1)}, f32[3,16,32,128]{3,2,1,0...) custom-call(f32[3,16,32,128]{3,2,1,0:T(8,128)} %ef.1, ...), custom_call_target="tpu_custom_call" | custom-call | flops 3000000 | bytes 3000000 | tf_op jit(solution)/shard_map/first_faces/pallas_call | solution.py:116
  2.7 0.0 copy-start
  2.7 0.0 copy-start.1
  2.7 0.0 copy-start.2
  2.8 2.4 %collective-permute-start = (f32[2,2,32,128]{3,2,1,0:T(8,128)S(1)}, f32[2,2,32,128]{3,2,1,0:T(8,128)S(1)}, u32[]{:S(2)}, u32[]{:S(2)}) collective-permute-start(f32[2,2,32,128]{3,2,1,0:T(8,128)S(1)} %get-tuple-element.42), channel_id=1, source_target_pairs={{0,24},{8,0},{16,8},{24,16},{1,25},{9,1},{17,9},{25,17},{2,26},{10... | collective-permute-start | bytes 196616 | tf_op jit(solution)/shard_map/ppermute | solution.py:34
  5.2 3.6 %collective-permute-start.1 = (f32[2,2,16,128]{3,2,1,0:T(8,128)S(1)}, f32[2,2,16,128]{3,2,1,0:T(8,128)S(1)}, u32[]{:S(2)}, u32[]{:S(2)}) collective-permute-start(f32[2,2,16,128]{3,2,1,0:T(8,128)S(1)} %get-tuple-element.46.first_y), channel_id=1, source_target_pairs={{0,6},{2,0},{4,2},{6,4},{1,7},{3,1},{5,3},{7,5},{8,14},{10,8},{12,... | collective-permute-start | bytes 98312 | tf_op jit(solution)/shard_map/ppermute | solution.py:34
  8.8 0.1 last_y.1.after
  8.9 0.1 collective-permute-start.4
  9.0 1.0 %magnetic.1 = (f32[3,16,32,128]{3,2,1,0:T(8,128)S(1)}, f32[3,16,32,128]{3,2,1,0:T(8,128)S(1)}, f32[32,128]{1,0:T(8,128)S(1)}, f32[32,128]{1,0:T(8,128)S(1)}) custom-call(f32[3,16,32,128]{3,2,1,0:T(8,128)S(1)} %get-tuple-element.38.ef, f32[3,16,32,128]{3,2,1,0:T(8,128)S(1)} %get-tuple-element.39.ea, f32[3,16,32,128]{3,2,1,0:T(8,128)S(1)} %get-tuple-element.40.hf, ...), custom_call_target="tpu_custom_call" | custom-call | flops 4800000 | bytes 4800000 | tf_op jit(solution)/shard_map/magnetic/pallas_call | solution.py:178
  10.0 0.6 %collective-permute-done.1.yr = f32[2,2,16,128]{3,2,1,0:T(8,128)S(1)} collective-permute-done((f32[2,2,16,128]{3,2,1,0:T(8,128)S(1)}, f32[2,2,16,128]{3,2,1,0:T(8,128)S(1)}, u32[]{:S(2)}, u32[]{:S(2)}) %collective-permute-start.1) | collective-permute-done | bytes 32800 | tf_op jit(solution)/shard_map/ppermute | solution.py:34
  10.6 0.2 last_faces.1
  10.8 0.1 collective-permute-start.3
  10.8 1.6 %collective-permute-start.2 = (f32[32,128]{1,0:T(8,128)S(1)}, f32[32,128]{1,0:T(8,128)S(1)}, u32[]{:S(2)}, u32[]{:S(2)}) collective-permute-start(f32[32,128]{1,0:T(8,128)S(1)} %get-tuple-element.52.after), channel_id=1, source_target_pairs={{0,1},{1,0},{2,3},{3,2},{4,5},{5,4},{6,7},{7,6},{8,9},{9,8},{10,11... | collective-permute-start | bytes 49160 | tf_op jit(solution)/shard_map/ppermute | solution.py:34
  12.4 0.0 copy-start.3
  12.5 1.2 %spectra.1 = (f32[7,16,32,128]{3,2,1,0:T(8,128)S(1)}, f32[3,32,128]{2,1,0:T(8,128)S(1)}) custom-call(f32[3,2,3,16,32,48]{5,4,3,2,1,0:T(8,128)S(1)} %bitcast.6, f32[3,2,3,16,32,48]{5,4,3,2,1,0:T(8,128)S(1)} %bitcast.7, f32[1,3]{1,0:T(1,128)S(1)} %bitcast.8, s32[16,32,128]{2,1,0:T(8,128)S(1)} %copy-done.1, f32[32,128]{1,0:T(8,128)S(1)} %get-tuple-element.52.after), custom_call_target="tpu_custom_call" | custom-call | flops 11000000 | bytes 11000000 | tf_op jit(solution)/shard_map/spectra/pallas_call | solution.py:308
  13.7 0.9 %collective-permute-done.2.zr = f32[32,128]{1,0:T(8,128)S(1)} collective-permute-done((f32[32,128]{1,0:T(8,128)S(1)}, f32[32,128]{1,0:T(8,128)S(1)}, u32[]{:S(2)}, u32[]{:S(2)}) %collective-permute-start.2) | collective-permute-done | bytes 16416 | tf_op jit(solution)/shard_map/ppermute | solution.py:34
  14.6 0.4 %complete.1 = (f32[2,16,32,128]{3,2,1,0:T(8,128)S(1)}, f32[2,16,32,128]{3,2,1,0:T(8,128)S(1)}, f32[32,128]{1,0:T(8,128)S(1)}) custom-call(f32[3,16,32,128]{3,2,1,0:T(8,128)S(1)} %get-tuple-element.50.hf.hzf, f32[3,16,32,128]{3,2,1,0:T(8,128)S(1)} %get-tuple-element.51.ha.hza, f32[32,128]{1,0:T(8,128)S(1)} %collective-permute-done.2.zr, ...), custom_call_target="tpu_custom_call" | custom-call | flops 2000000 | bytes 2000000 | tf_op jit(solution)/shard_map/complete/pallas_call | solution.py:334
  15.1 0.1 collective-permute-done.4.yr
  15.1 1.1 %electric.1 = (f32[3,16,32,128]{3,2,1,0:T(8,128)S(1)}, f32[3,16,32,128]{3,2,1,0:T(8,128)S(1)}, f32[32,128]{1,0:T(8,128)S(1)}, f32[64,128]{1,0:T(8,128)S(1)}, f32[32,128]{1,0:T(8,128)S(1)}) custom-call(f32[3,16,32,128]{3,2,1,0:T(8,128)S(1)} %get-tuple-element.38.ef, f32[3,16,32,128]{3,2,1,0:T(8,128)S(1)} %get-tuple-element.39.ea, ...), custom_call_target="tpu_custom_call" | custom-call | flops 6700000 | bytes 6700000 | tf_op jit(solution)/shard_map/electric/pallas_call | solution.py:430
  16.2 1.5 %collective-permute-start.5 = (f32[64,128]{1,0:T(8,128)S(1)}, f32[64,128]{1,0:T(8,128)S(1)}, u32[]{:S(2)}, u32[]{:S(2)}) collective-permute-start(f32[64,128]{1,0:T(8,128)S(1)} %get-tuple-element.63), channel_id=1, source_target_pairs={{0,1},{1,0},{2,3},{3,2},{4,5},{5,4},{6,7},{7,6},{8,9},{9,8},{10,11... | collective-permute-start | bytes 98312 | tf_op jit(solution)/shard_map/ppermute | solution.py:34
  17.7 1.8 %store.1 = (f32[3,16,32,128]{3,2,1,0:T(8,128)}, f32[3,16,32,128]{3,2,1,0:T(8,128)}, f32[3,16,32,128]{3,2,1,0:T(8,128)}, f32[3,16,32,128]{3,2,1,0:T(8,128)}) custom-call(f32[3,16,32,128]{3,2,1,0:T(8,128)S(1)} %get-tuple-element.59.ef, f32[3,16,32,128]{3,2,1,0:T(8,128)S(1)} %get-tuple-element.60.ea, f32[2,16,32,128]{3,2,1,0:T(8,128)S(1)} %get-tuple-element.53.hf, ...), custom_call_target="tpu_custom_call" | custom-call | flops 3000000 | bytes 3000000 | tf_op jit(solution)/shard_map/store/pallas_call | solution.py:454
  19.5 0.6 %collective-permute-done.5.came = f32[64,128]{1,0:T(8,128)S(1)} collective-permute-done((f32[64,128]{1,0:T(8,128)S(1)}, f32[64,128]{1,0:T(8,128)S(1)}, u32[]{:S(2)}, u32[]{:S(2)}) %collective-permute-start.5) | collective-permute-done | bytes 32800 | tf_op jit(solution)/shard_map/ppermute | solution.py:34
  20.1 1.0 %gradient.1 = (f32[8,16,32]{2,1,0:T(8,128)}, f32[3,16,32,128]{3,2,1,0:T(8,128)}, f32[3,16,32,128]{3,2,1,0:T(8,128)}) custom-call(f32[3,16,32,128]{3,2,1,0:T(8,128)S(1)} %get-tuple-element.59.ef, f32[3,16,32,128]{3,2,1,0:T(8,128)S(1)} %get-tuple-element.60.ea, ...), custom_call_target="tpu_custom_call", output_to_operand_aliasing={{1}: (6, {}), {2}: (7, {})} | custom-call | flops 100000 | bytes 400000 | tf_op jit(solution)/shard_map/gradient/pallas_call | solution.py:509
  (10 shorter events, 0.0 us)
Async XLA Ops:
  0.6 11.8 %slice-start = ((s8[4718592]{0:T(1024)(128)(4,1)}), s8[4194304]{0:T(1024)(128)(4,1)S(1)}, s32[]{:S(2)}) async-start(s8[4718592]{0:T(1024)(128)(4,1)} %bitcast.4), calls=%async_computation | async-start | bytes 8388608
  2.7 9.7 %copy-start = (f32[3,2,3,48,16,32]{3,5,4,2,1,0:T(8,128)S(1)}, f32[3,2,3,48,16,32]{3,5,4,2,1,0:T(8,128)}, u32[]{:S(2)}) copy-start(f32[3,2,3,48,16,32]{3,5,4,2,1,0:T(8,128)} %param.15) | copy-start | bytes 5308420
  2.7 9.7 %copy-start.1 = (s32[16,32,128]{2,1,0:T(8,128)S(1)}, s32[16,32,128]{2,1,0:T(8,128)}, u32[]{:S(2)}) copy-start(s32[16,32,128]{2,1,0:T(8,128)} %material.3) | copy-start | bytes 786436
  2.7 9.7 %copy-start.2 = (f32[3]{0:T(128)S(1)}, f32[3]{0:T(128)}, u32[]{:S(2)}) copy-start(f32[3]{0:T(128)} %param.16) | copy-start | bytes 40
  2.8 6.0 %collective-permute-start = (f32[2,2,32,128]{3,2,1,0:T(8,128)S(1)}, f32[2,2,32,128]{3,2,1,0:T(8,128)S(1)}, u32[]{:S(2)}, u32[]{:S(2)}) collective-permute-start(f32[2,2,32,128]{3,2,1,0:T(8,128)S(1)} %get-tuple-element.42), channel_id=1, source_target_pairs={{0,24},{8,0},{16,8},{24,16},{1,25},{9,1},{17,9},{25,17},{2,26},{10... | collective-permute-start | bytes 196616 | tf_op jit(solution)/shard_map/ppermute | solution.py:34
  5.2 5.4 %collective-permute-start.1 = (f32[2,2,16,128]{3,2,1,0:T(8,128)S(1)}, f32[2,2,16,128]{3,2,1,0:T(8,128)S(1)}, u32[]{:S(2)}, u32[]{:S(2)}) collective-permute-start(f32[2,2,16,128]{3,2,1,0:T(8,128)S(1)} %get-tuple-element.46.first_y), channel_id=1, source_target_pairs={{0,6},{2,0},{4,2},{6,4},{1,7},{3,1},{5,3},{7,5},{8,14},{10,8},{12,... | collective-permute-start | bytes 98312 | tf_op jit(solution)/shard_map/ppermute | solution.py:34
  8.8 3.6 %slice-start.1 = ((s8[4718592]{0:T(1024)(128)(4,1)}), s8[524288]{0:T(1024)(128)(4,1)S(1)}, s32[]{:S(2)}) async-start(s8[4718592]{0:T(1024)(128)(4,1)} %bitcast.4), calls=%async_computation.1 | async-start | bytes 1048576
  8.9 6.2 %collective-permute-start.4 = (f32[144,128]{1,0:T(8,128)S(1)}, f32[144,128]{1,0:T(8,128)S(1)}, u32[]{:S(2)}, u32[]{:S(2)}) collective-permute-start(f32[144,128]{1,0:T(8,128)S(1)} %last_y.1.after), channel_id=1, source_target_pairs={{0,2},{2,4},{4,6},{6,0},{1,3},{3,5},{5,7},{7,1},{8,10},{10,12},{12... | collective-permute-start | bytes 221192 | tf_op jit(solution)/shard_map/ppermute | solution.py:34
  10.8 4.3 %collective-permute-start.3 = (f32[136,128]{1,0:T(8,128)S(1)}, f32[136,128]{1,0:T(8,128)S(1)}, u32[]{:S(2)}, u32[]{:S(2)}) collective-permute-start(f32[136,128]{1,0:T(8,128)S(1)} %get-tuple-element.55), channel_id=1, source_target_pairs={{0,8},{8,16},{16,24},{24,0},{1,9},{9,17},{17,25},{25,1},{2,10},{10... | collective-permute-start | bytes 208904 | tf_op jit(solution)/shard_map/ppermute | solution.py:34
  10.8 3.8 %collective-permute-start.2 = (f32[32,128]{1,0:T(8,128)S(1)}, f32[32,128]{1,0:T(8,128)S(1)}, u32[]{:S(2)}, u32[]{:S(2)}) collective-permute-start(f32[32,128]{1,0:T(8,128)S(1)} %get-tuple-element.52.after), channel_id=1, source_target_pairs={{0,1},{1,0},{2,3},{3,2},{4,5},{5,4},{6,7},{7,6},{8,9},{9,8},{10,11... | collective-permute-start | bytes 49160 | tf_op jit(solution)/shard_map/ppermute | solution.py:34
  12.4 2.7 %copy-start.3 = (s32[96]{0:T(128)S(1)}, s32[96]{0:T(128)}, u32[]{:S(2)}) copy-start(s32[96]{0:T(128)} %param.17) | copy-start | bytes 1156
  16.2 3.9 %collective-permute-start.5 = (f32[64,128]{1,0:T(8,128)S(1)}, f32[64,128]{1,0:T(8,128)S(1)}, u32[]{:S(2)}, u32[]{:S(2)}) collective-permute-start(f32[64,128]{1,0:T(8,128)S(1)} %get-tuple-element.63), channel_id=1, source_target_pairs={{0,1},{1,0},{2,3},{3,2},{4,5},{5,4},{6,7},{7,6},{8,9},{9,8},{10,11... | collective-permute-start | bytes 98312 | tf_op jit(solution)/shard_map/ppermute | solution.py:34

commit v8 on v7

--- a/solution.py
+++ b/solution.py
@@ -263,6 +263,24 @@
             jnp.where(m == 2, COURANT / PERMITTIVITIES[2], COURANT / PERMITTIVITIES[3]),
         ),
     )
+
+
+def fold_cells(tile, nx):
+    lane = lane_ids(8)
+    folded = jnp.where(lane < 4 * nx, tile[0:8, :], 0.0)
+    for g in range(1, tile.shape[0] // 8):
+        here = (lane >= 4 * nx) & (lax.rem(lane, nx) == g)
+        folded = jnp.where(here, pltpu.roll(tile[8 * g : 8 * g + 8, :], 4 * nx + g, 1), folded)
+    return folded
+
+
+def unfold_cells(folded, rows, nx):
+    lane = lane_ids(8)
+    groups = [jnp.where(lane < 4 * nx, folded, 0.0)]
+    for g in range(1, rows // 8):
+        here = (lane < 4 * nx) & (lax.rem(lane, nx) == 0)
+        groups.append(jnp.where(here, pltpu.roll(folded, LANES - 4 * nx - g, 1), 0.0))
+    return jnp.concatenate(groups, axis=0)
 
 
 def slab_start(nz, half):
@@ -420,7 +438,7 @@
     along = along + jnp.concatenate([yr[4 * nx : 4 * nx + 8, :], jnp.zeros((ny - 8, LANES), jnp.float32)], axis=0)
     rest = jnp.where(lower, rest, along)
     tile[...] = rest
-    other[nx // group * owned :, :] = rest
+    other[nx // group * owned :, :] = fold_cells(rest, nx)
 
 
 def electric(ef, ea, hf, ha, hzf, hza, material, xr, yr, zr, first_y, spec, still, freq, layer_map, half, owned):
@@ -430,7 +448,7 @@
     return call(
         functools.partial(electric_body, half, owned),
         "electric",
-        (field, field, vmem(rows, LANES), vmem(rows + ny, LANES), vmem(ny, LANES)),
+        (field, field, vmem(rows, LANES), vmem(rows + 8, LANES), vmem(ny, LANES)),
         (VMEM,) * 5,
         [VMEM] * 15,
         nbytes=6700000,
@@ -469,7 +487,7 @@
     gz = lax.axis_index("gz")
     lower = gz == 0
     sums = own.shape[0]
-    mine, theirs = tile[...], came[sums:, :]
+    mine, theirs = tile[...], unfold_cells(came[sums:, :], tile.shape[0], nx)
     change, cells = jnp.where(lower, mine, theirs), jnp.where(lower, theirs, mine)
     cell = [cells, pltpu.roll(cells, LANES - nx, 1)]
     ratio = jnp.where(lower, pltpu.roll(change, LANES - 3 * nx, 1), 0.0)

time: 21.3 us -> 21.2 us (level)
  no operation moved by 1% of the time
where the time goes in v8:
time: 21.2 us; the launch traced here: 21 us
  starting transfers between devices  9.3 us (44%)
  Pallas kernels  8.82 us (42%)
  waiting for transfers between devices  2.11 us (10%)
  between operations  0.76 us (4%)
    ppermute x6, starting transfers between devices, ring(): return lax.ppermute(x, axis, [(i, (i + by) % peers) for i in range(peers)])  9.3 us
    ppermute x6, waiting for transfers between devices, ring(): return lax.ppermute(x, axis, [(i, (i + by) % peers) for i in range(peers)])  2.11 us
    pallas_call x1, Pallas kernels, first_faces(): call(first_faces_body, 'first_faces', (vmem(2, 2, ny, nz), vmem(2, 2, nx,...  2.07 us
    pallas_call x1, Pallas kernels, store(): call(store_body, 'store', (field,) * 4, (ANY,) * 4, [VMEM] * 6 + [ANY], [...  1.75 us
    pallas_call x1, Pallas kernels, spectra(): call(functools.partial(spectra_body, half, nz), 'spectra', (vmem(7, nx, n...  1.22 us
    pallas_call x1, Pallas kernels, electric(): call(functools.partial(electric_body, half, owned), 'electric', (field, f...  1.06 us
    pallas_call x1, Pallas kernels, gradient(): pl.pallas_call(gradient_body, out_shape=(f32(owned, nx, ny), f32(*efn.sha...  1.01 us
    pallas_call x1, Pallas kernels, magnetic(): call(magnetic_body, 'magnetic', (field, field, vmem(ny, LANES), vmem(ny,...  0.99 us
  transfers between devices with their start and end apart: 6, of which 4 were waited for; matrix products, arithmetic and copies ran while one was open for 0% of the time, Pallas kernels for 22%

profile of v8, /device:TPU:0, one launch (start us, length us, event | category | flops | bytes accessed | tf_op | source)
XLA Modules:
  0.0 21.0 jit_solution(10471405004678709981)
XLA Ops:
  0.6 0.0 slice-start
  0.6 2.1 %first_faces.1 = (f32[2,2,32,128]{3,2,1,0:T(8,128)S(1)}, f32[2,2,16,128]{3,2,1,0:T(8,128)S(1)}, f32[3,16,32,128]{3,2,1,0:T(8,128)S(1)}, f32[3,16,32,128]{3,2,1,0...) custom-call(f32[3,16,32,128]{3,2,1,0:T(8,128)} %ef.1, ...), custom_call_target="tpu_custom_call" | custom-call | flops 3000000 | bytes 3000000 | tf_op jit(solution)/shard_map/first_faces/pallas_call | solution.py:116
  2.7 0.0 copy-start
  2.7 0.0 copy-start.1
  2.7 0.0 copy-start.2
  2.8 2.4 %collective-permute-start = (f32[2,2,32,128]{3,2,1,0:T(8,128)S(1)}, f32[2,2,32,128]{3,2,1,0:T(8,128)S(1)}, u32[]{:S(2)}, u32[]{:S(2)}) collective-permute-start(f32[2,2,32,128]{3,2,1,0:T(8,128)S(1)} %get-tuple-element.42), channel_id=1, source_target_pairs={{0,24},{8,0},{16,8},{24,16},{1,25},{9,1},{17,9},{25,17},{2,26},{10... | collective-permute-start | bytes 196616 | tf_op jit(solution)/shard_map/ppermute | solution.py:34
  5.2 3.6 %collective-permute-start.1 = (f32[2,2,16,128]{3,2,1,0:T(8,128)S(1)}, f32[2,2,16,128]{3,2,1,0:T(8,128)S(1)}, u32[]{:S(2)}, u32[]{:S(2)}) collective-permute-start(f32[2,2,16,128]{3,2,1,0:T(8,128)S(1)} %get-tuple-element.46.first_y), channel_id=1, source_target_pairs={{0,6},{2,0},{4,2},{6,4},{1,7},{3,1},{5,3},{7,5},{8,14},{10,8},{12,... | collective-permute-start | bytes 98312 | tf_op jit(solution)/shard_map/ppermute | solution.py:34
  8.8 0.1 last_y.1.after
  8.9 0.1 collective-permute-start.4
  9.0 1.0 %magnetic.1 = (f32[3,16,32,128]{3,2,1,0:T(8,128)S(1)}, f32[3,16,32,128]{3,2,1,0:T(8,128)S(1)}, f32[32,128]{1,0:T(8,128)S(1)}, f32[32,128]{1,0:T(8,128)S(1)}) custom-call(f32[3,16,32,128]{3,2,1,0:T(8,128)S(1)} %get-tuple-element.38.ef, f32[3,16,32,128]{3,2,1,0:T(8,128)S(1)} %get-tuple-element.39.ea, f32[3,16,32,128]{3,2,1,0:T(8,128)S(1)} %get-tuple-element.40.hf, ...), custom_call_target="tpu_custom_call" | custom-call | flops 4800000 | bytes 4800000 | tf_op jit(solution)/shard_map/magnetic/pallas_call | solution.py:178
  10.0 0.6 %collective-permute-done.1.yr = f32[2,2,16,128]{3,2,1,0:T(8,128)S(1)} collective-permute-done((f32[2,2,16,128]{3,2,1,0:T(8,128)S(1)}, f32[2,2,16,128]{3,2,1,0:T(8,128)S(1)}, u32[]{:S(2)}, u32[]{:S(2)}) %collective-permute-start.1) | collective-permute-done | bytes 32800 | tf_op jit(solution)/shard_map/ppermute | solution.py:34
  10.6 0.2 last_faces.1
  10.8 0.1 collective-permute-start.3
  10.8 1.6 %collective-permute-start.2 = (f32[32,128]{1,0:T(8,128)S(1)}, f32[32,128]{1,0:T(8,128)S(1)}, u32[]{:S(2)}, u32[]{:S(2)}) collective-permute-start(f32[32,128]{1,0:T(8,128)S(1)} %get-tuple-element.52.after), channel_id=1, source_target_pairs={{0,1},{1,0},{2,3},{3,2},{4,5},{5,4},{6,7},{7,6},{8,9},{9,8},{10,11... | collective-permute-start | bytes 49160 | tf_op jit(solution)/shard_map/ppermute | solution.py:34
  12.4 0.0 copy-start.3
  12.5 1.2 %spectra.1 = (f32[7,16,32,128]{3,2,1,0:T(8,128)S(1)}, f32[3,32,128]{2,1,0:T(8,128)S(1)}) custom-call(f32[3,2,3,16,32,48]{5,4,3,2,1,0:T(8,128)S(1)} %bitcast.6, f32[3,2,3,16,32,48]{5,4,3,2,1,0:T(8,128)S(1)} %bitcast.7, f32[1,3]{1,0:T(1,128)S(1)} %bitcast.8, s32[16,32,128]{2,1,0:T(8,128)S(1)} %copy-done.1, f32[32,128]{1,0:T(8,128)S(1)} %get-tuple-element.52.after), custom_call_target="tpu_custom_call" | custom-call | flops 11000000 | bytes 11000000 | tf_op jit(solution)/shard_map/spectra/pallas_call | solution.py:326
  13.7 0.9 %collective-permute-done.2.zr = f32[32,128]{1,0:T(8,128)S(1)} collective-permute-done((f32[32,128]{1,0:T(8,128)S(1)}, f32[32,128]{1,0:T(8,128)S(1)}, u32[]{:S(2)}, u32[]{:S(2)}) %collective-permute-start.2) | collective-permute-done | bytes 16416 | tf_op jit(solution)/shard_map/ppermute | solution.py:34
  14.6 0.4 %complete.1 = (f32[2,16,32,128]{3,2,1,0:T(8,128)S(1)}, f32[2,16,32,128]{3,2,1,0:T(8,128)S(1)}, f32[32,128]{1,0:T(8,128)S(1)}) custom-call(f32[3,16,32,128]{3,2,1,0:T(8,128)S(1)} %get-tuple-element.50.hf.hzf, f32[3,16,32,128]{3,2,1,0:T(8,128)S(1)} %get-tuple-element.51.ha.hza, f32[32,128]{1,0:T(8,128)S(1)} %collective-permute-done.2.zr, ...), custom_call_target="tpu_custom_call" | custom-call | flops 2000000 | bytes 2000000 | tf_op jit(solution)/shard_map/complete/pallas_call | solution.py:352
  15.1 0.1 collective-permute-done.4.yr
  15.1 1.1 %electric.1 = (f32[3,16,32,128]{3,2,1,0:T(8,128)S(1)}, f32[3,16,32,128]{3,2,1,0:T(8,128)S(1)}, f32[32,128]{1,0:T(8,128)S(1)}, f32[40,128]{1,0:T(8,128)S(1)}, f32[32,128]{1,0:T(8,128)S(1)}) custom-call(f32[3,16,32,128]{3,2,1,0:T(8,128)S(1)} %get-tuple-element.38.ef, f32[3,16,32,128]{3,2,1,0:T(8,128)S(1)} %get-tuple-element.39.ea, ...), custom_call_target="tpu_custom_call" | custom-call | flops 6700000 | bytes 6700000 | tf_op jit(solution)/shard_map/electric/pallas_call | solution.py:448
  16.2 1.6 %collective-permute-start.5 = (f32[40,128]{1,0:T(8,128)S(1)}, f32[40,128]{1,0:T(8,128)S(1)}, u32[]{:S(2)}, u32[]{:S(2)}) collective-permute-start(f32[40,128]{1,0:T(8,128)S(1)} %get-tuple-element.63), channel_id=1, source_target_pairs={{0,1},{1,0},{2,3},{3,2},{4,5},{5,4},{6,7},{7,6},{8,9},{9,8},{10,11... | collective-permute-start | bytes 61448 | tf_op jit(solution)/shard_map/ppermute | solution.py:34
  17.8 1.8 %store.1 = (f32[3,16,32,128]{3,2,1,0:T(8,128)}, f32[3,16,32,128]{3,2,1,0:T(8,128)}, f32[3,16,32,128]{3,2,1,0:T(8,128)}, f32[3,16,32,128]{3,2,1,0:T(8,128)}) custom-call(f32[3,16,32,128]{3,2,1,0:T(8,128)S(1)} %get-tuple-element.59.ef, f32[3,16,32,128]{3,2,1,0:T(8,128)S(1)} %get-tuple-element.60.ea, f32[2,16,32,128]{3,2,1,0:T(8,128)S(1)} %get-tuple-element.53.hf, ...), custom_call_target="tpu_custom_call" | custom-call | flops 3000000 | bytes 3000000 | tf_op jit(solution)/shard_map/store/pallas_call | solution.py:472
  19.5 0.5 %collective-permute-done.5.came = f32[40,128]{1,0:T(8,128)S(1)} collective-permute-done((f32[40,128]{1,0:T(8,128)S(1)}, f32[40,128]{1,0:T(8,128)S(1)}, u32[]{:S(2)}, u32[]{:S(2)}) %collective-permute-start.5) | collective-permute-done | bytes 20512 | tf_op jit(solution)/shard_map/ppermute | solution.py:34
  20.0 1.0 %gradient.1 = (f32[8,16,32]{2,1,0:T(8,128)}, f32[3,16,32,128]{3,2,1,0:T(8,128)}, f32[3,16,32,128]{3,2,1,0:T(8,128)}) custom-call(f32[3,16,32,128]{3,2,1,0:T(8,128)S(1)} %get-tuple-element.59.ef, f32[3,16,32,128]{3,2,1,0:T(8,128)S(1)} %get-tuple-element.60.ea, ...), custom_call_target="tpu_custom_call", output_to_operand_aliasing={{1}: (6, {}), {2}: (7, {})} | custom-call | flops 100000 | bytes 400000 | tf_op jit(solution)/shard_map/gradient/pallas_call | solution.py:527
  (10 shorter events, 0.0 us)
Async XLA Ops:
  0.6 11.8 %slice-start = ((s8[4718592]{0:T(1024)(128)(4,1)}), s8[4194304]{0:T(1024)(128)(4,1)S(1)}, s32[]{:S(2)}) async-start(s8[4718592]{0:T(1024)(128)(4,1)} %bitcast.4), calls=%async_computation | async-start | bytes 8388608
  2.7 9.7 %copy-start = (f32[3,2,3,48,16,32]{3,5,4,2,1,0:T(8,128)S(1)}, f32[3,2,3,48,16,32]{3,5,4,2,1,0:T(8,128)}, u32[]{:S(2)}) copy-start(f32[3,2,3,48,16,32]{3,5,4,2,1,0:T(8,128)} %param.15) | copy-start | bytes 5308420
  2.7 9.7 %copy-start.1 = (s32[16,32,128]{2,1,0:T(8,128)S(1)}, s32[16,32,128]{2,1,0:T(8,128)}, u32[]{:S(2)}) copy-start(s32[16,32,128]{2,1,0:T(8,128)} %material.3) | copy-start | bytes 786436
  2.7 9.7 %copy-start.2 = (f32[3]{0:T(128)S(1)}, f32[3]{0:T(128)}, u32[]{:S(2)}) copy-start(f32[3]{0:T(128)} %param.16) | copy-start | bytes 40
  2.8 6.0 %collective-permute-start = (f32[2,2,32,128]{3,2,1,0:T(8,128)S(1)}, f32[2,2,32,128]{3,2,1,0:T(8,128)S(1)}, u32[]{:S(2)}, u32[]{:S(2)}) collective-permute-start(f32[2,2,32,128]{3,2,1,0:T(8,128)S(1)} %get-tuple-element.42), channel_id=1, source_target_pairs={{0,24},{8,0},{16,8},{24,16},{1,25},{9,1},{17,9},{25,17},{2,26},{10... | collective-permute-start | bytes 196616 | tf_op jit(solution)/shard_map/ppermute | solution.py:34
  5.2 5.4 %collective-permute-start.1 = (f32[2,2,16,128]{3,2,1,0:T(8,128)S(1)}, f32[2,2,16,128]{3,2,1,0:T(8,128)S(1)}, u32[]{:S(2)}, u32[]{:S(2)}) collective-permute-start(f32[2,2,16,128]{3,2,1,0:T(8,128)S(1)} %get-tuple-element.46.first_y), channel_id=1, source_target_pairs={{0,6},{2,0},{4,2},{6,4},{1,7},{3,1},{5,3},{7,5},{8,14},{10,8},{12,... | collective-permute-start | bytes 98312 | tf_op jit(solution)/shard_map/ppermute | solution.py:34
  8.8 3.6 %slice-start.1 = ((s8[4718592]{0:T(1024)(128)(4,1)}), s8[524288]{0:T(1024)(128)(4,1)S(1)}, s32[]{:S(2)}) async-start(s8[4718592]{0:T(1024)(128)(4,1)} %bitcast.4), calls=%async_computation.1 | async-start | bytes 1048576
  8.9 6.2 %collective-permute-start.4 = (f32[144,128]{1,0:T(8,128)S(1)}, f32[144,128]{1,0:T(8,128)S(1)}, u32[]{:S(2)}, u32[]{:S(2)}) collective-permute-start(f32[144,128]{1,0:T(8,128)S(1)} %last_y.1.after), channel_id=1, source_target_pairs={{0,2},{2,4},{4,6},{6,0},{1,3},{3,5},{5,7},{7,1},{8,10},{10,12},{12... | collective-permute-start | bytes 221192 | tf_op jit(solution)/shard_map/ppermute | solution.py:34
  10.8 4.3 %collective-permute-start.3 = (f32[136,128]{1,0:T(8,128)S(1)}, f32[136,128]{1,0:T(8,128)S(1)}, u32[]{:S(2)}, u32[]{:S(2)}) collective-permute-start(f32[136,128]{1,0:T(8,128)S(1)} %get-tuple-element.55), channel_id=1, source_target_pairs={{0,8},{8,16},{16,24},{24,0},{1,9},{9,17},{17,25},{25,1},{2,10},{10... | collective-permute-start | bytes 208904 | tf_op jit(solution)/shard_map/ppermute | solution.py:34
  10.8 3.8 %collective-permute-start.2 = (f32[32,128]{1,0:T(8,128)S(1)}, f32[32,128]{1,0:T(8,128)S(1)}, u32[]{:S(2)}, u32[]{:S(2)}) collective-permute-start(f32[32,128]{1,0:T(8,128)S(1)} %get-tuple-element.52.after), channel_id=1, source_target_pairs={{0,1},{1,0},{2,3},{3,2},{4,5},{5,4},{6,7},{7,6},{8,9},{9,8},{10,11... | collective-permute-start | bytes 49160 | tf_op jit(solution)/shard_map/ppermute | solution.py:34
  12.4 2.7 %copy-start.3 = (s32[96]{0:T(128)S(1)}, s32[96]{0:T(128)}, u32[]{:S(2)}) copy-start(s32[96]{0:T(128)} %param.17) | copy-start | bytes 1156
  16.2 3.8 %collective-permute-start.5 = (f32[40,128]{1,0:T(8,128)S(1)}, f32[40,128]{1,0:T(8,128)S(1)}, u32[]{:S(2)}, u32[]{:S(2)}) collective-permute-start(f32[40,128]{1,0:T(8,128)S(1)} %get-tuple-element.63), channel_id=1, source_target_pairs={{0,1},{1,0},{2,3},{3,2},{4,5},{5,4},{6,7},{7,6},{8,9},{9,8},{10,11... | collective-permute-start | bytes 61448 | tf_op jit(solution)/shard_map/ppermute | solution.py:34

commit v9 on v8

--- a/solution.py
+++ b/solution.py
@@ -204,8 +204,8 @@
         xs[at + 2 * ny - 8 : at + 2 * ny, :] = hz
     xs[4 * ny :, :] = along_x[...]
     lower = lax.axis_index("gz") == 0
-    zs[...] = jnp.where(lower, top[...], layer[...])
-    zs[last, :] = jnp.where(lower, rows, layer[last, :])
+    sent = jnp.where(lower, jnp.concatenate([top[0 : ny - 8, :], rows], axis=0), layer[...])
+    zs[...] = sent[0 : ny // 2] + pltpu.roll(sent[ny // 2 :], 4 * nx, 1)
 
 
 def last_faces(hf, ha, yr, along_x, layer, top):
@@ -213,7 +213,7 @@
     field = vmem(3, nx, ny, nz)
     return pl.pallas_call(
         last_faces_body,
-        out_shape=(field, field, vmem(4 * ny + 8, nz), vmem(ny, LANES)),
+        out_shape=(field, field, vmem(4 * ny + 8, nz), vmem(ny // 2, LANES)),
         in_specs=[VMEM] * 6,
         out_specs=(VMEM,) * 4,
         input_output_aliases={0: 0, 1: 1},
@@ -336,7 +336,8 @@
 def complete_body(hf, ha, zr, layer, hfn, han, below):
     _, nx, ny, nz = hf.shape
     lower = lax.axis_index("gz") == 0
-    came = zr[...]
+    came = jnp.concatenate([zr[...], pltpu.roll(zr[...], LANES - 4 * nx, 1)], axis=0)
+    came = jnp.where(lane_ids(ny) < 4 * nx, came, 0.0)
     above = jnp.where(lower, from_layer_above(came, nx), 0.0)
     below[...] = jnp.where(lower, 0.0, came + from_layer_above(layer[...], nx))
     top = lane_ids(ny) == nz - 1

time: 21.2 us -> 21.3 us (level)
  no operation moved by 1% of the time
where the time goes in v9:
time: 21.3 us; the launch traced here: 21.1 us
  starting transfers between devices  9.25 us (43%)
  Pallas kernels  8.95 us (42%)
  waiting for transfers between devices  2.11 us (10%)
  between operations  0.76 us (4%)
    ppermute x6, starting transfers between devices, ring(): return lax.ppermute(x, axis, [(i, (i + by) % peers) for i in range(peers)])  9.25 us
    ppermute x6, waiting for transfers between devices, ring(): return lax.ppermute(x, axis, [(i, (i + by) % peers) for i in range(peers)])  2.11 us
    pallas_call x1, Pallas kernels, first_faces(): call(first_faces_body, 'first_faces', (vmem(2, 2, ny, nz), vmem(2, 2, nx,...  2.07 us
    pallas_call x1, Pallas kernels, store(): call(store_body, 'store', (field,) * 4, (ANY,) * 4, [VMEM] * 6 + [ANY], [...  1.75 us
    pallas_call x1, Pallas kernels, spectra(): call(functools.partial(spectra_body, half, nz), 'spectra', (vmem(7, nx, n...  1.23 us
    pallas_call x1, Pallas kernels, electric(): call(functools.partial(electric_body, half, owned), 'electric', (field, f...  1.12 us
    pallas_call x1, Pallas kernels, gradient(): pl.pallas_call(gradient_body, out_shape=(f32(owned, nx, ny), f32(*efn.sha...  1.01 us
    pallas_call x1, Pallas kernels, magnetic(): call(magnetic_body, 'magnetic', (field, field, vmem(ny, LANES), vmem(ny,...  0.98 us
  transfers between devices with their start and end apart: 6, of which 4 were waited for; matrix products, arithmetic and copies ran while one was open for 0% of the time, Pallas kernels for 22%

profile of v9, /device:TPU:0, one launch (start us, length us, event | category | flops | bytes accessed | tf_op | source)
XLA Modules:
  0.0 21.1 jit_solution(322115524846365356)
XLA Ops:
  0.6 0.0 slice-start
  0.6 2.1 %first_faces.1 = (f32[2,2,32,128]{3,2,1,0:T(8,128)S(1)}, f32[2,2,16,128]{3,2,1,0:T(8,128)S(1)}, f32[3,16,32,128]{3,2,1,0:T(8,128)S(1)}, f32[3,16,32,128]{3,2,1,0...) custom-call(f32[3,16,32,128]{3,2,1,0:T(8,128)} %ef.1, ...), custom_call_target="tpu_custom_call" | custom-call | flops 3000000 | bytes 3000000 | tf_op jit(solution)/shard_map/first_faces/pallas_call | solution.py:116
  2.7 0.0 copy-start
  2.7 0.0 copy-start.1
  2.7 0.0 copy-start.2
  2.8 2.4 %collective-permute-start = (f32[2,2,32,128]{3,2,1,0:T(8,128)S(1)}, f32[2,2,32,128]{3,2,1,0:T(8,128)S(1)}, u32[]{:S(2)}, u32[]{:S(2)}) collective-permute-start(f32[2,2,32,128]{3,2,1,0:T(8,128)S(1)} %get-tuple-element.42), channel_id=1, source_target_pairs={{0,24},{8,0},{16,8},{24,16},{1,25},{9,1},{17,9},{25,17},{2,26},{10... | collective-permute-start | bytes 196616 | tf_op jit(solution)/shard_map/ppermute | solution.py:34
  5.2 3.6 %collective-permute-start.1 = (f32[2,2,16,128]{3,2,1,0:T(8,128)S(1)}, f32[2,2,16,128]{3,2,1,0:T(8,128)S(1)}, u32[]{:S(2)}, u32[]{:S(2)}) collective-permute-start(f32[2,2,16,128]{3,2,1,0:T(8,128)S(1)} %get-tuple-element.46.first_y), channel_id=1, source_target_pairs={{0,6},{2,0},{4,2},{6,4},{1,7},{3,1},{5,3},{7,5},{8,14},{10,8},{12,... | collective-permute-start | bytes 98312 | tf_op jit(solution)/shard_map/ppermute | solution.py:34
  8.8 0.1 last_y.1.after
  8.9 0.1 collective-permute-start.4
  9.0 1.0 %magnetic.1 = (f32[3,16,32,128]{3,2,1,0:T(8,128)S(1)}, f32[3,16,32,128]{3,2,1,0:T(8,128)S(1)}, f32[32,128]{1,0:T(8,128)S(1)}, f32[32,128]{1,0:T(8,128)S(1)}) custom-call(f32[3,16,32,128]{3,2,1,0:T(8,128)S(1)} %get-tuple-element.38.ef, f32[3,16,32,128]{3,2,1,0:T(8,128)S(1)} %get-tuple-element.39.ea, f32[3,16,32,128]{3,2,1,0:T(8,128)S(1)} %get-tuple-element.40.hf, ...), custom_call_target="tpu_custom_call" | custom-call | flops 4800000 | bytes 4800000 | tf_op jit(solution)/shard_map/magnetic/pallas_call | solution.py:178
  10.0 0.6 %collective-permute-done.1.yr = f32[2,2,16,128]{3,2,1,0:T(8,128)S(1)} collective-permute-done((f32[2,2,16,128]{3,2,1,0:T(8,128)S(1)}, f32[2,2,16,128]{3,2,1,0:T(8,128)S(1)}, u32[]{:S(2)}, u32[]{:S(2)}) %collective-permute-start.1) | collective-permute-done | bytes 32800 | tf_op jit(solution)/shard_map/ppermute | solution.py:34
  10.6 0.3 %last_faces.1 = (f32[3,16,32,128]{3,2,1,0:T(8,128)S(1)}, f32[3,16,32,128]{3,2,1,0:T(8,128)S(1)}, f32[136,128]{1,0:T(8,128)S(1)}, f32[16,128]{1,0:T(8,128)S(1)}) custom-call(f32[3,16,32,128]{3,2,1,0:T(8,128)S(1)} %get-tuple-element.44.hf, f32[3,16,32,128]{3,2,1,0:T(8,128)S(1)} %get-tuple-element.45.ha, ...), custom_call_target="tpu_custom_call", output_to_operand_aliasing={{0}: (0, {}), {1}: (1, {})} | custom-call | flops 500000 | bytes 500000 | tf_op jit(solution)/shard_map/last_faces/pallas_call | solution.py:214
  10.8 0.0 collective-permute-start.3
  10.8 1.6 %collective-permute-start.2 = (f32[16,128]{1,0:T(8,128)S(1)}, f32[16,128]{1,0:T(8,128)S(1)}, u32[]{:S(2)}, u32[]{:S(2)}) collective-permute-start(f32[16,128]{1,0:T(8,128)S(1)} %get-tuple-element.52.after), channel_id=1, source_target_pairs={{0,1},{1,0},{2,3},{3,2},{4,5},{5,4},{6,7},{7,6},{8,9},{9,8},{10,11... | collective-permute-start | bytes 24584 | tf_op jit(solution)/shard_map/ppermute | solution.py:34
  12.4 0.0 copy-start.3
  12.5 1.2 %spectra.1 = (f32[7,16,32,128]{3,2,1,0:T(8,128)S(1)}, f32[3,32,128]{2,1,0:T(8,128)S(1)}) custom-call(f32[3,2,3,16,32,48]{5,4,3,2,1,0:T(8,128)S(1)} %bitcast.6, f32[3,2,3,16,32,48]{5,4,3,2,1,0:T(8,128)S(1)} %bitcast.7, f32[1,3]{1,0:T(1,128)S(1)} %bitcast.8, s32[16,32,128]{2,1,0:T(8,128)S(1)} %copy-done.1, f32[16,128]{1,0:T(8,128)S(1)} %get-tuple-element.52.after), custom_call_target="tpu_custom_call" | custom-call | flops 11000000 | bytes 11000000 | tf_op jit(solution)/shard_map/spectra/pallas_call | solution.py:326
  13.7 0.9 %collective-permute-done.2.zr = f32[16,128]{1,0:T(8,128)S(1)} collective-permute-done((f32[16,128]{1,0:T(8,128)S(1)}, f32[16,128]{1,0:T(8,128)S(1)}, u32[]{:S(2)}, u32[]{:S(2)}) %collective-permute-start.2) | collective-permute-done | bytes 8224 | tf_op jit(solution)/shard_map/ppermute | solution.py:34
  14.6 0.4 %complete.1 = (f32[2,16,32,128]{3,2,1,0:T(8,128)S(1)}, f32[2,16,32,128]{3,2,1,0:T(8,128)S(1)}, f32[32,128]{1,0:T(8,128)S(1)}) custom-call(f32[3,16,32,128]{3,2,1,0:T(8,128)S(1)} %get-tuple-element.50.hf.hzf, f32[3,16,32,128]{3,2,1,0:T(8,128)S(1)} %get-tuple-element.51.ha.hza, f32[16,128]{1,0:T(8,128)S(1)} %collective-permute-done.2.zr, ...), custom_call_target="tpu_custom_call" | custom-call | flops 2000000 | bytes 2000000 | tf_op jit(solution)/shard_map/complete/pallas_call | solution.py:353
  15.0 0.1 collective-permute-done.4.yr
  15.1 1.1 %electric.1 = (f32[3,16,32,128]{3,2,1,0:T(8,128)S(1)}, f32[3,16,32,128]{3,2,1,0:T(8,128)S(1)}, f32[32,128]{1,0:T(8,128)S(1)}, f32[40,128]{1,0:T(8,128)S(1)}, f32[32,128]{1,0:T(8,128)S(1)}) custom-call(f32[3,16,32,128]{3,2,1,0:T(8,128)S(1)} %get-tuple-element.38.ef, f32[3,16,32,128]{3,2,1,0:T(8,128)S(1)} %get-tuple-element.39.ea, ...), custom_call_target="tpu_custom_call" | custom-call | flops 6700000 | bytes 6700000 | tf_op jit(solution)/shard_map/electric/pallas_call | solution.py:449
  16.3 1.6 %collective-permute-start.5 = (f32[40,128]{1,0:T(8,128)S(1)}, f32[40,128]{1,0:T(8,128)S(1)}, u32[]{:S(2)}, u32[]{:S(2)}) collective-permute-start(f32[40,128]{1,0:T(8,128)S(1)} %get-tuple-element.63), channel_id=1, source_target_pairs={{0,1},{1,0},{2,3},{3,2},{4,5},{5,4},{6,7},{7,6},{8,9},{9,8},{10,11... | collective-permute-start | bytes 61448 | tf_op jit(solution)/shard_map/ppermute | solution.py:34
  17.8 1.8 %store.1 = (f32[3,16,32,128]{3,2,1,0:T(8,128)}, f32[3,16,32,128]{3,2,1,0:T(8,128)}, f32[3,16,32,128]{3,2,1,0:T(8,128)}, f32[3,16,32,128]{3,2,1,0:T(8,128)}) custom-call(f32[3,16,32,128]{3,2,1,0:T(8,128)S(1)} %get-tuple-element.59.ef, f32[3,16,32,128]{3,2,1,0:T(8,128)S(1)} %get-tuple-element.60.ea, f32[2,16,32,128]{3,2,1,0:T(8,128)S(1)} %get-tuple-element.53.hf, ...), custom_call_target="tpu_custom_call" | custom-call | flops 3000000 | bytes 3000000 | tf_op jit(solution)/shard_map/store/pallas_call | solution.py:473
  19.6 0.5 %collective-permute-done.5.came = f32[40,128]{1,0:T(8,128)S(1)} collective-permute-done((f32[40,128]{1,0:T(8,128)S(1)}, f32[40,128]{1,0:T(8,128)S(1)}, u32[]{:S(2)}, u32[]{:S(2)}) %collective-permute-start.5) | collective-permute-done | bytes 20512 | tf_op jit(solution)/shard_map/ppermute | solution.py:34
  20.1 1.0 %gradient.1 = (f32[8,16,32]{2,1,0:T(8,128)}, f32[3,16,32,128]{3,2,1,0:T(8,128)}, f32[3,16,32,128]{3,2,1,0:T(8,128)}) custom-call(f32[3,16,32,128]{3,2,1,0:T(8,128)S(1)} %get-tuple-element.59.ef, f32[3,16,32,128]{3,2,1,0:T(8,128)S(1)} %get-tuple-element.60.ea, ...), custom_call_target="tpu_custom_call", output_to_operand_aliasing={{1}: (6, {}), {2}: (7, {})} | custom-call | flops 100000 | bytes 400000 | tf_op jit(solution)/shard_map/gradient/pallas_call | solution.py:528
  (10 shorter events, 0.0 us)
Async XLA Ops:
  0.6 11.8 %slice-start = ((s8[4718592]{0:T(1024)(128)(4,1)}), s8[4194304]{0:T(1024)(128)(4,1)S(1)}, s32[]{:S(2)}) async-start(s8[4718592]{0:T(1024)(128)(4,1)} %bitcast.4), calls=%async_computation | async-start | bytes 8388608
  2.7 9.7 %copy-start = (f32[3,2,3,48,16,32]{3,5,4,2,1,0:T(8,128)S(1)}, f32[3,2,3,48,16,32]{3,5,4,2,1,0:T(8,128)}, u32[]{:S(2)}) copy-start(f32[3,2,3,48,16,32]{3,5,4,2,1,0:T(8,128)} %param.15) | copy-start | bytes 5308420
  2.7 9.7 %copy-start.1 = (s32[16,32,128]{2,1,0:T(8,128)S(1)}, s32[16,32,128]{2,1,0:T(8,128)}, u32[]{:S(2)}) copy-start(s32[16,32,128]{2,1,0:T(8,128)} %material.3) | copy-start | bytes 786436
  2.7 9.7 %copy-start.2 = (f32[3]{0:T(128)S(1)}, f32[3]{0:T(128)}, u32[]{:S(2)}) copy-start(f32[3]{0:T(128)} %param.16) | copy-start | bytes 40
  2.8 6.0 %collective-permute-start = (f32[2,2,32,128]{3,2,1,0:T(8,128)S(1)}, f32[2,2,32,128]{3,2,1,0:T(8,128)S(1)}, u32[]{:S(2)}, u32[]{:S(2)}) collective-permute-start(f32[2,2,32,128]{3,2,1,0:T(8,128)S(1)} %get-tuple-element.42), channel_id=1, source_target_pairs={{0,24},{8,0},{16,8},{24,16},{1,25},{9,1},{17,9},{25,17},{2,26},{10... | collective-permute-start | bytes 196616 | tf_op jit(solution)/shard_map/ppermute | solution.py:34
  5.2 5.4 %collective-permute-start.1 = (f32[2,2,16,128]{3,2,1,0:T(8,128)S(1)}, f32[2,2,16,128]{3,2,1,0:T(8,128)S(1)}, u32[]{:S(2)}, u32[]{:S(2)}) collective-permute-start(f32[2,2,16,128]{3,2,1,0:T(8,128)S(1)} %get-tuple-element.46.first_y), channel_id=1, source_target_pairs={{0,6},{2,0},{4,2},{6,4},{1,7},{3,1},{5,3},{7,5},{8,14},{10,8},{12,... | collective-permute-start | bytes 98312 | tf_op jit(solution)/shard_map/ppermute | solution.py:34
  8.8 3.6 %slice-start.1 = ((s8[4718592]{0:T(1024)(128)(4,1)}), s8[524288]{0:T(1024)(128)(4,1)S(1)}, s32[]{:S(2)}) async-start(s8[4718592]{0:T(1024)(128)(4,1)} %bitcast.4), calls=%async_computation.1 | async-start | bytes 1048576
  8.9 6.2 %collective-permute-start.4 = (f32[144,128]{1,0:T(8,128)S(1)}, f32[144,128]{1,0:T(8,128)S(1)}, u32[]{:S(2)}, u32[]{:S(2)}) collective-permute-start(f32[144,128]{1,0:T(8,128)S(1)} %last_y.1.after), channel_id=1, source_target_pairs={{0,2},{2,4},{4,6},{6,0},{1,3},{3,5},{5,7},{7,1},{8,10},{10,12},{12... | collective-permute-start | bytes 221192 | tf_op jit(solution)/shard_map/ppermute | solution.py:34
  10.8 4.1 %collective-permute-start.3 = (f32[136,128]{1,0:T(8,128)S(1)}, f32[136,128]{1,0:T(8,128)S(1)}, u32[]{:S(2)}, u32[]{:S(2)}) collective-permute-start(f32[136,128]{1,0:T(8,128)S(1)} %get-tuple-element.55), channel_id=1, source_target_pairs={{0,8},{8,16},{16,24},{24,0},{1,9},{9,17},{17,25},{25,1},{2,10},{10... | collective-permute-start | bytes 208904 | tf_op jit(solution)/shard_map/ppermute | solution.py:34
  10.8 3.7 %collective-permute-start.2 = (f32[16,128]{1,0:T(8,128)S(1)}, f32[16,128]{1,0:T(8,128)S(1)}, u32[]{:S(2)}, u32[]{:S(2)}) collective-permute-start(f32[16,128]{1,0:T(8,128)S(1)} %get-tuple-element.52.after), channel_id=1, source_target_pairs={{0,1},{1,0},{2,3},{3,2},{4,5},{5,4},{6,7},{7,6},{8,9},{9,8},{10,11... | collective-permute-start | bytes 24584 | tf_op jit(solution)/shard_map/ppermute | solution.py:34
  12.4 2.7 %copy-start.3 = (s32[96]{0:T(128)S(1)}, s32[96]{0:T(128)}, u32[]{:S(2)}) copy-start(s32[96]{0:T(128)} %param.17) | copy-start | bytes 1156
  16.3 3.8 %collective-permute-start.5 = (f32[40,128]{1,0:T(8,128)S(1)}, f32[40,128]{1,0:T(8,128)S(1)}, u32[]{:S(2)}, u32[]{:S(2)}) collective-permute-start(f32[40,128]{1,0:T(8,128)S(1)} %get-tuple-element.63), channel_id=1, source_target_pairs={{0,1},{1,0},{2,3},{3,2},{4,5},{5,4},{6,7},{7,6},{8,9},{9,8},{10,11... | collective-permute-start | bytes 61448 | tf_op jit(solution)/shard_map/ppermute | solution.py:34

commit v10 on v6

--- a/solution.py
+++ b/solution.py
@@ -396,7 +396,7 @@
             block = jnp.concatenate(products, axis=0)
             products = []
             sums = jnp.zeros((2 * owned, group * ny), jnp.float32)
-            for _ in range(3):
+            for _ in range(2):
                 part = block.astype(jnp.bfloat16)
                 block = block - part.astype(jnp.float32)
                 sums = sums + lax.dot_general(hot, part, dims, preferred_element_type=jnp.float32)

time: 21.3 us -> 21.3 us (level)
  no operation moved by 1% of the time
where the time goes in v10:
time: 21.3 us; the launch traced here: 21.1 us
  starting transfers between devices  9.28 us (44%)
  Pallas kernels  8.79 us (41%)
  waiting for transfers between devices  2.24 us (11%)
  between operations  0.76 us (4%)
    ppermute x6, starting transfers between devices, ring(): return lax.ppermute(x, axis, [(i, (i + by) % peers) for i in range(peers)])  9.28 us
    ppermute x6, waiting for transfers between devices, ring(): return lax.ppermute(x, axis, [(i, (i + by) % peers) for i in range(peers)])  2.24 us
    pallas_call x1, Pallas kernels, first_faces(): call(first_faces_body, 'first_faces', (vmem(2, 2, ny, nz), vmem(2, 2, nx,...  2.07 us
    pallas_call x1, Pallas kernels, store(): call(store_body, 'store', (field,) * 4, (ANY,) * 4, [VMEM] * 6 + [ANY], [...  1.75 us
    pallas_call x1, Pallas kernels, spectra(): call(functools.partial(spectra_body, half, nz), 'spectra', (vmem(7, nx, n...  1.22 us
    pallas_call x1, Pallas kernels, gradient(): pl.pallas_call(gradient_body, out_shape=(f32(owned, nx, ny), f32(*efn.sha...  1.01 us
    pallas_call x1, Pallas kernels, electric(): call(functools.partial(electric_body, half, owned), 'electric', (field, f...  1.01 us
    pallas_call x1, Pallas kernels, magnetic(): call(magnetic_body, 'magnetic', (field, field, vmem(ny, LANES), vmem(ny,...  0.99 us
  transfers between devices with their start and end apart: 6, of which 4 were waited for; matrix products, arithmetic and copies ran while one was open for 0% of the time, Pallas kernels for 22%

profile of v10, /device:TPU:0, one launch (start us, length us, event | category | flops | bytes accessed | tf_op | source)
XLA Modules:
  0.0 21.1 jit_solution(17185715739780185299)
XLA Ops:
  0.6 0.0 slice-start
  0.6 2.1 %first_faces.1 = (f32[2,2,32,128]{3,2,1,0:T(8,128)S(1)}, f32[2,2,16,128]{3,2,1,0:T(8,128)S(1)}, f32[3,16,32,128]{3,2,1,0:T(8,128)S(1)}, f32[3,16,32,128]{3,2,1,0...) custom-call(f32[3,16,32,128]{3,2,1,0:T(8,128)} %ef.1, ...), custom_call_target="tpu_custom_call" | custom-call | flops 3000000 | bytes 3000000 | tf_op jit(solution)/shard_map/first_faces/pallas_call | solution.py:116
  2.7 0.0 copy-start
  2.7 0.0 copy-start.1
  2.7 0.0 copy-start.2
  2.8 2.4 %collective-permute-start = (f32[2,2,32,128]{3,2,1,0:T(8,128)S(1)}, f32[2,2,32,128]{3,2,1,0:T(8,128)S(1)}, u32[]{:S(2)}, u32[]{:S(2)}) collective-permute-start(f32[2,2,32,128]{3,2,1,0:T(8,128)S(1)} %get-tuple-element.42), channel_id=1, source_target_pairs={{0,24},{8,0},{16,8},{24,16},{1,25},{9,1},{17,9},{25,17},{2,26},{10... | collective-permute-start | bytes 196616 | tf_op jit(solution)/shard_map/ppermute | solution.py:34
  5.2 3.6 %collective-permute-start.1 = (f32[2,2,16,128]{3,2,1,0:T(8,128)S(1)}, f32[2,2,16,128]{3,2,1,0:T(8,128)S(1)}, u32[]{:S(2)}, u32[]{:S(2)}) collective-permute-start(f32[2,2,16,128]{3,2,1,0:T(8,128)S(1)} %get-tuple-element.46.first_y), channel_id=1, source_target_pairs={{0,6},{2,0},{4,2},{6,4},{1,7},{3,1},{5,3},{7,5},{8,14},{10,8},{12,... | collective-permute-start | bytes 98312 | tf_op jit(solution)/shard_map/ppermute | solution.py:34
  8.8 0.1 last_y.1.after
  8.9 0.1 collective-permute-start.4
  9.0 1.0 %magnetic.1 = (f32[3,16,32,128]{3,2,1,0:T(8,128)S(1)}, f32[3,16,32,128]{3,2,1,0:T(8,128)S(1)}, f32[32,128]{1,0:T(8,128)S(1)}, f32[32,128]{1,0:T(8,128)S(1)}) custom-call(f32[3,16,32,128]{3,2,1,0:T(8,128)S(1)} %get-tuple-element.38.ef, f32[3,16,32,128]{3,2,1,0:T(8,128)S(1)} %get-tuple-element.39.ea, f32[3,16,32,128]{3,2,1,0:T(8,128)S(1)} %get-tuple-element.40.hf, ...), custom_call_target="tpu_custom_call" | custom-call | flops 4800000 | bytes 4800000 | tf_op jit(solution)/shard_map/magnetic/pallas_call | solution.py:177
  10.0 0.6 %collective-permute-done.1.yr = f32[2,2,16,128]{3,2,1,0:T(8,128)S(1)} collective-permute-done((f32[2,2,16,128]{3,2,1,0:T(8,128)S(1)}, f32[2,2,16,128]{3,2,1,0:T(8,128)S(1)}, u32[]{:S(2)}, u32[]{:S(2)}) %collective-permute-start.1) | collective-permute-done | bytes 32800 | tf_op jit(solution)/shard_map/ppermute | solution.py:34
  10.6 0.2 last_faces.1
  10.8 0.1 collective-permute-start.3
  10.8 1.6 %collective-permute-start.2 = (f32[32,128]{1,0:T(8,128)S(1)}, f32[32,128]{1,0:T(8,128)S(1)}, u32[]{:S(2)}, u32[]{:S(2)}) collective-permute-start(f32[32,128]{1,0:T(8,128)S(1)} %get-tuple-element.52.after), channel_id=1, source_target_pairs={{0,1},{1,0},{2,3},{3,2},{4,5},{5,4},{6,7},{7,6},{8,9},{9,8},{10,11... | collective-permute-start | bytes 49160 | tf_op jit(solution)/shard_map/ppermute | solution.py:34
  12.4 0.0 copy-start.3
  12.5 1.2 %spectra.1 = (f32[7,16,32,128]{3,2,1,0:T(8,128)S(1)}, f32[3,32,128]{2,1,0:T(8,128)S(1)}) custom-call(f32[3,2,3,16,32,48]{5,4,3,2,1,0:T(8,128)S(1)} %bitcast.6, f32[3,2,3,16,32,48]{5,4,3,2,1,0:T(8,128)S(1)} %bitcast.7, f32[1,3]{1,0:T(1,128)S(1)} %bitcast.8, s32[16,32,128]{2,1,0:T(8,128)S(1)} %copy-done.1, f32[32,128]{1,0:T(8,128)S(1)} %get-tuple-element.52.after), custom_call_target="tpu_custom_call" | custom-call | flops 11000000 | bytes 11000000 | tf_op jit(solution)/shard_map/spectra/pallas_call | solution.py:307
  13.7 0.9 %collective-permute-done.2.zr = f32[32,128]{1,0:T(8,128)S(1)} collective-permute-done((f32[32,128]{1,0:T(8,128)S(1)}, f32[32,128]{1,0:T(8,128)S(1)}, u32[]{:S(2)}, u32[]{:S(2)}) %collective-permute-start.2) | collective-permute-done | bytes 16416 | tf_op jit(solution)/shard_map/ppermute | solution.py:34
  14.6 0.4 %complete.1 = (f32[2,16,32,128]{3,2,1,0:T(8,128)S(1)}, f32[2,16,32,128]{3,2,1,0:T(8,128)S(1)}, f32[32,128]{1,0:T(8,128)S(1)}) custom-call(f32[3,16,32,128]{3,2,1,0:T(8,128)S(1)} %get-tuple-element.50.hf.hzf, f32[3,16,32,128]{3,2,1,0:T(8,128)S(1)} %get-tuple-element.51.ha.hza, f32[32,128]{1,0:T(8,128)S(1)} %collective-permute-done.2.zr, ...), custom_call_target="tpu_custom_call" | custom-call | flops 2000000 | bytes 2000000 | tf_op jit(solution)/shard_map/complete/pallas_call | solution.py:333
  15.1 0.1 collective-permute-done.4.yr
  15.1 1.0 %electric.1 = (f32[3,16,32,128]{3,2,1,0:T(8,128)S(1)}, f32[3,16,32,128]{3,2,1,0:T(8,128)S(1)}, f32[32,128]{1,0:T(8,128)S(1)}, f32[64,128]{1,0:T(8,128)S(1)}, f32[32,128]{1,0:T(8,128)S(1)}) custom-call(f32[3,16,32,128]{3,2,1,0:T(8,128)S(1)} %get-tuple-element.38.ef, f32[3,16,32,128]{3,2,1,0:T(8,128)S(1)} %get-tuple-element.39.ea, ...), custom_call_target="tpu_custom_call" | custom-call | flops 6700000 | bytes 6700000 | tf_op jit(solution)/shard_map/electric/pallas_call | solution.py:429
  16.1 1.5 %collective-permute-start.5 = (f32[64,128]{1,0:T(8,128)S(1)}, f32[64,128]{1,0:T(8,128)S(1)}, u32[]{:S(2)}, u32[]{:S(2)}) collective-permute-start(f32[64,128]{1,0:T(8,128)S(1)} %get-tuple-element.63), channel_id=1, source_target_pairs={{0,1},{1,0},{2,3},{3,2},{4,5},{5,4},{6,7},{7,6},{8,9},{9,8},{10,11... | collective-permute-start | bytes 98312 | tf_op jit(solution)/shard_map/ppermute | solution.py:34
  17.7 1.8 %store.1 = (f32[3,16,32,128]{3,2,1,0:T(8,128)}, f32[3,16,32,128]{3,2,1,0:T(8,128)}, f32[3,16,32,128]{3,2,1,0:T(8,128)}, f32[3,16,32,128]{3,2,1,0:T(8,128)}) custom-call(f32[3,16,32,128]{3,2,1,0:T(8,128)S(1)} %get-tuple-element.59.ef, f32[3,16,32,128]{3,2,1,0:T(8,128)S(1)} %get-tuple-element.60.ea, f32[2,16,32,128]{3,2,1,0:T(8,128)S(1)} %get-tuple-element.53.hf, ...), custom_call_target="tpu_custom_call" | custom-call | flops 3000000 | bytes 3000000 | tf_op jit(solution)/shard_map/store/pallas_call | solution.py:453
  19.5 0.6 %collective-permute-done.5.came = f32[64,128]{1,0:T(8,128)S(1)} collective-permute-done((f32[64,128]{1,0:T(8,128)S(1)}, f32[64,128]{1,0:T(8,128)S(1)}, u32[]{:S(2)}, u32[]{:S(2)}) %collective-permute-start.5) | collective-permute-done | bytes 32800 | tf_op jit(solution)/shard_map/ppermute | solution.py:34
  20.1 1.0 %gradient.1 = (f32[8,16,32]{2,1,0:T(8,128)}, f32[3,16,32,128]{3,2,1,0:T(8,128)}, f32[3,16,32,128]{3,2,1,0:T(8,128)}) custom-call(f32[3,16,32,128]{3,2,1,0:T(8,128)S(1)} %get-tuple-element.59.ef, f32[3,16,32,128]{3,2,1,0:T(8,128)S(1)} %get-tuple-element.60.ea, ...), custom_call_target="tpu_custom_call", output_to_operand_aliasing={{1}: (6, {}), {2}: (7, {})} | custom-call | flops 100000 | bytes 400000 | tf_op jit(solution)/shard_map/gradient/pallas_call | solution.py:508
  (10 shorter events, 0.0 us)
Async XLA Ops:
  0.6 11.8 %slice-start = ((s8[4718592]{0:T(1024)(128)(4,1)}), s8[4194304]{0:T(1024)(128)(4,1)S(1)}, s32[]{:S(2)}) async-start(s8[4718592]{0:T(1024)(128)(4,1)} %bitcast.4), calls=%async_computation | async-start | bytes 8388608
  2.7 9.7 %copy-start = (f32[3,2,3,48,16,32]{3,5,4,2,1,0:T(8,128)S(1)}, f32[3,2,3,48,16,32]{3,5,4,2,1,0:T(8,128)}, u32[]{:S(2)}) copy-start(f32[3,2,3,48,16,32]{3,5,4,2,1,0:T(8,128)} %param.15) | copy-start | bytes 5308420
  2.7 9.7 %copy-start.1 = (s32[16,32,128]{2,1,0:T(8,128)S(1)}, s32[16,32,128]{2,1,0:T(8,128)}, u32[]{:S(2)}) copy-start(s32[16,32,128]{2,1,0:T(8,128)} %material.3) | copy-start | bytes 786436
  2.7 9.7 %copy-start.2 = (f32[3]{0:T(128)S(1)}, f32[3]{0:T(128)}, u32[]{:S(2)}) copy-start(f32[3]{0:T(128)} %param.16) | copy-start | bytes 40
  2.8 6.0 %collective-permute-start = (f32[2,2,32,128]{3,2,1,0:T(8,128)S(1)}, f32[2,2,32,128]{3,2,1,0:T(8,128)S(1)}, u32[]{:S(2)}, u32[]{:S(2)}) collective-permute-start(f32[2,2,32,128]{3,2,1,0:T(8,128)S(1)} %get-tuple-element.42), channel_id=1, source_target_pairs={{0,24},{8,0},{16,8},{24,16},{1,25},{9,1},{17,9},{25,17},{2,26},{10... | collective-permute-start | bytes 196616 | tf_op jit(solution)/shard_map/ppermute | solution.py:34
  5.2 5.4 %collective-permute-start.1 = (f32[2,2,16,128]{3,2,1,0:T(8,128)S(1)}, f32[2,2,16,128]{3,2,1,0:T(8,128)S(1)}, u32[]{:S(2)}, u32[]{:S(2)}) collective-permute-start(f32[2,2,16,128]{3,2,1,0:T(8,128)S(1)} %get-tuple-element.46.first_y), channel_id=1, source_target_pairs={{0,6},{2,0},{4,2},{6,4},{1,7},{3,1},{5,3},{7,5},{8,14},{10,8},{12,... | collective-permute-start | bytes 98312 | tf_op jit(solution)/shard_map/ppermute | solution.py:34
  8.8 3.6 %slice-start.1 = ((s8[4718592]{0:T(1024)(128)(4,1)}), s8[524288]{0:T(1024)(128)(4,1)S(1)}, s32[]{:S(2)}) async-start(s8[4718592]{0:T(1024)(128)(4,1)} %bitcast.4), calls=%async_computation.1 | async-start | bytes 1048576
  8.9 6.2 %collective-permute-start.4 = (f32[144,128]{1,0:T(8,128)S(1)}, f32[144,128]{1,0:T(8,128)S(1)}, u32[]{:S(2)}, u32[]{:S(2)}) collective-permute-start(f32[144,128]{1,0:T(8,128)S(1)} %last_y.1.after), channel_id=1, source_target_pairs={{0,2},{2,4},{4,6},{6,0},{1,3},{3,5},{5,7},{7,1},{8,10},{10,12},{12... | collective-permute-start | bytes 221192 | tf_op jit(solution)/shard_map/ppermute | solution.py:34
  10.8 4.3 %collective-permute-start.3 = (f32[136,128]{1,0:T(8,128)S(1)}, f32[136,128]{1,0:T(8,128)S(1)}, u32[]{:S(2)}, u32[]{:S(2)}) collective-permute-start(f32[136,128]{1,0:T(8,128)S(1)} %get-tuple-element.55), channel_id=1, source_target_pairs={{0,8},{8,16},{16,24},{24,0},{1,9},{9,17},{17,25},{25,1},{2,10},{10... | collective-permute-start | bytes 208904 | tf_op jit(solution)/shard_map/ppermute | solution.py:34
  10.8 3.8 %collective-permute-start.2 = (f32[32,128]{1,0:T(8,128)S(1)}, f32[32,128]{1,0:T(8,128)S(1)}, u32[]{:S(2)}, u32[]{:S(2)}) collective-permute-start(f32[32,128]{1,0:T(8,128)S(1)} %get-tuple-element.52.after), channel_id=1, source_target_pairs={{0,1},{1,0},{2,3},{3,2},{4,5},{5,4},{6,7},{7,6},{8,9},{9,8},{10,11... | collective-permute-start | bytes 49160 | tf_op jit(solution)/shard_map/ppermute | solution.py:34
  12.4 2.7 %copy-start.3 = (s32[96]{0:T(128)S(1)}, s32[96]{0:T(128)}, u32[]{:S(2)}) copy-start(s32[96]{0:T(128)} %param.17) | copy-start | bytes 1156
  16.1 3.9 %collective-permute-start.5 = (f32[64,128]{1,0:T(8,128)S(1)}, f32[64,128]{1,0:T(8,128)S(1)}, u32[]{:S(2)}, u32[]{:S(2)}) collective-permute-start(f32[64,128]{1,0:T(8,128)S(1)} %get-tuple-element.63), channel_id=1, source_target_pairs={{0,1},{1,0},{2,3},{3,2},{4,5},{5,4},{6,7},{7,6},{8,9},{9,8},{10,11... | collective-permute-start | bytes 98312 | tf_op jit(solution)/shard_map/ppermute | solution.py:34
